TPU v7x, 32 devices: a whole 2x2x4 slice. The times are simulated.
32 devices in a mesh: dp: 16 (over z, y, x), mp: 2 (over core).
Axes of the slice: x: 2, y: 2, z: 4, core: 2. Of those that a mesh axis runs over, the one named last changes fastest.
Arguments:
- tokens: float32 [32, 896, 384], P(('dp', 'mp')), may hold values from -90 to 90
- segment_ids: int32 [32, 896], P(('dp', 'mp')), may hold values from 0 to 4, as said below
- gains: float32 [5, 384], replicated, may hold values from 0.5 to 1.5
- shifts: float32 [6, 384], replicated, may hold values from -1 to 1
- kernels: float32 [3, 9, 384], replicated, may hold values from -2 to 2
- qkv_weight: float32 [384, 1152], replicated, may hold values from -0.3125 to 0.3125
- out_weight: float32 [384, 384], replicated, may hold values from -1.75 to 1.75
- mlp_in_weight: float32 [384, 1536], P(None, 'mp'), may hold values from -0.3125 to 0.3125
- mlp_in_bias: float32 [1536], P('mp'), may hold values from -2.5 to 2.5
- mlp_out_weight: float32 [1536, 384], P('mp'), may hold values from -0.15625 to 0.15625
- cotangent: float32 [32, 896, 384], P(('dp', 'mp')), may hold values from -20 to 20
Outputs:
- output: float32 [32, 896, 384], P(('dp', 'mp'))
- grad_tokens: float32 [32, 896, 384], P(('dp', 'mp'))
- grad_gains: float32 [5, 384], replicated
- grad_shifts: float32 [6, 384], replicated
- grad_kernels: float32 [3, 9, 384], replicated
- grad_qkv: float32 [384, 1152], replicated
- grad_out: float32 [384, 384], replicated
- grad_mlp_in: float32 [384, 1536], P(None, 'mp')
- grad_mlp_bias: float32 [1536], P('mp')
- grad_mlp_out: float32 [1536, 384], P('mp')
Inputs may be any that keep to these rules, and one draw needn't show every extreme that they name: `segment_ids`: each canvas is 14 rows of 64 columns stored row by row; it holds 4 images of 14 x 14 cells in disjoint runs of 14 whole columns, numbered 1 to 4 from left to right; all other cells are 0.
All inputs are finite; a program needn't handle non-finite values.
Results may differ from a plain program's by a relative error of at most 0.012.
The roundings to bfloat16 on the way count: a program that leaves them out, or rounds other values in their place, can miss the bound.
Values may be sent and summed in bfloat16 or wider, within the bound.
A program may use at most 192 MiB of HBM per device.

v0:
```python
import math

import jax
import jax.numpy as jnp
from jax import lax
from jax.sharding import PartitionSpec as P

HEADS = 6
IMG = 14
IMAGES = 4
CANVAS_W = 64


EPS = 1e-05
MASKED = -1e30


def norm_rows(values, gain_row, shift_row):
    centred = values - jnp.mean(values, -1, keepdims=True)
    variance = jnp.mean(centred * centred, -1, keepdims=True)
    return centred * lax.rsqrt(variance + EPS) * gain_row + shift_row


def tap_masks(segment_ids):
    canvases = segment_ids.shape[0]
    layout = segment_ids.reshape(canvases, IMG, CANVAS_W)
    padded = jnp.pad(layout, ((0, 0), (1, 1), (1, 1)), constant_values=-1)
    collected = []
    for row_off in range(3):
        for col_off in range(3):
            neighbour = padded[:, row_off : row_off + IMG, col_off : col_off + CANVAS_W]
            collected.append(((neighbour == layout) & (layout > 0)).reshape(canvases, -1))
    return jnp.stack(collected).astype(jnp.float32)


def shifted(feature_map, row_off, col_off):
    canvases, positions, features = feature_map.shape
    layout = feature_map.reshape(canvases, IMG, CANVAS_W, features)
    padded = jnp.pad(layout, ((0, 0), (1, 1), (1, 1), (0, 0)))
    return padded[:, row_off : row_off + IMG, col_off : col_off + CANVAS_W].reshape(
        canvases, positions, features
    )


def depthwise(feature_map, kernels, masks_all):
    accum = jnp.zeros((3,) + feature_map.shape, jnp.float32)
    for offset_index in range(9):
        displaced = (
            shifted(feature_map, offset_index // 3, offset_index % 3)
            * masks_all[offset_index][:, :, None]
        )
        accum = accum + displaced[None] * kernels[:, offset_index][:, None, None, :]
    return accum


def smooth(values):
    return jax.nn.gelu(values, approximate=False)


def local(
    tokens,
    segment_ids,
    gains,
    shifts,
    kernels,
    qkv_weight,
    out_weight,
    mlp_in_weight,
    mlp_in_bias,
    mlp_out_weight,
    cotangent,
):
    canvases, positions, features = tokens.shape
    head_size = features // HEADS
    score_scale = 1.0 / math.sqrt(head_size)
    total_rows = IMAGES * IMG * IMG * canvases * lax.axis_size("dp") * lax.axis_size("mp")
    masks_all = tap_masks(segment_ids)
    inside_mask = (segment_ids > 0).astype(jnp.float32)[:, :, None]
    allowed = segment_ids[:, :, None] == segment_ids[:, None, :]
    normed, norm_back = jax.vjp(norm_rows, tokens, gains[0], shifts[0])
    conv_out, conv_back = jax.vjp(
        lambda feature_map, kern_arg: depthwise(feature_map, kern_arg, masks_all), normed, kernels
    )
    bn_mean = lax.psum(jnp.sum(conv_out * inside_mask, (1, 2)), ("dp", "mp")) / total_rows
    centred = conv_out - bn_mean[:, None, None, :]
    bn_var = lax.psum(jnp.sum(centred * centred * inside_mask, (1, 2)), ("dp", "mp")) / total_rows
    inverse = lax.rsqrt(bn_var + EPS)
    bn_shift = jnp.stack([shifts[1], jnp.zeros_like(shifts[1]), shifts[2]])
    standard = (conv_out - bn_mean[:, None, None, :]) * inverse[:, None, None, :]
    low_bn = (standard * gains[1:4][:, None, None, :] + bn_shift[:, None, None, :]).astype(
        jnp.bfloat16
    )
    qkv_low = qkv_weight.astype(jnp.bfloat16).reshape(features, 3, features)
    projected = jnp.einsum(
        "icte,eif->ictf", low_bn, qkv_low, preferred_element_type=jnp.float32
    ).astype(jnp.bfloat16)
    queries = projected[0].reshape(canvases, positions, HEADS, head_size)
    key_rows = projected[1].reshape(canvases, positions, HEADS, head_size)
    value_rows = projected[2].reshape(canvases, positions, HEADS, head_size)

    def masked_scores(query_block, key_block, allowed_block):
        scores = (
            jnp.einsum("qhe,khe->hqk", query_block, key_block, preferred_element_type=jnp.float32)
            * score_scale
        )
        return jnp.where(allowed_block[None], scores, MASKED)

    def attend(block_items):
        query_block, key_block, value_block, allowed_block = block_items
        scores = masked_scores(query_block, key_block, allowed_block)
        largest = jnp.max(scores, -1, keepdims=True)
        expo = jnp.exp(scores - largest)
        denominator = jnp.sum(expo, -1, keepdims=True)
        softmaxed = (expo / denominator).astype(jnp.bfloat16)
        attended = jnp.einsum(
            "hqk,khe->qhe", softmaxed, value_block, preferred_element_type=jnp.float32
        )
        return (attended, largest[..., 0] + jnp.log(denominator[..., 0]))

    attended, log_total = lax.map(attend, (queries, key_rows, value_rows, allowed))
    attended_low = attended.reshape(canvases, positions, features).astype(jnp.bfloat16)
    out_low = out_weight.astype(jnp.bfloat16)
    attn_branch = (
        jnp.einsum("ctd,de->cte", attended_low, out_low, preferred_element_type=jnp.float32)
        + shifts[3]
    )
    residual = tokens + attn_branch
    normed2, norm2_back = jax.vjp(norm_rows, residual, gains[4], shifts[4])
    normed2_low = normed2.astype(jnp.bfloat16)
    cot_low = cotangent.astype(jnp.bfloat16)
    in_low = mlp_in_weight.astype(jnp.bfloat16)
    down_low = mlp_out_weight.astype(jnp.bfloat16)
    gathered = lax.all_gather(normed2_low, "mp", axis=0, tiled=True)
    pre_gelu = (
        jnp.einsum("cte,ef->ctf", gathered, in_low, preferred_element_type=jnp.float32)
        + mlp_in_bias
    )
    activated, gelu_back = jax.vjp(smooth, pre_gelu)
    activated_low = activated.astype(jnp.bfloat16)
    block_rows = activated_low
    branch = lax.psum_scatter(
        jnp.einsum("ctf,fd->ctd", block_rows, down_low, preferred_element_type=jnp.float32).astype(
            jnp.bfloat16
        ),
        "mp",
        scatter_dimension=0,
        tiled=True,
    ).astype(jnp.float32)
    output = residual + branch + shifts[5]
    cot_gathered = lax.all_gather(cot_low, "mp", axis=0, tiled=True)
    grad_act = jnp.einsum("ctd,fd->ctf", cot_gathered, down_low, preferred_element_type=jnp.float32)
    grad_pre = gelu_back(grad_act)[0]
    grad_pre_low = grad_pre.astype(jnp.bfloat16)
    grad_in_part = jnp.einsum(
        "cte,ctf->ef", gathered, grad_pre_low, preferred_element_type=jnp.float32
    )
    grad_bias_part = jnp.sum(grad_pre, (0, 1))
    grad_down_part = jnp.einsum(
        "ctf,ctd->fd", activated_low, cot_gathered, preferred_element_type=jnp.float32
    )
    block_rows = grad_pre_low
    grad_normed2 = lax.psum_scatter(
        jnp.einsum("ctf,ef->cte", block_rows, in_low, preferred_element_type=jnp.float32).astype(
            jnp.bfloat16
        ),
        "mp",
        scatter_dimension=0,
        tiled=True,
    ).astype(jnp.float32)
    grad_mlp_in, grad_mlp_bias, grad_mlp_out = lax.psum(
        (grad_in_part, grad_bias_part, grad_down_part), "dp"
    )
    grad_res_extra, grad_gain4, grad_shift4 = norm2_back(grad_normed2)
    grad_res = cotangent + grad_res_extra
    grad_shift5 = jnp.sum(cotangent, (0, 1))
    grad_shift3 = jnp.sum(grad_res, (0, 1))
    grad_attn_low = grad_res.astype(jnp.bfloat16)
    grad_out_proj = jnp.einsum(
        "ctd,cte->de", attended_low, grad_attn_low, preferred_element_type=jnp.float32
    )
    grad_att = jnp.einsum("cte,de->ctd", grad_attn_low, out_low, preferred_element_type=jnp.float32)
    grad_att_low = grad_att.astype(jnp.bfloat16).reshape(canvases, positions, HEADS, head_size)

    def attend_back(block_items):
        query_block, key_block, value_block, allowed_block, total_block, grad_block = block_items
        scores = masked_scores(query_block, key_block, allowed_block)
        softmaxed = jnp.exp(scores - total_block[..., None])
        grad_soft = jnp.einsum(
            "qhe,khe->hqk", grad_block, value_block, preferred_element_type=jnp.float32
        )
        row_delta = jnp.sum(softmaxed * grad_soft, -1, keepdims=True)
        grad_scores = (softmaxed * (grad_soft - row_delta)).astype(jnp.bfloat16)
        grad_value = jnp.einsum(
            "hqk,qhe->khe",
            softmaxed.astype(jnp.bfloat16),
            grad_block,
            preferred_element_type=jnp.float32,
        )
        grad_query = (
            jnp.einsum("hqk,khe->qhe", grad_scores, key_block, preferred_element_type=jnp.float32)
            * score_scale
        )
        grad_key = (
            jnp.einsum("hqk,qhe->khe", grad_scores, query_block, preferred_element_type=jnp.float32)
            * score_scale
        )
        return (grad_query, grad_key, grad_value)

    grad_query, grad_key, grad_value = lax.map(
        attend_back, (queries, key_rows, value_rows, allowed, log_total, grad_att_low)
    )
    grad_proj = (
        jnp.stack([grad_query, grad_key, grad_value])
        .reshape(3, canvases, positions, features)
        .astype(jnp.bfloat16)
    )
    grad_qkv_w = jnp.einsum(
        "icte,ictf->eif", low_bn, grad_proj, preferred_element_type=jnp.float32
    ).reshape(features, 3 * features)
    grad_bn = jnp.einsum("ictf,eif->icte", grad_proj, qkv_low, preferred_element_type=jnp.float32)
    sum_plain, sum_standard = lax.psum(
        (jnp.sum(grad_bn, (1, 2)), jnp.sum(grad_bn * standard, (1, 2))), ("dp", "mp")
    )
    correction = (
        inside_mask[None]
        * (sum_plain[:, None, None, :] + standard * sum_standard[:, None, None, :])
        / total_rows
    )
    grad_conv = gains[1:4][:, None, None, :] * inverse[:, None, None, :] * (grad_bn - correction)
    grad_normed, grad_kern_part = conv_back(grad_conv)
    grad_tok_part, grad_gain0, grad_shift0 = norm_back(grad_normed)
    grad_tokens = grad_res + grad_tok_part
    ln_gains, plain_shifts, grad_kernels, grad_qkv, grad_out = lax.psum(
        (
            jnp.stack([grad_gain0, grad_gain4]),
            jnp.stack([grad_shift0, grad_shift3, grad_shift4, grad_shift5]),
            grad_kern_part,
            grad_qkv_w,
            grad_out_proj,
        ),
        ("dp", "mp"),
    )
    grad_gains = jnp.stack(
        [ln_gains[0], sum_standard[0], sum_standard[1], sum_standard[2], ln_gains[1]]
    )
    grad_shifts = jnp.stack(
        [
            plain_shifts[0],
            sum_plain[0],
            sum_plain[2],
            plain_shifts[1],
            plain_shifts[2],
            plain_shifts[3],
        ]
    )
    return (
        output,
        grad_tokens,
        grad_gains,
        grad_shifts,
        grad_kernels,
        grad_qkv,
        grad_out,
        grad_mlp_in,
        grad_mlp_bias,
        grad_mlp_out,
    )


def solution(mesh):
    return jax.shard_map(
        local,
        mesh=mesh,
        in_specs=(
            P(("dp", "mp"), None, None),
            P(("dp", "mp"), None),
            P(),
            P(),
            P(),
            P(),
            P(),
            P(None, "mp"),
            P("mp"),
            P("mp", None),
            P(("dp", "mp"), None, None),
        ),
        out_specs=(
            P(("dp", "mp"), None, None),
            P(("dp", "mp"), None, None),
            P(),
            P(),
            P(),
            P(),
            P(),
            P(None, "mp"),
            P("mp"),
            P("mp", None),
        ),
        check_vma=False,
    )
```

profile of v0, /device:TPU:0, one launch (start us, length us, event | category | flops | bytes accessed | tf_op | source)
XLA Modules:
  0.0 641.0 jit_solution(16313632625381057719)
XLA Ops:
  7.2 1.4 compare_bitcast_fusion
  8.6 1.3 fusion.65
  11.8 1.8 copy.132
  15.1 1.4 slice_reduce_fusion.11
  18.2 2.1 fusion.76
  21.8 1.5 slice_bitcast_fusion.8
  23.3 2.4 copy.130
  25.9 1.8 multiply_bitcast_fusion
  27.7 1.8 copy.128
  29.5 3.4 copy.119
  32.8 8.7 %pad_slice_fusion.7 = (f32[1,14,64,384]{3,2,1,0:T(8,128)}, f32[1,14,64,384]{3,2,1,0:T(8,128)}, f32[1,14,64,384]{3,2,1,0:T(8,128)}, f32[1,14,64,384]{3,2,1,0:T(8,...) fusion(f32[1,14,64,384]{3,2,1,0:T(8,128)} %bitcast.162), kind=kLoop, calls=%fused_computation.64 | loop fusion | bytes 12386304 | tf_op jit(solution)/shard_map/jvp()/slice | solution.py:40
  41.6 2.2 bitcast_multiply_fusion.7
  47.2 4.9 multiply_reduce_fusion.21
  52.1 42.3 %psum.84 = f32[3,384]{1,0:T(4,128)} all-reduce(f32[3,384]{1,0:T(4,128)} %get-tuple-element.161), channel_id=1, replica_groups=mesh['dp'=16,'mp'=2] {'dp','mp'}, use_global_device_ids=true, to_apply=%region_3.4 | all-reduce | flops 1152 | bytes 9216 | tf_op jit(solution)/shard_map/psum | solution.py:84
  95.7 3.3 multiply_reduce_fusion.20
  99.0 40.9 %psum.85 = f32[3,384]{1,0:T(4,128)} all-reduce(f32[3,384]{1,0:T(4,128)} %multiply_reduce_fusion.20), channel_id=1, replica_groups=mesh['dp'=16,'mp'=2] {'dp','mp'}, use_global_device_ids=true, to_apply=%region_5.6 | all-reduce | flops 1152 | bytes 9216 | tf_op jit(solution)/shard_map/psum | solution.py:86
  139.9 1.3 slice_multiply_fusion
  141.2 6.1 subtract_multiply_fusion.1
  147.5 1.4 convolution_convert_fusion
  149.5 8.8 %fusion.79 = (f32[6,896]{1,0:T(8,128)S(1)}, f32[6,896,896]{1,2,0:T(8,128)}) fusion(bf16[896,6,64]{0,2,1:T(8,128)(2,1)S(1)} %bitcast.160, bf16[896,6,64]{0,2,1:T(8,128)(2,1)S(1)} %bitcast.158, pred[896,896]{0,1:T(8,128)(4,1)S(1)} %broadcast_compare_fusion), kind=kOutput, calls=%fused_computation.232 | convolution fusion | flops 631008000 | bytes 21468160 | tf_op jit(solution)/shard_map/while/body/eval_jaxpr/qhe,khe->hqk/dot_general | solution.py:103
  158.3 9.0 %fusion = f32[6,896]{1,0:T(8,128)S(1)} fusion(f32[6,896,896]{1,2,0:T(8,128)} %get-tuple-element.214, f32[6,896]{1,0:T(8,128)S(1)} %get-tuple-element.213), kind=kLoop, calls=%fused_computation.6 | loop fusion | flops 9628416 | bytes 19310592 | tf_op jit(solution)/shard_map/while/body/eval_jaxpr/reduce_sum | solution.py:113
  167.3 10.0 %fusion.35 = bf16[6,64,896]{2,1,0:T(8,128)(2,1)S(1)} fusion(bf16[896,6,64]{0,2,1:T(8,128)(2,1)S(1)} %bitcast.181, f32[6,896,896]{1,2,0:T(8,128)} %get-tuple-element.214, f32[6,896]{1,0:T(8,128)S(1)} %fusion, f32[6,896]{1,0:T(8,128)S(1)} %get-tuple-element.213), kind=kOutput, calls=%fused_computation.130 | convolution fusion | flops 631357440 | bytes 20686848 | tf_op jit(solution)/shard_map/while/body/eval_jaxpr/hqk,khe->qhe/dot_general | solution.py:115
  179.6 2.8 fusion.75
  182.6 7.6 %all-gather.3.cloned.1.call-done = bf16[2,896,384]{2,1,0:T(8,128)(2,1)} async-done(((bf16[1,896,384]{2,1,0:T(8,128)(2,1)}), bf16[2,896,384]{2,1,0:T(8,128)(2,1)}) %all-gather.3.cloned.1.call-update) | async-done | bytes 1376272 | tf_op jit(solution)/shard_map/all_gather | solution.py:133
  190.2 4.8 fusion.28
  195.0 2.4 copy-done.24
  197.5 14.3 %multiply_convert_fusion.1 = (bf16[2,896,768]{2,1,0:T(8,128)(2,1)}, f32[2,896,768]{2,1,0:T(8,128)}) fusion(f32[2,896,768]{2,1,0:T(8,128)S(1)} %get-tuple-element.217, f32[768]{0:T(1024)S(1)} %copy-done.129, u8[896,768]{1,0:T(8,128)(4,1)S(1)} %get-tuple-element.102, u8[896,768]{1,0:T(8,128)(4,1)S(1)} %get-tuple-element.101), kind=kLoop, calls=%fused_computation.19 | loop fusion | flops 97714176 | bytes 15141888 | tf_op jit(solution)/shard_map/convert_element_type | solution.py:139
  211.7 8.2 %fusion.81 = (f32[768]{0:T(1024)S(1)}, bf16[2,896,768]{2,1,0:T(8,128)(2,1)S(1)}) fusion(f32[2,896,768]{2,1,0:T(8,128)} %get-tuple-element.160, bf16[2,896,384]{2,1,0:T(8,128)(2,1)} %all-gather.5.cloned.1.call-done, f32[768,384]{1,0:T(8,128)} %param.20, f32[2,896,768]{2,1,0:T(8,128)} %copy-done.24, f32[768]{0:T(1024)S(1)} %copy-done.129), kind=kOutput, calls=%fused_computation.234 | convolution fusion | flops 1079278848 | bytes 16324608 | tf_op jit(solution)/shard_map/ctd,fd->ctf/dot_general | solution.py:151
  219.9 1.5 copy-done.34
  221.5 2.4 convolution_convert_fusion.1
  224.0 4.5 convolution_convert_fusion.2
  233.4 2.9 copy.136
  236.9 42.5 %psum.94 = f32[768]{0:T(1024)} all-reduce(f32[768]{0:T(1024)S(1)} %get-tuple-element.221), channel_id=1, replica_groups=mesh['dp'=16,'mp'=2] {'dp'}, use_global_device_ids=true, to_apply=%region_52.53 | all-reduce | flops 768 | bytes 6144 | tf_op jit(solution)/shard_map/psum | solution.py:170
  279.4 4.6 convolution_bitcast_fusion.1
  284.1 2.6 convolution_bitcast_fusion
  287.0 1.7 convert_reduce_fusion
  289.4 3.4 fusion.71
  294.4 9.8 %fusion.32 = bf16[6,64,896]{2,1,0:T(8,128)(2,1)S(1)} fusion(bf16[896,6,64]{0,2,1:T(8,128)(2,1)S(1)} %bitcast.156, f32[6,896,896]{1,2,0:T(8,128)} %get-tuple-element.214, f32[6,896]{1,0:T(8,128)S(1)} %log_add_fusion), kind=kOutput, calls=%fused_computation.128 | convolution fusion | flops 626540544 | bytes 20665344 | tf_op jit(solution)/shard_map/while/body/eval_jaxpr/hqk,qhe->khe/dot_general | solution.py:193
  304.3 12.4 %multiply_reduce_fusion = (f32[6,896]{1,0:T(8,128)S(1)}, f32[6,896,896]{1,2,0:T(8,128)}) fusion(f32[6,896,896]{1,2,0:T(8,128)} %get-tuple-element.214, f32[6,896]{1,0:T(8,128)S(1)} %log_add_fusion, bf16[896,6,64]{0,2,1:T(8,128)(2,1)S(1)} %bitcast.157, bf16[896,6,64]{0,2,1:T(8,128)(2,1)S(1)} %bitcast.182), kind=kOutput, calls=%fused_computation.1 | convolution fusion | flops 631008000 | bytes 39954432 | tf_op jit(solution)/shard_map/while/body/eval_jaxpr/qhe,khe->hqk/dot_general | solution.py:188
  316.7 13.3 %multiply_convert_fusion = bf16[6,896,896]{1,2,0:T(8,128)(2,1)S(1)} fusion(f32[6,896,896]{1,2,0:T(8,128)} %get-tuple-element.219, f32[6,896,896]{1,2,0:T(8,128)} %get-tuple-element.214, f32[6,896]{1,0:T(8,128)S(1)} %get-tuple-element.218, f32[6,896]{1,0:T(8,128)S(1)} %log_add_fusion), kind=kLoop, calls=%fused_computation | loop fusion | flops 19267584 | bytes 48211968 | tf_op jit(solution)/shard_map/while/body/eval_jaxpr/convert_element_type | solution.py:192
  330.0 3.1 fusion.31
  333.0 2.5 fusion.30
  337.6 2.2 copy.140
  341.1 7.0 %fusion.69 = (f32[3,384]{1,0:T(4,128)}, f32[3,384]{1,0:T(4,128)}, f32[3,896,384]{2,1,0:T(8,128)}) fusion(f32[3,896,384]{2,1,0:T(8,128)} %copy-done, bf16[384,3,384]{0,2,1:T(8,128)(2,1)} %bitcast.154, bf16[1,896,384]{2,1,0:T(8,128)(2,1)S(1)} %copy.142, bf16[1,896,384]{2,1,0:T(8,128)(2,1)} %copy.141, bf16[1,896,384]{2,1,0:T(8,128)(2,1)} %copy.140), kind=kOutput, calls=%fused_computation.225 | convolution fusion | flops 797882112 | bytes 11215872 | tf_op jit(solution)/shard_map/ictf,eif->icte/dot_general | solution.py:220
  348.1 37.7 %all-reduce.20 = (f32[3,384]{1,0:T(4,128)}, f32[3,384]{1,0:T(4,128)}) all-reduce(f32[3,384]{1,0:T(4,128)} %get-tuple-element.122, f32[3,384]{1,0:T(4,128)} %get-tuple-element.121), channel_id=1, replica_groups=mesh['dp'=16,'mp'=2] {'dp','mp'}, use_global_device_ids=true, to_apply=%region_18.19 | all-reduce | flops 2304 | bytes 18432 | tf_op jit(solution)/shard_map/psum | solution.py:221
  385.9 19.6 %multiply_reduce_fusion.9 = (f32[3,384]{1,0:T(4,128)}, f32[3,384]{1,0:T(4,128)}, f32[3,384]{1,0:T(4,128)}, f32[3,384]{1,0:T(4,128)}, f32[3,384]{1,0:T(4,128)}, /...) fusion(f32[896,384]{1,0:T(8,128)} %copy-done.11, ...), kind=kLoop, calls=%fused_computation.40 | loop fusion | flops 59856768 | bytes 29010944 | tf_op jit(solution)/shard_map/transpose(jvp())/reduce_sum | solution.py:52
  405.5 1.8 copy.144
  407.4 1.6 broadcast_multiply_fusion
  415.2 3.3 add_reduce_fusion
  418.5 2.9 copy.145
  421.4 2.9 copy.149
  424.2 2.9 copy.148
  427.1 2.9 copy.147
  430.0 2.9 copy.146
  432.9 3.5 multiply_reduce_fusion.23
  438.3 42.9 %all-reduce.19 = (f32[2,384]{1,0:T(2,128)}, f32[4,384]{1,0:T(4,128)S(1)}, f32[3,9,384]{2,0,1:T(4,128)}) all-reduce(f32[2,384]{1,0:T(2,128)S(1)} %pad_maximum_fusion.7, f32[4,384]{1,0:T(4,128)S(1)} %pad_maximum_fusion.6, f32[3,9,384]{2,0,1:T(4,128)S(1)} %pad_add_fusion), channel_id=1, replica_groups=mesh['dp'=16,'mp'=2] {'dp','mp'}, use_global_device_ids=true, to_apply=%region_32.33 | all-reduce | flops 12672 | bytes 101376 | tf_op jit(solution)/shard_map/psum | solution.py:233
  481.2 1.5 copy.154
  482.7 5.2 fusion.36
  487.9 3.0 copy.151
  490.9 1.4 fusion.38
  492.3 2.9 add_add_fusion.2
  495.2 2.9 copy.155
  499.3 128.8 %all-reduce.26.cloned.1.call-done = (f32[384,1152]{1,0:T(8,128)}, f32[384,384]{1,0:T(8,128)}) async-done(((f32[384,1152]{1,0:T(8,128)}, f32[384,384]{1,0:T(8,128)}), (f32[384,1152]{1,0:T(8,128)}, f32[384,384]{1,0:T(8,128)})) %all-reduce.26.cloned.1.call-update) | async-done | bytes 2359312 | tf_op jit(solution)/shard_map/psum | solution.py:233
  628.1 2.9 copy.170
  (354 shorter events, 37.6 us)
Async XLA Ops:
  7.2 6.4 copy-start.25
  7.2 183.0 %all-gather.3.cloned.1.call-start = ((), (), s32[]{:S(2)}) async-start(), calls=%async_computation.2 | async-start | bytes 2064384 | tf_op jit(solution)/shard_map/all_gather | solution.py:133
  15.1 10.8 %copy-start.47 = (f32[896]{0:T(1024)}, f32[896]{0:T(1024)S(1)}, u32[]{:S(2)}) copy-start(f32[896]{0:T(1024)S(1)} %broadcast_multiply_fusion.10) | copy-start | bytes 10756
  16.4 9.4 %copy-start.77 = (f32[384]{0:T(512)}, f32[384]{0:T(512)S(1)}, u32[]{:S(2)}) copy-start(f32[384]{0:T(512)S(1)} %get-tuple-element.143) | copy-start | bytes 4612
  21.8 4.1 copy-start.69
  29.5 111.7 %copy-start.3 = (f32[896,384]{1,0:T(8,128)}, f32[896,384]{1,0:T(8,128)S(1)}, u32[]{:S(2)}) copy-start(f32[896,384]{1,0:T(8,128)S(1)} %copy.128) | copy-start | bytes 4128772
  32.8 8.7 %copy-start.82 = (f32[896]{0:T(1024)S(1)}, f32[896]{0:T(1024)}, u32[]{:S(2)}) copy-start(f32[896]{0:T(1024)} %get-tuple-element.137) | copy-start | bytes 10756
  32.8 8.7 %copy-start.96 = (f32[896]{0:T(1024)S(1)}, f32[896]{0:T(1024)}, u32[]{:S(2)}) copy-start(f32[896]{0:T(1024)} %get-tuple-element.129) | copy-start | bytes 10756
  46.0 6.0 copy-start.11
  46.0 6.0 copy-start.12
  141.2 6.1 copy-start.75
  141.2 6.3 copy-start.117
  141.2 6.2 copy-start.126
  141.2 6.2 copy-start.127
  141.2 6.3 copy-start.16
  149.4 8.8 %copy-start.18 = (bf16[1,896,384]{1,2,0:T(8,128)(2,1)}, bf16[1,896,384]{1,2,0:T(8,128)(2,1)S(1)}, u32[]{:S(2)}) copy-start(bf16[1,896,384]{1,2,0:T(8,128)(2,1)S(1)} %get-tuple-element.165) | copy-start | bytes 2064388
  149.4 8.8 %copy-start.20 = (bf16[1,896,384]{1,2,0:T(8,128)(2,1)}, bf16[1,896,384]{1,2,0:T(8,128)(2,1)S(1)}, u32[]{:S(2)}) copy-start(bf16[1,896,384]{1,2,0:T(8,128)(2,1)S(1)} %get-tuple-element.166) | copy-start | bytes 2064388
  149.4 17.8 %copy-start.37 = (bf16[1,896,384]{1,2,0:T(8,128)(2,1)}, bf16[1,896,384]{1,2,0:T(8,128)(2,1)S(1)}, u32[]{:S(2)}) copy-start(bf16[1,896,384]{1,2,0:T(8,128)(2,1)S(1)} %get-tuple-element.167) | copy-start | bytes 2064388
  158.3 9.0 %copy-start.45 = (f32[6,896]{1,0:T(8,128)}, f32[6,896]{1,0:T(8,128)S(1)}, u32[]{:S(2)}) copy-start(f32[6,896]{1,0:T(8,128)S(1)} %get-tuple-element.213) | copy-start | bytes 64516
  167.3 10.0 %copy-start.39 = (f32[384,384]{1,0:T(8,128)S(1)}, f32[384,384]{1,0:T(8,128)}, u32[]{:S(2)}) copy-start(f32[384,384]{1,0:T(8,128)} %param.17) | copy-start | bytes 1769476
  167.3 10.0 %copy-start.121 = (f32[384]{0:T(512)S(1)}, f32[384]{0:T(512)}, u32[]{:S(2)}) copy-start(f32[384]{0:T(512)} %get-tuple-element.198) | copy-start | bytes 4612
  179.6 10.6 %copy-start.129 = (f32[768]{0:T(1024)S(1)}, f32[768]{0:T(1024)}, u32[]{:S(2)}) copy-start(f32[768]{0:T(1024)} %param.19) | copy-start | bytes 9220
  179.6 32.1 %all-gather.5.cloned.1.call-start = ((), (), s32[]{:S(2)}) async-start(), calls=%async_computation.4 | async-start | bytes 2064384 | tf_op jit(solution)/shard_map/all_gather | solution.py:150
  182.5 104.4 %reduce-scatter.5.cloned.1.call-start = ((), (), s32[]{:S(2)}) async-start(), calls=%async_computation.5 | async-start | bytes 2064384 | tf_op jit(solution)/shard_map/reduce_scatter | solution.py:162
  211.7 9.7 %copy-start.131 = (f32[384,768]{1,0:T(8,128)S(1)}, f32[384,768]{1,0:T(8,128)}, u32[]{:S(2)}) copy-start(f32[384,768]{1,0:T(8,128)} %param.18) | copy-start | bytes 3538948
  223.9 65.5 %reduce-scatter.3.cloned.1.call-start = ((), (), s32[]{:S(2)}) async-start(), calls=%async_computation.3 | async-start | bytes 2064384 | tf_op jit(solution)/shard_map/reduce_scatter | solution.py:141
  223.9 4.7 copy-start.97
  223.9 5.3 copy-start.95
  223.9 5.4 copy-start.93
  223.9 5.4 copy-start.91
  223.9 6.1 copy-start.89
  224.0 6.7 %copy-start.87 = (f32[896]{0:T(1024)S(1)}, f32[896]{0:T(1024)}, u32[]{:S(2)}) copy-start(f32[896]{0:T(1024)} %get-tuple-element.135) | copy-start | bytes 10756
  224.0 7.4 %copy-start.85 = (f32[896]{0:T(1024)S(1)}, f32[896]{0:T(1024)}, u32[]{:S(2)}) copy-start(f32[896]{0:T(1024)} %get-tuple-element.136) | copy-start | bytes 10756
  224.0 8.1 %copy-start.83 = (f32[896]{0:T(1024)S(1)}, f32[896]{0:T(1024)}, u32[]{:S(2)}) copy-start(f32[896]{0:T(1024)} %get-tuple-element.137) | copy-start | bytes 10756
  224.0 8.7 %copy-start.70 = (f32[896]{0:T(1024)S(1)}, f32[896]{0:T(1024)}, u32[]{:S(2)}) copy-start(f32[896]{0:T(1024)} %copy-done.69) | copy-start | bytes 10756
  228.5 8.4 %copy-start.46 = (f32[6,896]{1,0:T(8,128)S(1)}, f32[6,896]{1,0:T(8,128)}, u32[]{:S(2)}) copy-start(f32[6,896]{1,0:T(8,128)} %copy-done.45) | copy-start | bytes 64516
  228.5 270.8 %all-reduce.28.cloned.1.call-start = ((), (), s32[]{:S(2)}) async-start(), calls=%async_computation.7 | async-start | bytes 4718592 | tf_op jit(solution)/shard_map/psum | solution.py:170
  279.4 4.6 copy-start.15
  279.4 4.6 copy-start.41
  286.7 341.4 %all-reduce.26.cloned.1.call-start = ((), (), s32[]{:S(2)}) async-start(), calls=%async_computation.6 | async-start | bytes 4718592 | tf_op jit(solution)/shard_map/psum | solution.py:233
  289.4 4.5 copy-start.40
  294.4 9.9 %copy-start.38 = (bf16[1,896,384]{1,2,0:T(8,128)(2,1)S(1)}, bf16[1,896,384]{1,2,0:T(8,128)(2,1)}, u32[]{:S(2)}) copy-start(bf16[1,896,384]{1,2,0:T(8,128)(2,1)} %copy-done.37) | copy-start | bytes 2064388
  316.7 13.3 %copy-start.21 = (bf16[1,896,384]{1,2,0:T(8,128)(2,1)S(1)}, bf16[1,896,384]{1,2,0:T(8,128)(2,1)}, u32[]{:S(2)}) copy-start(bf16[1,896,384]{1,2,0:T(8,128)(2,1)} %copy-done.20) | copy-start | bytes 2064388
  329.9 3.1 copy-start.19
  341.0 44.8 %copy-start.4 = (f32[896,384]{1,0:T(8,128)S(1)}, f32[896,384]{1,0:T(8,128)}, u32[]{:S(2)}) copy-start(f32[896,384]{1,0:T(8,128)} %copy-done.3) | copy-start | bytes 4128772
  341.0 44.8 %copy-start.50 = (f32[3,384]{1,0:T(4,128)S(1)}, f32[3,384]{1,0:T(4,128)}, u32[]{:S(2)}) copy-start(f32[3,384]{1,0:T(4,128)} %get-tuple-element.183) | copy-start | bytes 13828
  341.0 44.8 %copy-start.52 = (f32[3,384]{1,0:T(4,128)S(1)}, f32[3,384]{1,0:T(4,128)}, u32[]{:S(2)}) copy-start(f32[3,384]{1,0:T(4,128)} %get-tuple-element.184) | copy-start | bytes 13828
  341.0 44.8 %copy-start.54 = (f32[3,384]{1,0:T(4,128)S(1)}, f32[3,384]{1,0:T(4,128)}, u32[]{:S(2)}) copy-start(f32[3,384]{1,0:T(4,128)} %get-tuple-element.185) | copy-start | bytes 13828
  341.0 44.8 %copy-start.56 = (f32[3,384]{1,0:T(4,128)S(1)}, f32[3,384]{1,0:T(4,128)}, u32[]{:S(2)}) copy-start(f32[3,384]{1,0:T(4,128)} %get-tuple-element.186) | copy-start | bytes 13828
  341.1 44.8 %copy-start.58 = (f32[3,384]{1,0:T(4,128)S(1)}, f32[3,384]{1,0:T(4,128)}, u32[]{:S(2)}) copy-start(f32[3,384]{1,0:T(4,128)} %get-tuple-element.187) | copy-start | bytes 13828
  341.1 44.8 %copy-start.60 = (f32[3,384]{1,0:T(4,128)S(1)}, f32[3,384]{1,0:T(4,128)}, u32[]{:S(2)}) copy-start(f32[3,384]{1,0:T(4,128)} %get-tuple-element.188) | copy-start | bytes 13828
  341.1 44.8 %copy-start.62 = (f32[3,384]{1,0:T(4,128)S(1)}, f32[3,384]{1,0:T(4,128)}, u32[]{:S(2)}) copy-start(f32[3,384]{1,0:T(4,128)} %get-tuple-element.189) | copy-start | bytes 13828
  341.1 44.8 %copy-start.64 = (f32[3,384]{1,0:T(4,128)S(1)}, f32[3,384]{1,0:T(4,128)}, u32[]{:S(2)}) copy-start(f32[3,384]{1,0:T(4,128)} %get-tuple-element.190) | copy-start | bytes 13828
  341.1 44.8 %copy-start.66 = (f32[3,384]{1,0:T(4,128)S(1)}, f32[3,384]{1,0:T(4,128)}, u32[]{:S(2)}) copy-start(f32[3,384]{1,0:T(4,128)} %get-tuple-element.191) | copy-start | bytes 13828
  341.1 44.8 %copy-start.68 = (f32[3,384]{1,0:T(4,128)S(1)}, f32[3,384]{1,0:T(4,128)}, u32[]{:S(2)}) copy-start(f32[3,384]{1,0:T(4,128)} %copy-done.67) | copy-start | bytes 13828
  341.1 44.8 %copy-start.74 = (f32[896]{0:T(1024)S(1)}, f32[896]{0:T(1024)}, u32[]{:S(2)}) copy-start(f32[896]{0:T(1024)} %fusion.65) | copy-start | bytes 10756
  341.1 44.8 %copy-start.76 = (f32[3,384]{1,0:T(4,128)S(1)}, f32[3,384]{1,0:T(4,128)}, u32[]{:S(2)}) copy-start(f32[3,384]{1,0:T(4,128)} %copy-done.75) | copy-start | bytes 13828
  432.9 3.7 copy-start.81
  432.9 4.6 copy-start.72
  436.5 44.6 %copy-start.26 = (f32[1,896,384]{1,2,0:T(8,128)S(1)}, f32[1,896,384]{1,2,0:T(8,128)}, u32[]{:S(2)}) copy-start(f32[1,896,384]{1,2,0:T(8,128)} %get-tuple-element.174) | copy-start | bytes 4128772
  438.1 44.6 %copy-start.116 = (f32[3,384]{1,0:T(4,128)S(1)}, f32[3,384]{1,0:T(4,128)}, u32[]{:S(2)}) copy-start(f32[3,384]{1,0:T(4,128)} %copy-done.115) | copy-start | bytes 13828
  438.1 44.6 %copy-start.118 = (f32[3,384]{1,0:T(4,128)S(1)}, f32[3,384]{1,0:T(4,128)}, u32[]{:S(2)}) copy-start(f32[3,384]{1,0:T(4,128)} %copy-done.117) | copy-start | bytes 13828
  495.2 3.5 copy-start.119
  628.1 3.8 copy-start.43
  (74 other events, 127.4 us)
Sparse Core Ops, SparseCore 0:
  179.7 10.4 all-gather.2
  192.3 10.6 all-gather.4
  224.0 10.0 reduce-scatter.4
  236.3 10.0 reduce-scatter.2
  286.8 127.3 all-reduce.27
  492.4 135.6 all-reduce.25
where the time goes:
time: 649 us; the launch traced here: 641 us
  blocking collectives  206 us (32%)
  waiting for transfers between devices  137 us (21%)
  other arithmetic  108 us (17%)
  matrix products  89.7 us (14%)
  local copies, waits for them, and re-layouts  84.5 us (13%)
  between operations  15.9 us (2%)
    psum x1, waiting for transfers between devices, local(): lax.psum((jnp.stack([grad_gain0, grad_gain4]), jnp.stack([grad_shift0, gr...  129 us
    psum x1, blocking collectives, local(): lax.psum((jnp.stack([grad_gain0, grad_gain4]), jnp.stack([grad_shift0, gr...  42.9 us
    psum x1, blocking collectives, local(): lax.psum((grad_in_part, grad_bias_part, grad_down_part), 'dp')  42.5 us
    psum x1, blocking collectives, local(): lax.psum(jnp.sum(conv_out * inside_mask, (1, 2)), ('dp', 'mp')) / total_rows  42.3 us
    psum x1, blocking collectives, local(): lax.psum(jnp.sum(centred * centred * inside_mask, (1, 2)), ('dp', 'mp'))  40.9 us
    psum x1, blocking collectives, local(): lax.psum((jnp.sum(grad_bn, (1, 2)), jnp.sum(grad_bn * standard, (1, 2))),...  37.7 us
    unnamed x273, local copies, waits for them, and re-layouts  31.5 us
    reduce_sum x1, other arithmetic, depthwise(): accum = accum + displaced[None] * kernels[:, offset_index][:, None, None, :]  19.6 us
  transfers between devices with their start and end apart: 6, of which 2 were waited for; matrix products, arithmetic and copies ran while one was open for 26% of the time, Pallas kernels for 0%

commit v1 on v0

v1 whole, which is shorter than its diff:
```python
import functools
import math

import jax
import jax.numpy as jnp
from jax import lax
from jax.experimental import pallas as pl
from jax.experimental.pallas import tpu as pltpu
from jax.sharding import PartitionSpec as P

F32 = jnp.float32
BF = jnp.bfloat16
MESH = pl.DeviceIdType.MESH
D = 384
IMG = 14
IMAGES = 4
CW = 64
CELLS = IMG * CW
IR = 224
GAP0 = IMAGES * IR
GAPS = 112
R = 1024
CH = 256
STRIDE = IR + 16
CONVR = IMAGES * STRIDE + 16
EPS = 1e-05
MASKED = -1e30
QUAD = 4
VLIM = 60 * 2**20
SCALE = 0.125


def params(**kw):
    return pltpu.CompilerParams(vmem_limit_bytes=VLIM, **kw)


VM = pl.BlockSpec(memory_space=pltpu.VMEM)
SM = pl.BlockSpec(memory_space=pltpu.SMEM)
ANY = pl.BlockSpec(memory_space=pl.ANY)


def shape(*dims, dtype=F32):
    return jax.ShapeDtypeStruct(dims, dtype)


def dot(a, b):
    return jnp.dot(a, b, preferred_element_type=F32)


def dot_t(a, b):
    return lax.dot_general(a, b, (((1,), (1,)), ((), ())), preferred_element_type=F32)


def t_dot(a, b):
    return lax.dot_general(a, b, (((0,), (0,)), ((), ())), preferred_element_type=F32)


def cell_mask(rows):
    row = lax.broadcasted_iota(jnp.int32, (rows, 1), 0)
    return (row % 16 < IMG).astype(F32)


def rows_at(start, size, align=16):
    return pl.ds(pl.multiple_of(start, align), size)


def find_columns(seg, starts, gaps):
    def step(col, count):
        here = seg[0, col]
        before = jnp.where(col == 0, 0, seg[0, jnp.maximum(col - 1, 0)])

        @pl.when(here == 0)
        def _():
            gaps[count] = col

        @pl.when((here > 0) & (here != before))
        def _():
            starts[here - 1] = col

        return count + jnp.where(here == 0, 1, 0)

    lax.fori_loop(0, CW, step, 0)


def to_images(scr, out, starts, gaps):
    col = lax.broadcasted_iota(jnp.int32, (16, 128), 0)
    sub = lax.broadcasted_iota(jnp.int32, (8, 128), 0)

    def step(r, carry):
        for i in range(IMAGES):
            for t in range(3):
                window = scr[t, pl.ds(r * CW + starts[i], 16), :]
                out[rows_at(i * IR + r * 16, 16), t * 128 : t * 128 + 128] = jnp.where(col < IMG, window, 0.0)
        for t in range(3):
            block = jnp.zeros((8, 128), F32)
            for k in range(8):
                block = jnp.where(sub == k, scr[t, pl.ds(r * CW + gaps[k], 1), :], block)
            out[rows_at(GAP0 + r * 8, 8, 8), t * 128 : t * 128 + 128] = block
        return carry

    lax.fori_loop(0, IMG, step, 0)
    out[GAP0 + GAPS : R, :] = jnp.zeros((R - GAP0 - GAPS, D), F32)


def to_canvas(src, scr, starts, gaps):
    def step(r, carry):
        for t in range(3):
            for i in range(IMAGES):
                block = src[rows_at(i * IR + r * 16, 16), t * 128 : t * 128 + 128]
                scr[t, pl.ds(r * CW + starts[i], 16), :] = block
            block = src[rows_at(GAP0 + r * 8, 8, 8), t * 128 : t * 128 + 128]
            for k in range(8):
                scr[t, pl.ds(r * CW + gaps[k], 1), :] = block[k : k + 1]
        return carry

    lax.fori_loop(0, IMG, step, 0)


def norm_parts(x):
    mean = jnp.sum(x, -1, keepdims=True) * (1.0 / D)
    centred = x - mean
    var = jnp.sum(centred * centred, -1, keepdims=True) * (1.0 / D)
    rstd = lax.rsqrt(var + EPS)
    return centred * rstd, rstd


def store_shifted(dst, i, t, x):
    lanes = slice(t * 128, t * 128 + 128)
    at = rows_at(i * STRIDE + 16, IR)
    dst[0, at, lanes] = pltpu.roll(x, 1, 0)
    dst[1, at, lanes] = x
    dst[2, at, lanes] = pltpu.roll(x, IR - 1, 0)


def zero_borders(dst):
    for i in range(IMAGES + 1):
        for c in range(3):
            dst[c, i * STRIDE : i * STRIDE + 16, :] = jnp.zeros((16, D), F32)


def first_norm(tokp, gains, shifts, nrm):
    zero_borders(nrm)
    mask = cell_mask(IR)

    def step(i, carry):
        xhat, _ = norm_parts(tokp[rows_at(i * IR, IR), :])
        normed = (xhat * gains[0:1] + shifts[0:1]) * mask
        for t in range(3):
            store_shifted(nrm, i, t, normed[:, t * 128 : t * 128 + 128])
        return carry

    lax.fori_loop(0, IMAGES, step, 0)


CB = 32


def conv_forward(nrm, kernels, conv, stats):
    mask = cell_mask(CB)
    blocks = IMAGES * IR // CB
    per = IR // CB
    for t in range(3):
        lanes = slice(t * 128, t * 128 + 128)
        taps = [[kernels[k, o : o + 1, lanes] for o in range(9)] for k in range(3)]

        def step(b, sums):
            base = (b // per) * STRIDE + 16 + (b % per) * CB
            acc = [jnp.zeros((CB, 128), F32)] * 3
            for o in range(9):
                x = nrm[o % 3, rows_at(base + (o // 3 - 1) * 16, CB), lanes]
                for k in range(3):
                    acc[k] = acc[k] + x * taps[k][o]
            new = []
            for k in range(3):
                conv[k, rows_at(b * CB, CB), lanes] = acc[k]
                new.append(sums[k] + jnp.sum((acc[k] * mask).reshape(CB // 8, 8, 128), 0))
            return tuple(new)

        sums = lax.fori_loop(0, blocks, step, (jnp.zeros((8, 128), F32),) * 3)
        means = [jnp.sum(s, 0, keepdims=True) * (1.0 / (IMAGES * IMG * IMG)) for s in sums]

        def spread(b, sums):
            new = []
            for k in range(3):
                away = (conv[k, rows_at(b * CB, CB), lanes] - means[k]) * mask
                new.append(sums[k] + jnp.sum((away * away).reshape(CB // 8, 8, 128), 0))
            return tuple(new)

        squares = lax.fori_loop(0, blocks, spread, (jnp.zeros((8, 128), F32),) * 3)
        for k in range(3):
            stats[k : k + 1, lanes] = means[k]
            stats[3 + k : 4 + k, lanes] = jnp.sum(squares[k], 0, keepdims=True)
        stats[6:8, lanes] = jnp.zeros((2, 128), F32)
    for k in range(3):
        conv[k, GAP0:R, :] = jnp.zeros((R - GAP0, D), F32)


def first_kernel(
    seg, tokens, cot, gains, shifts, kernels, wqkv, wout, win, wmo,
    tokp, cotp, conv, stats, wqkv_b, wout_b, win_b, wmo_b,
    scr, nrm, starts, gaps, sems,
):
    copies = []
    for n, src in enumerate((tokens, cot)):
        for t in range(3):
            copy = pltpu.make_async_copy(
                src.at[0, :, pl.ds(t * 128, 128)], scr.at[n, t, pl.ds(0, CELLS)], sems.at[n, t]
            )
            copy.start()
            copies.append(copy)
    find_columns(seg, starts, gaps)
    for k in range(3):
        wqkv_b[k] = wqkv[:, k * D : k * D + D].astype(BF)
    wout_b[...] = wout[...].astype(BF)
    for j in range(2):
        win_b[j] = win[:, j * D : j * D + D].astype(BF)
        wmo_b[j] = wmo[j * D : j * D + D].astype(BF)
    for copy in copies:
        copy.wait()
    to_images(scr.at[0], tokp, starts, gaps)
    to_images(scr.at[1], cotp, starts, gaps)
    first_norm(tokp, gains, shifts, nrm)
    conv_forward(nrm, kernels, conv, stats)


def first_call(seg, tokens, cot, gains, shifts, kernels, wqkv, wout, win, wmo):
    return pl.pallas_call(
        first_kernel,
        out_shape=(
            shape(R, D), shape(R, D), shape(3, R, D), shape(8, D),
            shape(3, D, D, dtype=BF), shape(D, D, dtype=BF), shape(2, D, D, dtype=BF), shape(2, D, D, dtype=BF),
        ),
        in_specs=[SM, ANY, ANY] + [VM] * 7,
        out_specs=(VM,) * 8,
        scratch_shapes=[
            pltpu.VMEM((2, 3, CELLS + 16, 128), F32),
            pltpu.VMEM((3, CONVR, D), F32),
            pltpu.SMEM((8,), jnp.int32),
            pltpu.SMEM((64,), jnp.int32),
            pltpu.SemaphoreType.DMA((2, 3)),
        ],
        compiler_params=params(),
    )(seg, tokens, cot, gains, shifts, kernels, wqkv, wout, win, wmo)


class Place:
    def __init__(self, groups):
        dp = lax.axis_index("dp")
        self.mp = lax.axis_index("mp")
        self.groups = groups
        self.quad = lax.rem(dp, QUAD)
        self.z = dp // QUAD
        self.slot = self.quad * 2 + self.mp

    def in_eight(self, offset):
        other = lax.rem(self.slot + offset, 8)
        return (self.z * QUAD + other // 2, lax.rem(other, 2))

    def in_quad(self, offset):
        return (self.z * QUAD + lax.rem(self.quad + offset, QUAD), self.mp)

    def along(self, offset):
        return (lax.rem(self.z + offset, self.groups) * QUAD + self.quad, self.mp)

    def other_core(self):
        return (self.z * QUAD + self.quad, 1 - self.mp)

    def greet(self):
        barrier = pltpu.get_barrier_semaphore()
        peers = [self.in_eight(o) for o in range(1, 8)] + [self.along(o) for o in range(1, self.groups)]
        for peer in peers:
            pl.semaphore_signal(barrier, inc=1, device_id=peer, device_id_type=MESH)
        pl.semaphore_wait(barrier, len(peers))


def remote(src, dst, send, recv, peer):
    copy = pltpu.make_async_remote_copy(
        src_ref=src, dst_ref=dst, send_sem=send, recv_sem=recv, device_id=peer, device_id_type=MESH
    )
    copy.start()
    return copy


def send_eight(place, src, rx, send, recv):
    return [remote(src, rx.at[place.slot], send.at[o], recv.at[o], place.in_eight(o)) for o in range(1, 8)]


def send_along(place, src, rx, send, recv):
    return [remote(src, rx.at[place.z], send.at[o], recv.at[o], place.along(o)) for o in range(1, place.groups)]


def finish(copies):
    for copy in copies:
        copy.wait()


def sum_slots(rx, count):
    total = rx[0]
    for s in range(1, count):
        total = total + rx[s]
    return total


def all_sum(place, src, rx1, rx2, sems):
    send1, recv1, send2, recv2 = sems
    copies = send_eight(place, src, rx1, send1, recv1)
    rx1[place.slot] = src[...]
    finish(copies)
    rx2[place.z] = sum_slots(rx1, 8)
    finish(send_along(place, rx2.at[place.z], rx2, send2, recv2))
    return sum_slots(rx2, place.groups)


def merge_moments(rx, count, cells):
    mean = sum([rx[s, 0:3] for s in range(1, count)], rx[0, 0:3]) * (1.0 / count)
    m2 = sum([rx[s, 3:6] for s in range(1, count)], rx[0, 3:6])
    for s in range(count):
        away = rx[s, 0:3] - mean
        m2 = m2 + away * away * float(cells)
    return mean, m2


def pair_weights(place, win_b, wmo_b, bias, win_f, wmo_f, bias_f, send, recv, local):
    copies = []
    half = pl.ds(place.mp * 2, 2)
    for n, (src, dst) in enumerate(((win_b, win_f), (wmo_b, wmo_f))):
        copies.append(remote(src, dst.at[half], send.at[n], recv.at[n], place.other_core()))
        here = pltpu.make_async_copy(src, dst.at[half], local.at[n])
        here.start()
        copies.append(here)
    copies.append(remote(bias, bias_f.at[place.mp], send.at[2], recv.at[2], place.other_core()))
    bias_f[place.mp] = bias[...]
    return copies


def stats_kernel(groups, stats, win_b, wmo_b, bias, moments, win_f, wmo_f, bias_f, rx1, rx2, s1, r1, s2, r2, sw, rw, lw):
    place = Place(groups)
    place.greet()
    copies = send_eight(place, stats, rx1, s1, r1)
    rx1[place.slot] = stats[...]
    weights = pair_weights(place, win_b, wmo_b, bias, win_f, wmo_f, bias_f, sw, rw, lw)
    finish(copies)
    cells = IMAGES * IMG * IMG
    mean, m2 = merge_moments(rx1, 8, cells)
    rx2[place.z, 0:3] = mean
    rx2[place.z, 3:6] = m2
    rx2[place.z, 6:8] = jnp.zeros((2, D), F32)
    finish(send_along(place, rx2.at[place.z], rx2, s2, r2))
    mean, m2 = merge_moments(rx2, groups, 8 * cells)
    moments[0:3] = mean
    moments[3:6] = lax.rsqrt(m2 * (1.0 / (cells * 8 * groups)) + EPS)
    moments[6:8] = jnp.zeros((2, D), F32)
    finish(weights)


def dma(*n):
    return pltpu.SemaphoreType.DMA(n)


def stats_call(groups, stats, win_b, wmo_b, bias):
    return pl.pallas_call(
        functools.partial(stats_kernel, groups),
        out_shape=(shape(8, D), shape(4, D, D, dtype=BF), shape(4, D, D, dtype=BF), shape(2, 8, D)),
        in_specs=[VM] * 4,
        out_specs=(VM,) * 4,
        scratch_shapes=[
            pltpu.VMEM((8, 8, D), F32), pltpu.VMEM((groups, 8, D), F32),
            dma(8), dma(8), dma(groups), dma(groups), dma(3), dma(3), dma(2),
        ],
        compiler_params=params(collective_id=0, has_side_effects=True),
    )(stats, win_b, wmo_b, bias)


def project(conv, moments, gains, shifts, wqkv, bn, qkv):
    def step(c, carry):
        rows = rows_at(c * CH, CH)
        for k in range(3):
            standard = (conv[k, rows, :] - moments[k : k + 1]) * moments[3 + k : 4 + k]
            value = standard * gains[1 + k : 2 + k]
            if k != 1:
                value = value + (shifts[1:2] if k == 0 else shifts[2:3])
            value = value.astype(BF)
            bn[k, rows, :] = value
            out = dot(value, wqkv[k]).astype(BF)
            if k == 0:
                out = (out * SCALE).astype(BF)
            for p in range(3):
                qkv[k, p, rows, :] = out[:, p * 128 : p * 128 + 128]
        return carry

    lax.fori_loop(0, R // CH, step, 0)


def key_bias():
    row = lax.broadcasted_iota(jnp.int32, (16, 256), 0)
    return jnp.where(row < IMG, 0.0, MASKED)


def query_mask():
    lane = lax.broadcasted_iota(jnp.int32, (1, 256), 1)
    return (lane < IR).astype(F32)


def halves(x):
    lane = lax.broadcasted_iota(jnp.int32, x.shape, 1)
    zero = jnp.zeros_like(x)
    return [jnp.where(lane < 64, x, zero), jnp.where(lane < 64, zero, x)]


def attend(qkv, probs, att):
    bias = key_bias()[None]
    live = query_mask()

    def step(n, carry):
        i, p = n // 3, lax.rem(n, 3)
        rows = rows_at(i * IR, IR)
        q = qkv[0, p, rows_at(i * IR, 256), :]
        k = qkv[1, p, rows, :]
        v_t = qkv[2, p, rows, :].T
        parts = []
        for h, k_h in enumerate(halves(k)):
            scores = (dot_t(k_h, q).reshape(IMG, 16, 256) + bias).reshape(IR, 256)
            largest = jnp.max(scores, 0, keepdims=True)
            expo = jnp.exp(scores - largest)
            soft = expo * (live / jnp.sum(expo, 0, keepdims=True))
            probs[n * 2 + h] = soft
            parts.append(dot(v_t[h * 64 : h * 64 + 64], soft.astype(BF)))
        out = jnp.concatenate(parts, 0).T
        att[p, rows, :] = out[:IR].astype(BF)
        return carry

    lax.fori_loop(0, 3 * IMAGES, step, 0)


def even_prob():
    return jnp.full((1, 1), 1.0 / GAPS, F32).astype(BF).astype(F32)


def attend_gap(qkv, att):
    for p in range(3):
        v = qkv[2, p, GAP0 : GAP0 + 16, :].astype(F32)
        out = (v * (even_prob() * float(GAPS))).astype(BF)
        for b in range((R - GAP0) // 16):
            att[p, GAP0 + b * 16 : GAP0 + b * 16 + 16, :] = out


def gelu_parts(x):
    cdf = 0.5 * (1.0 + lax.erf(x * (1.0 / math.sqrt(2.0))))
    density = jnp.exp(x * x * -0.5) * (1.0 / math.sqrt(2.0 * math.pi))
    return x * cdf, cdf + x * density


def col_sum(x):
    return jnp.sum(x, 0, keepdims=True)


def feed_forward(
    tokp, cotp, att, wout, win, wmo, bias, gains, shifts,
    outp, dres, n2, gm, gr, act, dpre, datt, small, acc,
):
    small[...] = jnp.zeros((16, D), F32)

    def step(c, carry):
        rows = rows_at(c * CH, CH)
        attended = jnp.concatenate([att[p, rows, :] for p in range(3)], 1)
        residual = tokp[rows, :] + (dot(attended, wout[...]) + shifts[3:4])
        xhat, rstd = norm_parts(residual)
        n2[rows, :] = (xhat * gains[4:5] + shifts[4:5]).astype(BF)
        cot = cotp[rows, :]
        gm[rows, :] = cot.astype(BF)
        outp[rows, :] = residual + shifts[5:6]
        acc[...] = jnp.zeros((CH, D), F32)

        for j in range(4):
            hidden_at(j, rows, n2, gm, win, wmo, bias, act, dpre, outp, acc, small)
        grad = acc[...]
        scaled = grad * gains[4:5]
        one = jnp.sum(scaled, -1, keepdims=True) * (1.0 / D)
        two = jnp.sum(scaled * xhat, -1, keepdims=True) * (1.0 / D)
        total = cot + rstd * (scaled - one - xhat * two)
        dres[rows, :] = total
        low = total.astype(BF)
        gr[rows, :] = low
        back = dot_t(low, wout[...]).astype(BF)
        for p in range(3):
            datt[p, rows, :] = back[:, p * 128 : p * 128 + 128]
        small[0:1] = small[0:1] + col_sum(grad * xhat)
        small[1:2] = small[1:2] + col_sum(total)
        small[2:3] = small[2:3] + col_sum(grad)
        small[3:4] = small[3:4] + col_sum(cot)
        return carry

    lax.fori_loop(0, R // CH, step, 0)


def hidden_at(j, rows, n2, gm, win, wmo, bias, act, dpre, outp, acc, small):
    pre = dot(n2[rows, :], win[j]) + bias[j // 2, j % 2 : j % 2 + 1]
    value, slope = gelu_parts(pre)
    value = value.astype(BF)
    act[j, rows, :] = value
    grad = dot_t(gm[rows, :], wmo[j]) * slope
    small[4 + j : 5 + j] = small[4 + j : 5 + j] + col_sum(grad)
    grad = grad.astype(BF)
    dpre[j, rows, :] = grad
    outp[rows, :] = outp[rows, :] + dot(value, wmo[j])
    acc[...] = acc[...] + dot_t(grad, win[j])


def feed_forward_grads(n2, gm, act, dpre, att, gr, grads):
    def step(j, carry):
        half, which = j // 2, lax.rem(j, 2)
        grads[0, half, rows_at(which * D, D), :] = t_dot(n2[...], dpre[j]).astype(BF)
        grads[1, half, rows_at(which * D, D), :] = t_dot(act[j], gm[...]).astype(BF)
        return carry

    lax.fori_loop(0, 4, step, 0)
    for p in range(3):
        grads[2, 1, D + p * 128 : D + p * 128 + 128, :] = t_dot(att[p], gr[...]).astype(BF)


def attend_back(qkv, probs, datt, dqkv):
    def step(n, carry):
        i, p = n // 3, lax.rem(n, 3)
        rows = rows_at(i * IR, IR)
        wide = rows_at(i * IR, 256)
        q = qkv[0, p, wide, :]
        k_t = qkv[1, p, rows, :].T
        v = qkv[2, p, rows, :]
        do = datt[p, wide, :]
        dq, dk, dv = [], [], []
        for h, v_h in enumerate(halves(v)):
            soft = probs[n * 2 + h]
            grad = dot_t(v_h, do)
            delta = jnp.sum(soft * grad, 0, keepdims=True)
            ds = (soft * (grad - delta)).astype(BF)
            dv.append(dot(soft.astype(BF), do))
            dk.append(dot(ds, q))
            dq.append(dot(k_t[h * 64 : h * 64 + 64], ds))
        lane = lax.broadcasted_iota(jnp.int32, (IR, 128), 1)
        dqkv[0, p, rows, :] = (jnp.concatenate(dq, 0).T[:IR] * SCALE).astype(BF)
        dqkv[1, p, rows, :] = jnp.where(lane < 64, dk[0], dk[1]).astype(BF)
        dqkv[2, p, rows, :] = jnp.where(lane < 64, dv[0], dv[1]).astype(BF)
        return carry

    lax.fori_loop(0, 3 * IMAGES, step, 0)


def attend_back_gap(datt, dqkv):
    for p in range(3):
        total = col_sum(datt[p, GAP0 : GAP0 + GAPS, :].astype(F32))
        grad = jnp.broadcast_to((total * even_prob()).astype(BF), (16, 128))
        zero = jnp.zeros((16, 128), BF)
        for b in range((R - GAP0) // 16):
            rows = slice(GAP0 + b * 16, GAP0 + b * 16 + 16)
            dqkv[0, p, rows, :] = zero
            dqkv[1, p, rows, :] = zero
            dqkv[2, p, rows, :] = grad if b < GAPS // 16 else zero


def project_back(conv, moments, wqkv, bn, dqkv, dbn, sums, grads):
    sums[...] = jnp.zeros((8, D), F32)

    def step(c, carry):
        rows = rows_at(c * CH, CH)
        for k in range(3):
            grad = jnp.concatenate([dqkv[k, p, rows, :] for p in range(3)], 1)
            back = dot_t(grad, wqkv[k])
            dbn[k, rows, :] = back
            standard = (conv[k, rows, :] - moments[k : k + 1]) * moments[3 + k : 4 + k]
            sums[k : k + 1] = sums[k : k + 1] + col_sum(back)
            sums[3 + k : 4 + k] = sums[3 + k : 4 + k] + col_sum(back * standard)
        return carry

    lax.fori_loop(0, R // CH, step, 0)
    for k in range(3):
        for p in range(3):
            grads[2, k // 2, (k % 2) * D : (k % 2) * D + D, p * 128 : p * 128 + 128] = t_dot(
                bn[k], dqkv[k, p]
            ).astype(BF)


def middle_kernel(
    tokp, cotp, conv, moments, gains, shifts, wqkv, wout, win, wmo, bias,
    outp, dres, dbn, sums, grads, small,
    bn, qkv, probs, att, n2, gm, gr, act, dpre, datt, dqkv, acc,
):
    project(conv, moments, gains, shifts, wqkv, bn, qkv)
    attend(qkv, probs, att)
    attend_gap(qkv, att)
    feed_forward(
        tokp, cotp, att, wout, win, wmo, bias, gains, shifts,
        outp, dres, n2, gm, gr, act, dpre, datt, small, acc,
    )
    feed_forward_grads(n2, gm, act, dpre, att, gr, grads)
    attend_back(qkv, probs, datt, dqkv)
    attend_back_gap(datt, dqkv)
    project_back(conv, moments, wqkv, bn, dqkv, dbn, sums, grads)


def middle_call(*args):
    return pl.pallas_call(
        middle_kernel,
        out_shape=(
            shape(R, D), shape(R, D), shape(3, R, D), shape(8, D), shape(3, 2, 2 * D, D, dtype=BF), shape(16, D),
        ),
        in_specs=[VM] * 11,
        out_specs=(VM,) * 6,
        scratch_shapes=[
            pltpu.VMEM((3, R, D), BF), pltpu.VMEM((3, 3, R, 128), BF), pltpu.VMEM((24, IR, 256), F32),
            pltpu.VMEM((3, R, 128), BF), pltpu.VMEM((R, D), BF), pltpu.VMEM((R, D), BF), pltpu.VMEM((R, D), BF),
            pltpu.VMEM((4, R, D), BF), pltpu.VMEM((4, R, D), BF), pltpu.VMEM((3, R, 128), BF),
            pltpu.VMEM((3, 3, R, 128), BF), pltpu.VMEM((CH, D), F32),
        ],
        compiler_params=params(),
    )(*args)


def sum_kernel(groups, src, out, rx1, rx2, *sems):
    place = Place(groups)
    place.greet()
    out[...] = all_sum(place, src, rx1, rx2, sems)


def sum_call(groups, src, collective_id):
    return pl.pallas_call(
        functools.partial(sum_kernel, groups),
        out_shape=shape(*src.shape),
        in_specs=[VM],
        out_specs=VM,
        scratch_shapes=[
            pltpu.VMEM((8,) + src.shape, F32), pltpu.VMEM((groups,) + src.shape, F32),
            dma(8), dma(8), dma(groups), dma(groups),
        ],
        compiler_params=params(collective_id=collective_id, has_side_effects=True),
    )(src)


def conv_back(dbn, conv, moments, sums, gains, nrm, shifted, kernels, dn, dker, inverse_total):
    mask = cell_mask(IR)
    for k in range(3):
        zero_borders(shifted.at[k])
    for k in range(3):

        def spread(i, carry):
            rows = rows_at(i * IR, IR)
            for t in range(3):
                lanes = slice(t * 128, t * 128 + 128)
                inv = moments[3 + k : 4 + k, lanes]
                standard = (conv[k, rows, lanes] - moments[k : k + 1, lanes]) * inv
                shift = (sums[k : k + 1, lanes] + standard * sums[3 + k : 4 + k, lanes]) * inverse_total
                grad = (gains[1 + k : 2 + k, lanes] * inv) * (dbn[k, rows, lanes] - mask * shift)
                store_shifted(shifted.at[k], i, t, grad)
            return carry

        lax.fori_loop(0, IMAGES, spread, 0)
    blocks = IMAGES * IR // CB
    per = IR // CB
    for t in range(3):
        lanes = slice(t * 128, t * 128 + 128)
        for k in range(3):
            taps = [kernels[k, o : o + 1, lanes] for o in range(9)]

            def step(b, sums9):
                base = (b // per) * STRIDE + 16 + (b % per) * CB
                here = nrm[1, rows_at(base, CB), lanes]
                acc = jnp.zeros((CB, 128), F32)
                new = []
                for o in range(9):
                    x = shifted[k, 2 - o % 3, rows_at(base - (o // 3 - 1) * 16, CB), lanes]
                    acc = acc + x * taps[o]
                    new.append(sums9[o] + jnp.sum((x * here).reshape(CB // 8, 8, 128), 0))
                rows = rows_at(b * CB, CB)
                if k == 0:
                    dn[rows, lanes] = acc
                else:
                    dn[rows, lanes] = dn[rows, lanes] + acc
                return tuple(new)

            sums9 = lax.fori_loop(0, blocks, step, (jnp.zeros((8, 128), F32),) * 9)
            for o in range(9):
                dker[k * 9 + o : k * 9 + o + 1, lanes] = col_sum(sums9[o])


def last_norm_back(tokp, dres, dn, gains, gtok, dker):
    mask = cell_mask(IR)
    dker[27:32] = jnp.zeros((5, D), F32)

    def step(i, carry):
        rows = rows_at(i * IR, IR)
        xhat, rstd = norm_parts(tokp[rows, :])
        grad = dn[rows, :] * mask
        dker[27:28] = dker[27:28] + col_sum(grad * xhat)
        dker[28:29] = dker[28:29] + col_sum(grad)
        scaled = grad * gains[0:1]
        one = jnp.sum(scaled, -1, keepdims=True) * (1.0 / D)
        two = jnp.sum(scaled * xhat, -1, keepdims=True) * (1.0 / D)
        gtok[rows, :] = dres[rows, :] + rstd * (scaled - one - xhat * two)
        return carry

    lax.fori_loop(0, IMAGES, step, 0)
    gtok[GAP0:R, :] = dres[GAP0:R, :]


def back_kernel(inverse_total, tokp, dres, dbn, conv, moments, sums, gains, shifts, kernels, gtok, dker, nrm, shifted, dn):
    first_norm(tokp, gains, shifts, nrm)
    conv_back(dbn, conv, moments, sums, gains, nrm, shifted, kernels, dn, dker, inverse_total)
    last_norm_back(tokp, dres, dn, gains, gtok, dker)


def back_call(inverse_total, *args):
    return pl.pallas_call(
        functools.partial(back_kernel, inverse_total),
        out_shape=(shape(R, D), shape(32, D)),
        in_specs=[VM] * 9,
        out_specs=(VM,) * 2,
        scratch_shapes=[
            pltpu.VMEM((3, CONVR, D), F32), pltpu.VMEM((3, 3, CONVR, D), F32), pltpu.VMEM((IMAGES * IR, D), F32),
        ],
        compiler_params=params(),
    )(*args)


HALF = 2 * D
QR = HALF // QUAD


class GradSum:
    def __init__(self, place, unit, src, bufs, sems):
        self.place, self.unit, self.src = place, unit, src
        self.rx_core, self.own, self.rx_quad, self.mid, self.rx_z, self.done = [b.at[unit] for b in bufs]
        self.send, self.recv = sems[0].at[unit], sems[1].at[unit]
        self.groups = place.groups
        self.part = -(-QR // (16 * self.groups)) * 16
        self.span = self.part * self.groups

    def core_start(self):
        mine = self.src.at[self.unit, 1 - self.place.mp]
        self.copies = [remote(mine, self.rx_core, self.send.at[0], self.recv.at[0], self.place.other_core())]

    def core_end(self):
        finish(self.copies)
        for b in range(HALF // 64):
            rows = slice(b * 64, b * 64 + 64)
            mine = self.src[self.unit, self.place.mp, rows, :].astype(F32)
            self.own[rows, :] = (mine + self.rx_core[rows, :].astype(F32)).astype(BF)

    def quad_start(self):
        self.copies = []
        for o in range(1, QUAD):
            rows = rows_at(lax.rem(self.place.quad + o, QUAD) * QR, QR)
            self.copies.append(
                remote(self.own.at[rows], self.rx_quad.at[o - 1], self.send.at[o], self.recv.at[o], self.place.in_quad(o))
            )

    def quad_end(self):
        finish(self.copies)
        for b in range(QR // 64):
            rows = slice(b * 64, b * 64 + 64)
            total = self.own[rows_at(self.place.quad * QR + b * 64, 64), :].astype(F32)
            for o in range(QUAD - 1):
                total = total + self.rx_quad[o, rows, :].astype(F32)
            self.mid[rows, :] = total.astype(BF)
        if self.span > QR:
            self.mid[QR:, :] = jnp.zeros((self.span - QR, D), BF)

    def z_start(self):
        self.copies = []
        for o in range(1, self.groups):
            rows = rows_at(lax.rem(self.place.z + o, self.groups) * self.part, self.part)
            at = 3 + o
            self.copies.append(
                remote(self.mid.at[rows], self.rx_z.at[o - 1], self.send.at[at], self.recv.at[at], self.place.along(o))
            )

    def z_end(self):
        finish(self.copies)
        total = self.mid[rows_at(self.place.z * self.part, self.part), :].astype(F32)
        for o in range(self.groups - 1):
            total = total + self.rx_z[o].astype(F32)
        self.done[self.place.mp, self.place.quad, rows_at(self.place.z * self.part, self.part), :] = total.astype(BF)

    def z_back_start(self):
        here = self.done.at[self.place.mp, self.place.quad, rows_at(self.place.z * self.part, self.part)]
        self.copies = []
        for o in range(1, self.groups):
            at = 2 + self.groups + o
            self.copies.append(remote(here, here, self.send.at[at], self.recv.at[at], self.place.along(o)))

    def quad_back_start(self):
        here = self.done.at[self.place.mp, self.place.quad]
        self.copies = []
        for o in range(1, QUAD):
            at = 1 + 2 * self.groups + o
            self.copies.append(remote(here, here, self.send.at[at], self.recv.at[at], self.place.in_quad(o)))

    def core_back_start(self):
        here = self.done.at[self.place.mp]
        at = 1 + 2 * self.groups + QUAD
        self.copies = [remote(here, here, self.send.at[at], self.recv.at[at], self.place.other_core())]

    def end(self):
        finish(self.copies)


def grad_buffers(groups):
    part = -(-QR // (16 * groups)) * 16
    return [
        pltpu.VMEM((3, HALF, D), BF),
        pltpu.VMEM((3, HALF, D), BF),
        pltpu.VMEM((3, QUAD - 1, QR, D), BF),
        pltpu.VMEM((3, part * groups, D), BF),
        pltpu.VMEM((3, groups - 1, part, D), BF),
    ], (3, 2, QUAD, part * groups, D)


def grads_kernel(groups, src, done, b0, b1, b2, b3, b4, send, recv):
    place = Place(groups)
    place.greet()
    units = [GradSum(place, u, src, (b0, b1, b2, b3, b4, done), (send, recv)) for u in range(3)]
    for u in units:
        u.core_start()
    for u in units:
        u.core_end()
        u.quad_start()
    for u in units:
        u.quad_end()
        u.z_start()
    for u in units:
        u.z_end()
        u.z_back_start()
    for u in units:
        u.end()
        u.quad_back_start()
    for u in units:
        u.end()
    units[2].core_back_start()
    units[2].end()


def grads_call(groups, src):
    bufs, done = grad_buffers(groups)
    n = 2 + 2 * groups + QUAD
    return pl.pallas_call(
        functools.partial(grads_kernel, groups),
        out_shape=shape(*done, dtype=BF),
        in_specs=[VM],
        out_specs=VM,
        scratch_shapes=bufs + [dma(3, n), dma(3, n)],
        compiler_params=params(collective_id=3, has_side_effects=True),
    )(src)


def last_kernel(seg, outp, gtok, output, grad_tokens, scr, starts, gaps):
    find_columns(seg, starts, gaps)
    for src, dst in ((outp, output), (gtok, grad_tokens)):
        to_canvas(src, scr, starts, gaps)
        for t in range(3):
            dst[0, :, t * 128 : t * 128 + 128] = scr[t, 0:CELLS, :]


def last_call(seg, outp, gtok):
    return pl.pallas_call(
        last_kernel,
        out_shape=(shape(1, CELLS, D), shape(1, CELLS, D)),
        in_specs=[SM, VM, VM],
        out_specs=(VM, VM),
        scratch_shapes=[
            pltpu.VMEM((3, CELLS + 16, 128), F32), pltpu.SMEM((8,), jnp.int32), pltpu.SMEM((64,), jnp.int32),
        ],
        compiler_params=params(),
    )(seg, outp, gtok)


def local(
    groups, total, tokens, segment_ids, gains, shifts, kernels, qkv_weight, out_weight,
    mlp_in_weight, mlp_in_bias, mlp_out_weight, cotangent,
):
    tokp, cotp, conv, stats, wqkv, wout, win_h, wmo_h = first_call(
        segment_ids, tokens, cotangent, gains, shifts, kernels, qkv_weight, out_weight, mlp_in_weight, mlp_out_weight
    )
    bias_h = jnp.pad(mlp_in_bias.reshape(2, D), ((0, 6), (0, 0)))
    moments, win, wmo, bias = stats_call(groups, stats, win_h, wmo_h, bias_h)
    outp, dres, dbn, sums, grads, small = middle_call(
        tokp, cotp, conv, moments, gains, shifts, wqkv, wout, win, wmo, bias
    )
    sums = sum_call(groups, sums, 1)
    gtok, dker = back_call(1.0 / total, tokp, dres, dbn, conv, moments, sums, gains, shifts, kernels)
    done = grads_call(groups, grads)[:, :, :, :QR]
    rest = sum_call(groups, jnp.concatenate([dker, small[:8]], 0), 2)
    output, grad_tokens = last_call(segment_ids, outp, gtok)
    mp = lax.axis_index("mp")
    done = done.reshape(3, 2, 2, D, D).astype(F32)
    mine = lax.dynamic_index_in_dim(done[:2], mp, 1, keepdims=False)
    grad_mlp_in = jnp.concatenate([mine[0, 0], mine[0, 1]], 1)
    grad_mlp_out = mine[1].reshape(2 * D, D)
    grad_qkv = jnp.concatenate([done[2, 0, 0], done[2, 0, 1], done[2, 1, 0]], 1)
    grad_out = done[2, 1, 1]
    grad_kernels = rest[:27].reshape(3, 9, D)
    grad_bias = lax.dynamic_slice_in_dim(rest[36:40], mp * 2, 2, 0).reshape(2 * D)
    grad_gains = jnp.stack([rest[27], sums[3], sums[4], sums[5], rest[32]])
    grad_shifts = jnp.stack([rest[28], sums[0], sums[2], rest[33], rest[34], rest[35]])
    return (
        output, grad_tokens, grad_gains, grad_shifts, grad_kernels, grad_qkv, grad_out,
        grad_mlp_in, grad_bias, grad_mlp_out,
    )


def solution(mesh):
    groups = mesh.shape["dp"] // QUAD
    total = IMAGES * IMG * IMG * mesh.shape["dp"] * mesh.shape["mp"]
    both = P(("dp", "mp"), None, None)
    return jax.shard_map(
        functools.partial(local, groups, total),
        mesh=mesh,
        in_specs=(
            both, P(("dp", "mp"), None), P(), P(), P(), P(), P(), P(None, "mp"), P("mp"), P("mp", None), both,
        ),
        out_specs=(both, both, P(), P(), P(), P(), P(), P(None, "mp"), P("mp"), P("mp", None)),
        check_vma=False,
    )
```

time: 649 us -> 214 us (0.33); the launches traced: 641 us -> 213 us
  blocking collectives: 206 us -> 0 us
  Pallas kernels: 0 us -> 189 us
  waiting for transfers between devices: 137 us -> 0 us
  other arithmetic: 108 us -> 7.11 us
  matrix products: 89.7 us -> 0 us
  local copies, waits for them, and re-layouts: 84.5 us -> 15.5 us
  between operations: 15.9 us -> 0.75 us
    psum x5 -> x0, blocking collectives: 206 us -> none  [the longest x1 42.9 us: local(): lax.psum((jnp.stack([grad_gain0, grad_gain4]), jnp.stack([grad_shift0, gr...]
    pallas_call x0 -> x8, Pallas kernels: none -> 189 us  [the longest x1 60.2 us: grads_call(): pl.pallas_call(functools.partial(grads_kernel, groups), out_shape=shape(*...]
    psum x2 -> x0, waiting for transfers between devices: 129 us -> none  [the longest x1 129 us: local(): lax.psum((jnp.stack([grad_gain0, grad_gain4]), jnp.stack([grad_shift0, gr...]
    dot_general x18 -> x0, matrix products: 89.7 us -> none  [the longest x1 12.4 us: attend_back(): jnp.einsum('qhe,khe->hqk', grad_block, value_block, preferred_element_typ...]
    reduce_sum x14 -> x0, other arithmetic: 53.9 us -> none  [the longest x1 19.6 us: depthwise(): accum = accum + displaced[None] * kernels[:, offset_index][:, None, None, :]]
    unnamed x273 -> x12, local copies, waits for them, and re-layouts: 31.5 us -> 3.43 us
    convert_element_type x4 -> x1, other arithmetic: 27.8 us -> 2.84 us  [local(): done = done.reshape(3, 2, 2, D, D).astype(F32)]
    mul x16 -> x0, other arithmetic: 16.6 us -> none  [the longest x1 6.08 us: local(): (conv_out - bn_mean[:, None, None, :]) * inverse[:, None, None, :]]
  transfers between devices with their start and end apart: 6 -> 0, of which waited for: 2 -> 0; matrix products, arithmetic and copies ran while one was open for 26% -> 0% of each run, Pallas kernels for 0% -> 0%
where the time goes in v1:
time: 214 us; the launch traced here: 213 us
  Pallas kernels  189 us (88%)
  local copies, waits for them, and re-layouts  15.5 us (7%)
  other arithmetic  7.11 us (3%)
    pallas_call x1, Pallas kernels, grads_call(): pl.pallas_call(functools.partial(grads_kernel, groups), out_shape=shape(*...  60.2 us
    pallas_call x1, Pallas kernels, middle_call(): pl.pallas_call(middle_kernel, out_shape=(shape(R, D), shape(R, D), shape(...  46.1 us
    pallas_call x2, Pallas kernels, sum_call(): pl.pallas_call(functools.partial(sum_kernel, groups), out_shape=shape(*sr...  27.8 us
    pallas_call x1, Pallas kernels, back_call(): pl.pallas_call(functools.partial(back_kernel, inverse_total), out_shape=(...  19.7 us
    pallas_call x1, Pallas kernels, first_call(): pl.pallas_call(first_kernel, out_shape=(shape(R, D), shape(R, D), shape(3...  15.4 us
    pallas_call x1, Pallas kernels, stats_call(): pl.pallas_call(functools.partial(stats_kernel, groups), out_shape=(shape(...  14.7 us
    pallas_call x1, Pallas kernels, last_call(): pl.pallas_call(last_kernel, out_shape=(shape(1, CELLS, D), shape(1, CELLS...  5.45 us

profile of v1, /device:TPU:0, one launch (start us, length us, event | category | flops | bytes accessed | tf_op | source)
XLA Modules:
  0.0 212.8 jit_solution(11479294570069570607)
XLA Ops:
  0.6 1.5 copy.24.kernels
  2.1 0.0 copy-start.4
  2.1 15.4 %shard_map.186 = (f32[1024,384]{1,0:T(8,128)}, f32[1024,384]{1,0:T(8,128)}, f32[3,1024,384]{2,1,0:T(8,128)}, f32[8,384]{1,0:T(8,128)}, bf16[3,384,384]{2,1,0:T(8...) custom-call(s32[1,896]{1,0:T(1,128)} %seg.3, ...), custom_call_target="tpu_custom_call" | custom-call | tf_op jit(solution)/shard_map/pallas_call | solution.py:227
  17.5 0.0 copy-done.4
  17.6 0.6 pad.4.bias
  18.2 14.7 %shard_map.187 = (f32[8,384]{1,0:T(8,128)}, bf16[4,384,384]{2,1,0:T(8,128)(2,1)}, bf16[4,384,384]{2,1,0:T(8,128)(2,1)}, f32[2,8,384]{2,1,0:T(8,128)}) custom-call(f32[8,384]{1,0:T(8,128)} %get-tuple-element.35.stats, bf16[2,384,384]{2,1,0:T(8,128)(2,1)} %get-tuple-element.36.win_b, bf16[2,384,384]{2,1,0:T(8,128)(2,1)} %get-tuple-element.37.wmo_b, ...), custom_call_target="tpu_custom_call" | custom-call | tf_op jit(solution)/shard_map/pallas_call | solution.py:361
  32.9 46.1 %shard_map.188 = (f32[1024,384]{1,0:T(8,128)}, f32[1024,384]{1,0:T(8,128)}, f32[3,1024,384]{2,1,0:T(8,128)}, f32[8,384]{1,0:T(8,128)}, bf16[3,2,768,384]{3,2,1,0:T(8,128)(2,1)}, /*index=5*/f32[16,384]{1,0:T(8,128)}) custom-call(f32[1024,384]{1,0:T(8,128)} %get-tuple-element.32.tokp, f32[1024,384]{1,0:T(8,128)} %get-tuple-element.33.cotp, ...), custom_call_target="tpu_custom_call" | custom-call | tf_op jit(solution)/shard_map/pallas_call | solution.py:601
  79.0 11.1 %shard_map.189.sums = f32[8,384]{1,0:T(8,128)} custom-call(f32[8,384]{1,0:T(8,128)} %get-tuple-element.47.src), custom_call_target="tpu_custom_call" | custom-call | tf_op jit(solution)/shard_map/pallas_call | solution.py:625
  90.1 19.7 %shard_map.190 = (f32[1024,384]{1,0:T(8,128)}, f32[32,384]{1,0:T(8,128)}) custom-call(f32[1024,384]{1,0:T(8,128)} %get-tuple-element.32.tokp, f32[1024,384]{1,0:T(8,128)} %get-tuple-element.45.dres, f32[3,1024,384]{2,1,0:T(8,128)} %get-tuple-element.46.dbn, f32[3,1024,384]{2,1,0:T(8,128)} %get-tuple-element.34.conv, f32[8,384]{1,0:T(8,128)} %get-tuple-element.38.moments, ...), custom_call_target="tpu_custom_call" | custom-call | tf_op jit(solution)/shard_map/pallas_call | solution.py:711
  109.7 0.0 copy-start.3
  109.7 0.0 copy-start.2
  109.7 0.0 copy-start.1
  109.7 5.5 %shard_map.191 = (f32[1,896,384]{2,1,0:T(8,128)}, f32[1,896,384]{2,1,0:T(8,128)}) custom-call(s32[1,896]{1,0:T(1,128)} %seg.3, f32[1024,384]{1,0:T(8,128)} %get-tuple-element.44.outp, f32[1024,384]{1,0:T(8,128)} %get-tuple-element.48.gtok), custom_call_target="tpu_custom_call" | custom-call | tf_op jit(solution)/shard_map/pallas_call | solution.py:862
  115.2 0.0 copy-done.3
  115.2 0.0 copy-done.2
  115.2 0.6 pad_maximum_fusion.2.src
  115.8 16.8 %shard_map.192 = f32[40,384]{1,0:T(8,128)} custom-call(f32[40,384]{1,0:T(8,128)} %pad_maximum_fusion.2.src), custom_call_target="tpu_custom_call" | custom-call | tf_op jit(solution)/shard_map/pallas_call | solution.py:625
  132.6 0.0 copy-done.1
  132.6 0.8 fusion
  133.4 0.6 pad_maximum_fusion.3
  134.0 0.7 slice.71
  134.7 0.6 pad_maximum_fusion.4
  135.3 0.8 slice.72
  136.2 0.6 copy.26
  136.8 60.2 %shard_map.193 = bf16[3,2,4,192,384]{4,3,2,1,0:T(8,128)(2,1)} custom-call(bf16[3,2,768,384]{3,2,1,0:T(8,128)(2,1)} %get-tuple-element.53.src), custom_call_target="tpu_custom_call" | custom-call | tf_op jit(solution)/shard_map/pallas_call | solution.py:843
  197.0 2.8 %convert_element_type.8 = f32[3,2,4,192,384]{4,3,2,1,0:T(8,128)S(1)} convert(bf16[3,2,4,192,384]{4,3,2,1,0:T(8,128)(2,1)} %shard_map.193) | non-fusion elementwise | flops 1769472 | bytes 10616832 | tf_op jit(solution)/shard_map/convert_element_type | solution.py:892
  199.9 1.0 slice_bitcast_fusion.2
  200.9 0.0 copy-start
  200.9 1.3 pad_maximum_fusion
  202.2 1.3 copy-done
  203.5 2.6 %slice.87 = f32[2,2,4,192,384]{4,3,2,1,0:T(8,128)} slice(bf16[3,2,4,192,384]{4,3,2,1,0:T(8,128)(2,1)S(1)} %copy-done), slice={[0:2], [0:2], [0:4], [0:192], [0:384]} | slice | bytes 9437184 | tf_op jit(solution)/shard_map/slice | solution.py:893
  206.1 1.8 dynamic-slice_bitcast_fusion
  208.0 0.1 slice_bitcast_fusion.1
  208.0 1.1 pad_maximum_fusion.1
  209.1 0.7 slice.81
  209.9 0.6 reshape.36
  210.5 2.4 %constant_dynamic-slice_fusion = f32[1,1,2,384,384]{4,3,2,1,0:T(8,128)} fusion(f32[2,2,2,384,384]{4,3,2,1,0:T(8,128)} %bitcast.18, s32[]{:T(128)S(6)} %add.11, s32[]{:T(128)S(6)} %select_n.7), kind=kLoop, calls=%fused_computation.12 | loop fusion | bytes 2359304 | tf_op jit(solution)/shard_map/slice | solution.py:895
  (5 shorter events, 0.0 us)
Async XLA Ops:
  2.1 15.5 %copy-start.4 = (f32[768]{0:T(1024)S(1)}, f32[768]{0:T(1024)}, u32[]{:S(2)}) copy-start(f32[768]{0:T(1024)} %param.19) | copy-start | bytes 9220
  109.7 5.5 %copy-start.3 = (f32[16,384]{1,0:T(8,128)S(1)}, f32[16,384]{1,0:T(8,128)}, u32[]{:S(2)}) copy-start(f32[16,384]{1,0:T(8,128)} %get-tuple-element.52) | copy-start | bytes 73732
  109.7 5.5 %copy-start.2 = (f32[32,384]{1,0:T(8,128)S(1)}, f32[32,384]{1,0:T(8,128)}, u32[]{:S(2)}) copy-start(f32[32,384]{1,0:T(8,128)} %get-tuple-element.51) | copy-start | bytes 147460
  109.7 22.9 %copy-start.1 = (f32[8,384]{1,0:T(8,128)S(1)}, f32[8,384]{1,0:T(8,128)}, u32[]{:S(2)}) copy-start(f32[8,384]{1,0:T(8,128)} %shard_map.189.sums) | copy-start | bytes 36868
  200.9 2.6 %copy-start = (bf16[3,2,4,192,384]{4,3,2,1,0:T(8,128)(2,1)S(1)}, bf16[3,2,4,192,384]{4,3,2,1,0:T(8,128)(2,1)}, u32[]{:S(2)}) copy-start(bf16[3,2,4,192,384]{4,3,2,1,0:T(8,128)(2,1)} %shard_map.193) | copy-start | bytes 10616836

commit v2 on v1

v2 whole, which is shorter than its diff:
```python
import functools
import math

import jax
import jax.numpy as jnp
from jax import lax
from jax.experimental import pallas as pl
from jax.experimental.pallas import tpu as pltpu
from jax.sharding import PartitionSpec as P

F32 = jnp.float32
BF = jnp.bfloat16
MESH = pl.DeviceIdType.MESH
D = 384
IMG = 14
IMAGES = 4
CW = 64
CELLS = IMG * CW
IR = 224
GAP0 = IMAGES * IR
GAPS = 112
R = 1024
CH = 256
STRIDE = IR + 16
CONVR = IMAGES * STRIDE + 16
EPS = 1e-05
MASKED = -1e30
QUAD = 4
VLIM = 60 * 2**20
SCALE = 0.125


def params(**kw):
    return pltpu.CompilerParams(vmem_limit_bytes=VLIM, **kw)


VM = pl.BlockSpec(memory_space=pltpu.VMEM)
SM = pl.BlockSpec(memory_space=pltpu.SMEM)
ANY = pl.BlockSpec(memory_space=pl.ANY)


def shape(*dims, dtype=F32):
    return jax.ShapeDtypeStruct(dims, dtype)


def dot(a, b):
    return jnp.dot(a, b, preferred_element_type=F32)


def dot_t(a, b):
    return lax.dot_general(a, b, (((1,), (1,)), ((), ())), preferred_element_type=F32)


def t_dot(a, b):
    return lax.dot_general(a, b, (((0,), (0,)), ((), ())), preferred_element_type=F32)


def cell_mask(rows):
    row = lax.broadcasted_iota(jnp.int32, (rows, 1), 0)
    return (row % 16 < IMG).astype(F32)


def rows_at(start, size, align=16):
    return pl.ds(pl.multiple_of(start, align), size)


def find_columns(seg):
    def step(col, found):
        count, starts, gaps = found
        here = seg[0, col]
        starts = tuple(jnp.minimum(s, jnp.where(here == i + 1, col, CW)) for i, s in enumerate(starts))
        empty = here == 0
        gaps = tuple(jnp.where(empty & (count == k), col, g) for k, g in enumerate(gaps))
        return count + jnp.where(empty, 1, 0), starts, gaps

    start = (jnp.int32(0), (jnp.int32(CW),) * IMAGES, (jnp.int32(0),) * 8)
    _, starts, gaps = lax.fori_loop(0, CW, step, start)
    return starts, gaps


SCR = CELLS + 16
POOL = 48 * IR


def empty_before(seg):
    lane = lax.broadcasted_iota(jnp.int32, (1, 128), 1)
    ids = seg[0:1, 0:128]
    firsts = [jnp.where((ids == i + 1) & (lane < CW), lane, CW).astype(F32) for i in range(IMAGES)]
    return [jnp.min(f, -1, keepdims=True) - float(i * IMG) for i, f in enumerate(firsts)]


def to_images(pool, base, out, ahead):
    col = lax.broadcasted_iota(jnp.int32, (16, 128), 0)
    sub = lax.broadcasted_iota(jnp.int32, (8, 128), 0).astype(F32)
    before = sum([jnp.where(a <= sub, 1.0, 0.0) for a in ahead])

    def step(r, carry):
        for t in range(3):
            row = base + t * SCR + r * CW
            for i in range(IMAGES):
                window = pool[pl.ds(row + i * IMG, 16), :]
                for e in range(1, 9):
                    moved = pool[pl.ds(row + i * IMG + e, 16), :]
                    window = jnp.where(ahead[i] == float(e), moved, window)
                out[rows_at(i * IR + r * 16, 16), t * 128 : t * 128 + 128] = jnp.where(col < IMG, window, 0.0)
            block = pool[rows_at(row, 8, 8), :]
            for n in range(1, IMAGES + 1):
                block = jnp.where(before == float(n), pool[pl.ds(row + n * IMG, 8), :], block)
            out[rows_at(GAP0 + r * 8, 8, 8), t * 128 : t * 128 + 128] = block
        return carry

    lax.fori_loop(0, IMG, step, 0)
    out[GAP0 + GAPS : R, :] = jnp.zeros((R - GAP0 - GAPS, D), F32)


def to_canvas(src, scr, starts, gaps):
    def step(r, carry):
        for t in range(3):
            for i in range(IMAGES):
                block = src[rows_at(i * IR + r * 16, 16), t * 128 : t * 128 + 128]
                scr[t, pl.ds(r * CW + starts[i], 16), :] = block
            block = src[rows_at(GAP0 + r * 8, 8, 8), t * 128 : t * 128 + 128]
            for k in range(8):
                scr[t, pl.ds(r * CW + gaps[k], 1), :] = block[k : k + 1]
        return carry

    lax.fori_loop(0, IMG, step, 0)


def norm_parts(x):
    mean = jnp.sum(x, -1, keepdims=True) * (1.0 / D)
    centred = x - mean
    var = jnp.sum(centred * centred, -1, keepdims=True) * (1.0 / D)
    rstd = lax.rsqrt(var + EPS)
    return centred * rstd, rstd


def store_shifted(dst, i, t, x):
    lanes = slice(t * 128, t * 128 + 128)
    at = rows_at(i * STRIDE + 16, IR)
    dst[0, at, lanes] = pltpu.roll(x, 1, 0)
    dst[1, at, lanes] = x
    dst[2, at, lanes] = pltpu.roll(x, IR - 1, 0)


def zero_borders(dst):
    for i in range(IMAGES + 1):
        for c in range(3):
            dst[c, i * STRIDE : i * STRIDE + 16, :] = jnp.zeros((16, D), F32)


def first_norm(tokp, gains, shifts, nrm):
    zero_borders(nrm)
    mask = cell_mask(IR)

    def step(i, carry):
        xhat, _ = norm_parts(tokp[rows_at(i * IR, IR), :])
        normed = (xhat * gains[0:1] + shifts[0:1]) * mask
        for t in range(3):
            store_shifted(nrm, i, t, normed[:, t * 128 : t * 128 + 128])
        return carry

    lax.fori_loop(0, IMAGES, step, 0)


CB = 32


def conv_forward(nrm, kernels, conv, stats):
    mask = cell_mask(CB)
    blocks = IMAGES * IR // CB
    per = IR // CB
    for t in range(3):
        lanes = slice(t * 128, t * 128 + 128)
        taps = [[kernels[k, o : o + 1, lanes] for o in range(9)] for k in range(3)]

        def step(b, sums):
            base = (b // per) * STRIDE + 16 + (b % per) * CB
            acc = [jnp.zeros((CB, 128), F32)] * 3
            for o in range(9):
                x = nrm[o % 3, rows_at(base + (o // 3 - 1) * 16, CB), lanes]
                for k in range(3):
                    acc[k] = acc[k] + x * taps[k][o]
            new = []
            for k in range(3):
                conv[k, rows_at(b * CB, CB), lanes] = acc[k]
                new.append(sums[k] + jnp.sum((acc[k] * mask).reshape(CB // 8, 8, 128), 0))
            return tuple(new)

        sums = lax.fori_loop(0, blocks, step, (jnp.zeros((8, 128), F32),) * 3)
        means = [jnp.sum(s, 0, keepdims=True) * (1.0 / (IMAGES * IMG * IMG)) for s in sums]

        def spread(b, sums):
            new = []
            for k in range(3):
                away = (conv[k, rows_at(b * CB, CB), lanes] - means[k]) * mask
                new.append(sums[k] + jnp.sum((away * away).reshape(CB // 8, 8, 128), 0))
            return tuple(new)

        squares = lax.fori_loop(0, blocks, spread, (jnp.zeros((8, 128), F32),) * 3)
        for k in range(3):
            stats[k : k + 1, lanes] = means[k]
            stats[3 + k : 4 + k, lanes] = jnp.sum(squares[k], 0, keepdims=True)
        stats[6:8, lanes] = jnp.zeros((2, 128), F32)
    for k in range(3):
        conv[k, GAP0:R, :] = jnp.zeros((R - GAP0, D), F32)


class Place:
    def __init__(self, groups):
        dp = lax.axis_index("dp")
        self.mp = lax.axis_index("mp")
        self.groups = groups
        self.quad = lax.rem(dp, QUAD)
        self.z = dp // QUAD
        self.slot = self.quad * 2 + self.mp

    def in_eight(self, offset):
        other = lax.rem(self.slot + offset, 8)
        return (self.z * QUAD + other // 2, lax.rem(other, 2))

    def in_quad(self, offset):
        return (self.z * QUAD + lax.rem(self.quad + offset, QUAD), self.mp)

    def along(self, offset):
        return (lax.rem(self.z + offset, self.groups) * QUAD + self.quad, self.mp)

    def other_core(self):
        return (self.z * QUAD + self.quad, 1 - self.mp)

    def peers(self):
        return [self.in_eight(o) for o in range(1, 8)] + [self.along(o) for o in range(1, self.groups)]

    def greet(self):
        barrier = pltpu.get_barrier_semaphore()
        for peer in self.peers():
            pl.semaphore_signal(barrier, inc=1, device_id=peer, device_id_type=MESH)

    def greeted(self):
        pl.semaphore_wait(pltpu.get_barrier_semaphore(), 7 + self.groups - 1)


def remote(src, dst, send, recv, peer):
    copy = pltpu.make_async_remote_copy(
        src_ref=src, dst_ref=dst, send_sem=send, recv_sem=recv, device_id=peer, device_id_type=MESH
    )
    copy.start()
    return copy


def send_eight(place, src, rx, send, recv):
    return [remote(src, rx.at[place.slot], send.at[o], recv.at[o], place.in_eight(o)) for o in range(1, 8)]


def send_along(place, src, rx, send, recv):
    return [remote(src, rx.at[place.z], send.at[o], recv.at[o], place.along(o)) for o in range(1, place.groups)]


def finish(copies):
    for copy in copies:
        copy.wait()


def sum_slots(rx, count):
    total = rx[0]
    for s in range(1, count):
        total = total + rx[s]
    return total


def merge_moments(rx, count, cells):
    mean = sum([rx[s, 0:3] for s in range(1, count)], rx[0, 0:3]) * (1.0 / count)
    m2 = sum([rx[s, 3:6] for s in range(1, count)], rx[0, 3:6])
    for s in range(count):
        away = rx[s, 0:3] - mean
        m2 = m2 + away * away * float(cells)
    return mean, m2


def dma(*n):
    return pltpu.SemaphoreType.DMA(n)


def project(conv, moments, gains, shifts, wqkv, bn, qkv):
    def step(c, carry):
        rows = rows_at(c * CH, CH)
        for k in range(3):
            standard = (conv[k, rows, :] - moments[k : k + 1]) * moments[3 + k : 4 + k]
            value = standard * gains[1 + k : 2 + k]
            if k != 1:
                value = value + (shifts[1:2] if k == 0 else shifts[2:3])
            value = value.astype(BF)
            bn[k, rows, :] = value
            out = dot(value, wqkv[k]).astype(BF)
            if k == 0:
                out = (out * SCALE).astype(BF)
            for p in range(3):
                qkv[k, p, rows, :] = out[:, p * 128 : p * 128 + 128]
        return carry

    lax.fori_loop(0, R // CH, step, 0)


def key_bias():
    row = lax.broadcasted_iota(jnp.int32, (16, 256), 0)
    return jnp.where(row < IMG, 0.0, MASKED)


def query_mask():
    lane = lax.broadcasted_iota(jnp.int32, (1, 256), 1)
    return (lane < IR).astype(F32)


def halves(x):
    lane = lax.broadcasted_iota(jnp.int32, x.shape, 1)
    zero = jnp.zeros_like(x)
    return [jnp.where(lane < 64, x, zero), jnp.where(lane < 64, zero, x)]


def probs_at(pool, n):
    return [rows_at((2 * n + half) * IR, IR) for half in range(2)]


def attend(qkv, pool, att):
    bias = key_bias()[None]
    live = query_mask()

    def step(n, carry):
        i, p = n // 3, lax.rem(n, 3)
        rows = rows_at(i * IR, IR)
        q = qkv[0, p, rows_at(i * IR, 256), :]
        k = qkv[1, p, rows, :]
        v_t = qkv[2, p, rows, :].T
        parts = []
        for h, k_h in enumerate(halves(k)):
            scores = (dot_t(k_h, q).reshape(IMG, 16, 256) + bias).reshape(IR, 256)
            largest = jnp.max(scores, 0, keepdims=True)
            expo = jnp.exp(scores - largest)
            soft = expo * (live / jnp.sum(expo, 0, keepdims=True))
            for half, at in enumerate(probs_at(pool, n * 2 + h)):
                pool[at, :] = soft[:, half * 128 : half * 128 + 128]
            parts.append(dot(v_t[h * 64 : h * 64 + 64], soft.astype(BF)))
        out = jnp.concatenate(parts, 0).T
        att[p, rows, :] = out[:IR].astype(BF)
        return carry

    lax.fori_loop(0, 3 * IMAGES, step, 0)


def even_prob():
    return jnp.full((1, 1), 1.0 / GAPS, F32).astype(BF).astype(F32)


def attend_gap(qkv, att):
    for p in range(3):
        v = qkv[2, p, GAP0 : GAP0 + 16, :].astype(F32)
        out = (v * (even_prob() * float(GAPS))).astype(BF)
        for b in range((R - GAP0) // 16):
            att[p, GAP0 + b * 16 : GAP0 + b * 16 + 16, :] = out


def gelu_parts(x):
    cdf = 0.5 * (1.0 + lax.erf(x * (1.0 / math.sqrt(2.0))))
    density = jnp.exp(x * x * -0.5) * (1.0 / math.sqrt(2.0 * math.pi))
    return x * cdf, cdf + x * density


def col_sum(x):
    return jnp.sum(x, 0, keepdims=True)


def feed_forward_in(tokp, cotp, att, wout, gains, shifts, dres, n2, gm, small):
    small[...] = jnp.zeros((8, D), F32)

    def step(c, carry):
        rows = rows_at(c * CH, CH)
        attended = jnp.concatenate([att[p, rows, :] for p in range(3)], 1)
        residual = tokp[rows, :] + (dot(attended, wout[...]) + shifts[3:4])
        dres[rows, :] = residual
        xhat, _ = norm_parts(residual)
        n2[rows, :] = (xhat * gains[4:5] + shifts[4:5]).astype(BF)
        cot = cotp[rows, :]
        gm[rows, :] = cot.astype(BF)
        small[3:4] = small[3:4] + col_sum(cot)
        return carry

    lax.fori_loop(0, R // CH, step, 0)


def hidden_tile(j, first, n2, gm, win, wmo, bias, act, dpre, outp, acc, small, grads):
    def step(c, carry):
        rows = rows_at(c * CH, CH)
        pre = dot(n2[rows, :], win[j]) + bias[j // 2, j % 2 : j % 2 + 1]
        value, slope = gelu_parts(pre)
        value = value.astype(BF)
        act[rows, :] = value
        grad = dot_t(gm[rows, :], wmo[j]) * slope
        small[4 + j : 5 + j] = small[4 + j : 5 + j] + col_sum(grad)
        grad = grad.astype(BF)
        dpre[rows, :] = grad
        forward = dot(value, wmo[j])
        back = dot_t(grad, win[j])
        outp[rows, :] = forward if first else outp[rows, :] + forward
        acc[rows, :] = back if first else acc[rows, :] + back
        return carry

    lax.fori_loop(0, R // CH, step, 0)
    unit, half = j % 2, j // 2
    grads[unit, half, 0:D, :] = t_dot(n2[...], dpre[...]).astype(BF)
    grads[unit, half, D : 2 * D, :] = t_dot(act[...], gm[...]).astype(BF)


def feed_forward_out(cotp, wout, gains, shifts, outp, acc, dres, gr, datt, small):
    def step(c, carry):
        rows = rows_at(c * CH, CH)
        residual = dres[rows, :]
        outp[rows, :] = residual + outp[rows, :] + shifts[5:6]
        xhat, rstd = norm_parts(residual)
        grad = acc[rows, :]
        scaled = grad * gains[4:5]
        one = jnp.sum(scaled, -1, keepdims=True) * (1.0 / D)
        two = jnp.sum(scaled * xhat, -1, keepdims=True) * (1.0 / D)
        total = cotp[rows, :] + rstd * (scaled - one - xhat * two)
        dres[rows, :] = total
        low = total.astype(BF)
        gr[rows, :] = low
        back = dot_t(low, wout[...]).astype(BF)
        for p in range(3):
            datt[p, rows, :] = back[:, p * 128 : p * 128 + 128]
        small[0:1] = small[0:1] + col_sum(grad * xhat)
        small[1:2] = small[1:2] + col_sum(total)
        small[2:3] = small[2:3] + col_sum(grad)
        return carry

    lax.fori_loop(0, R // CH, step, 0)


def attend_back(p, qkv, pool, datt, dqkv):
    def step(i, carry):
        n = i * 3 + p
        rows = rows_at(i * IR, IR)
        wide = rows_at(i * IR, 256)
        q = qkv[0, p, wide, :]
        k_t = qkv[1, p, rows, :].T
        v = qkv[2, p, rows, :]
        do = datt[p, wide, :]
        dq, dk, dv = [], [], []
        for h, v_h in enumerate(halves(v)):
            soft = jnp.concatenate([pool[at, :] for at in probs_at(pool, n * 2 + h)], 1)
            grad = dot_t(v_h, do)
            delta = jnp.sum(soft * grad, 0, keepdims=True)
            ds = (soft * (grad - delta)).astype(BF)
            dv.append(dot(soft.astype(BF), do))
            dk.append(dot(ds, q))
            dq.append(dot(k_t[h * 64 : h * 64 + 64], ds))
        lane = lax.broadcasted_iota(jnp.int32, (IR, 128), 1)
        dqkv[0, p, rows, :] = (jnp.concatenate(dq, 0).T[:IR] * SCALE).astype(BF)
        dqkv[1, p, rows, :] = jnp.where(lane < 64, dk[0], dk[1]).astype(BF)
        dqkv[2, p, rows, :] = jnp.where(lane < 64, dv[0], dv[1]).astype(BF)
        return carry

    lax.fori_loop(0, IMAGES, step, 0)


def attend_back_gap(datt, dqkv):
    for p in range(3):
        total = col_sum(datt[p, GAP0 : GAP0 + GAPS, :].astype(F32))
        grad = jnp.broadcast_to((total * even_prob()).astype(BF), (16, 128))
        zero = jnp.zeros((16, 128), BF)
        for b in range((R - GAP0) // 16):
            rows = slice(GAP0 + b * 16, GAP0 + b * 16 + 16)
            dqkv[0, p, rows, :] = zero
            dqkv[1, p, rows, :] = zero
            dqkv[2, p, rows, :] = grad if b < GAPS // 16 else zero


def project_back(conv, moments, wqkv, dqkv, dbn, sums):
    sums[...] = jnp.zeros((8, D), F32)

    def step(c, carry):
        rows = rows_at(c * CH, CH)
        for k in range(3):
            grad = jnp.concatenate([dqkv[k, p, rows, :] for p in range(3)], 1)
            back = dot_t(grad, wqkv[k])
            dbn[rows_at(k * R + c * CH, CH), :] = back
            standard = (conv[k, rows, :] - moments[k : k + 1]) * moments[3 + k : 4 + k]
            sums[k : k + 1] = sums[k : k + 1] + col_sum(back)
            sums[3 + k : 4 + k] = sums[3 + k : 4 + k] + col_sum(back * standard)
        return carry

    lax.fori_loop(0, R // CH, step, 0)


def project_grads(bn, dqkv, grads):
    for k in range(3):
        for p in range(3):
            grads[2, k // 2, (k % 2) * D : (k % 2) * D + D, p * 128 : p * 128 + 128] = t_dot(
                bn[k], dqkv[k, p]
            ).astype(BF)


def shifted_at(c, t, row, size):
    return rows_at((c * 3 + t) * CONVR + row, size)


def conv_back_zero(pool):
    for c in range(3):
        for t in range(3):
            for i in range(IMAGES + 1):
                pool[shifted_at(c, t, i * STRIDE, 16), :] = jnp.zeros((16, 128), F32)


def conv_back(k, dbn, conv, moments, sums, gains, nrm, pool, kernels, dn, dker, inverse_total):
    mask = cell_mask(IR)

    def spread(i, carry):
        rows = rows_at(i * IR, IR)
        for t in range(3):
            lanes = slice(t * 128, t * 128 + 128)
            inv = moments[3 + k : 4 + k, lanes]
            standard = (conv[k, rows, lanes] - moments[k : k + 1, lanes]) * inv
            shift = (sums[k : k + 1, lanes] + standard * sums[3 + k : 4 + k, lanes]) * inverse_total
            grad = dbn[rows_at(k * R + i * IR, IR), lanes]
            grad = (gains[1 + k : 2 + k, lanes] * inv) * (grad - mask * shift)
            pool[shifted_at(0, t, i * STRIDE + 16, IR), :] = pltpu.roll(grad, 1, 0)
            pool[shifted_at(1, t, i * STRIDE + 16, IR), :] = grad
            pool[shifted_at(2, t, i * STRIDE + 16, IR), :] = pltpu.roll(grad, IR - 1, 0)
        return carry

    lax.fori_loop(0, IMAGES, spread, 0)
    blocks = IMAGES * IR // CB
    per = IR // CB
    for t in range(3):
        lanes = slice(t * 128, t * 128 + 128)
        taps = [kernels[k, o : o + 1, lanes] for o in range(9)]

        def step(b, sums9):
            base = (b // per) * STRIDE + 16 + (b % per) * CB
            here = nrm[1, rows_at(base, CB), lanes]
            acc = jnp.zeros((CB, 128), F32)
            new = []
            for o in range(9):
                x = pool[shifted_at(2 - o % 3, t, base - (o // 3 - 1) * 16, CB), :]
                acc = acc + x * taps[o]
                new.append(sums9[o] + jnp.sum((x * here).reshape(CB // 8, 8, 128), 0))
            rows = rows_at(b * CB, CB)
            dn[rows, lanes] = acc if k == 0 else dn[rows, lanes] + acc
            return tuple(new)

        sums9 = lax.fori_loop(0, blocks, step, (jnp.zeros((8, 128), F32),) * 9)
        for o in range(9):
            dker[k * 9 + o : k * 9 + o + 1, lanes] = col_sum(sums9[o])


def last_norm_back(tokp, dres, dn, gains, gtok, dker):
    mask = cell_mask(IR)
    dker[27:32] = jnp.zeros((5, D), F32)

    def step(i, carry):
        rows = rows_at(i * IR, IR)
        xhat, rstd = norm_parts(tokp[rows, :])
        grad = dn[rows, :] * mask
        dker[27:28] = dker[27:28] + col_sum(grad * xhat)
        dker[28:29] = dker[28:29] + col_sum(grad)
        scaled = grad * gains[0:1]
        one = jnp.sum(scaled, -1, keepdims=True) * (1.0 / D)
        two = jnp.sum(scaled * xhat, -1, keepdims=True) * (1.0 / D)
        gtok[rows, :] = dres[rows, :] + rstd * (scaled - one - xhat * two)
        return carry

    lax.fori_loop(0, IMAGES, step, 0)
    gtok[GAP0:R, :] = dres[GAP0:R, :]


HALF = 2 * D
QR = HALF // QUAD


class GradSum:
    def __init__(self, place, unit, src, bufs, sems):
        self.place, self.unit, self.src = place, unit, src
        self.rx_core, self.rx_quad, self.mid, self.rx_z = [b.at[unit] for b in bufs[:4]]
        self.done = bufs[4]
        self.at = unit if unit < 2 else 2 + place.mp
        self.own = src.at[unit, place.mp]
        self.send, self.recv = sems[0].at[unit], sems[1].at[unit]
        self.groups = place.groups
        self.part = -(-QR // (16 * self.groups)) * 16
        self.span = self.part * self.groups

    def core_start(self):
        mine = self.src.at[self.unit, 1 - self.place.mp]
        self.copies = [remote(mine, self.rx_core, self.send.at[0], self.recv.at[0], self.place.other_core())]

    def core_end(self):
        finish(self.copies)
        for b in range(HALF // 64):
            rows = slice(b * 64, b * 64 + 64)
            mine = self.own[rows, :].astype(F32)
            self.own[rows, :] = (mine + self.rx_core[rows, :].astype(F32)).astype(BF)

    def quad_start(self):
        self.copies = []
        for o in range(1, QUAD):
            rows = rows_at(lax.rem(self.place.quad + o, QUAD) * QR, QR)
            self.copies.append(
                remote(self.own.at[rows], self.rx_quad.at[o - 1], self.send.at[o], self.recv.at[o], self.place.in_quad(o))
            )

    def quad_end(self):
        finish(self.copies)
        for b in range(QR // 64):
            rows = slice(b * 64, b * 64 + 64)
            total = self.own[rows_at(self.place.quad * QR + b * 64, 64), :].astype(F32)
            for o in range(QUAD - 1):
                total = total + self.rx_quad[o, rows, :].astype(F32)
            self.mid[rows, :] = total.astype(BF)
        if self.span > QR:
            self.mid[QR:, :] = jnp.zeros((self.span - QR, D), BF)

    def z_start(self):
        self.copies = []
        for o in range(1, self.groups):
            rows = rows_at(lax.rem(self.place.z + o, self.groups) * self.part, self.part)
            at = 3 + o
            self.copies.append(
                remote(self.mid.at[rows], self.rx_z.at[o - 1], self.send.at[at], self.recv.at[at], self.place.along(o))
            )

    def z_end(self):
        finish(self.copies)
        total = self.mid[rows_at(self.place.z * self.part, self.part), :].astype(F32)
        for o in range(self.groups - 1):
            total = total + self.rx_z[o].astype(F32)
        self.done[self.at, self.place.quad, rows_at(self.place.z * self.part, self.part), :] = total.astype(BF)

    def z_back_start(self):
        here = self.done.at[self.at, self.place.quad, rows_at(self.place.z * self.part, self.part)]
        self.copies = []
        for o in range(1, self.groups):
            at = 2 + self.groups + o
            self.copies.append(remote(here, here, self.send.at[at], self.recv.at[at], self.place.along(o)))

    def quad_back_start(self):
        here = self.done.at[self.at, self.place.quad]
        self.copies = []
        for o in range(1, QUAD):
            at = 1 + 2 * self.groups + o
            self.copies.append(remote(here, here, self.send.at[at], self.recv.at[at], self.place.in_quad(o)))

    def core_back_start(self):
        here = self.done.at[self.at]
        at = 1 + 2 * self.groups + QUAD
        self.copies = [remote(here, here, self.send.at[at], self.recv.at[at], self.place.other_core())]

    def end(self):
        finish(self.copies)


    def store(self, out, sem):
        copies = []
        for n in (2, 3) if self.unit == 2 else (self.unit,):
            for q in range(QUAD):
                copy = pltpu.make_async_copy(self.done.at[n, q, pl.ds(0, QR)], out.at[n, q], sem.at[n, q])
                copy.start()
                copies.append(copy)
        return copies


def grad_buffers(groups):
    part = -(-QR // (16 * groups)) * 16
    return [
        pltpu.VMEM((3, HALF, D), BF),
        pltpu.VMEM((3, QUAD - 1, QR, D), BF),
        pltpu.VMEM((3, part * groups, D), BF),
        pltpu.VMEM((3, groups - 1, part, D), BF),
        pltpu.VMEM((4, QUAD, part * groups, D), BF),
    ]


def main_kernel(
    groups, seg, tokens, cot, gains, shifts, kernels, wqkv, wout, win, wmo, bias_h,
    out_hbm, gtok_hbm, dw_hbm, rest_out, sums_out,
    pool, tokp, cotp, conv, nrm, dbn, outp, dres, bn, qkv, att, n2, gm, gr, act, dpre, datt, dqkv,
    wqkv_b, wout_b, win_f, wmo_f, bias_f, stats, moments, sums, small, rest,
    grads, b0, b1, b2, b3, b4, rx1, rx2, rx3, rx4, rx5, rx6,
    in_sems, w_sems, pair_s, pair_r, pair_l, es, er, zs, zr, gs, gr_sem, out_sems, dw_sems,
):
    place = Place(groups)
    place.greet()
    copies = []
    for n, src in enumerate((tokens, cot)):
        for t in range(3):
            copy = pltpu.make_async_copy(
                src.at[0, :, pl.ds(t * 128, 128)], pool.at[pl.ds((n * 3 + t) * SCR, CELLS)], in_sems.at[n, t]
            )
            copy.start()
            copies.append(copy)
    ahead = empty_before(seg)
    finish(copies)
    to_images(pool, 0, tokp, ahead)
    to_images(pool, 3 * SCR, cotp, ahead)
    blocks = [wqkv.at[:, pl.ds(k * D, D)] for k in range(3)] + [wout]
    blocks += [win.at[:, pl.ds(j * D, D)] for j in range(2)] + [wmo.at[pl.ds(j * D, D)] for j in range(2)]
    weights = []
    for n, src in enumerate(blocks):
        copy = pltpu.make_async_copy(src, dbn.at[pl.ds(n * D, D)], w_sems.at[n])
        copy.start()
        weights.append(copy)
    first_norm(tokp, gains, shifts, nrm)
    conv_forward(nrm, kernels, conv, stats)
    place.greeted()

    cells = IMAGES * IMG * IMG
    copies = send_eight(place, stats, rx1, es.at[0], er.at[0])
    rx1[place.slot] = stats[...]
    finish(weights)
    targets = [wqkv_b.at[k] for k in range(3)] + [wout_b]
    targets += [win_f.at[place.mp * 2 + j] for j in range(2)] + [wmo_f.at[place.mp * 2 + j] for j in range(2)]
    for n, dst in enumerate(targets):
        dst[...] = dbn[n * D : n * D + D, :].astype(BF)
    mine = pl.ds(place.mp * 2, 2)
    pairs = [
        remote(ref.at[mine], ref.at[mine], pair_s.at[n], pair_r.at[n], place.other_core())
        for n, ref in enumerate((win_f, wmo_f))
    ]
    pairs.append(remote(bias_h, bias_f.at[place.mp], pair_s.at[2], pair_r.at[2], place.other_core()))
    bias_f[place.mp] = bias_h[...]
    finish(copies)
    mean, m2 = merge_moments(rx1, 8, cells)
    rx2[place.z, 0:3] = mean
    rx2[place.z, 3:6] = m2
    rx2[place.z, 6:8] = jnp.zeros((2, D), F32)
    copies = send_along(place, rx2.at[place.z], rx2, zs.at[0], zr.at[0])
    finish(copies)
    mean, m2 = merge_moments(rx2, groups, 8 * cells)
    moments[0:3] = mean
    moments[3:6] = lax.rsqrt(m2 * (1.0 / (cells * 8 * groups)) + EPS)
    moments[6:8] = jnp.zeros((2, D), F32)

    project(conv, moments, gains, shifts, wqkv_b, bn, qkv)
    attend(qkv, pool, att)
    attend_gap(qkv, att)
    feed_forward_in(tokp, cotp, att, wout_b, gains, shifts, dres, n2, gm, small)
    finish(pairs)

    units = [GradSum(place, u, grads, (b0, b1, b2, b3, b4), (gs, gr_sem)) for u in range(3)]
    acc = dbn.at[pl.ds(0, R)]

    def hidden(j, first=False):
        hidden_tile(j, first, n2, gm, win_f, wmo_f, bias_f, act, dpre, outp, acc, small, grads)

    hidden(0, True)
    hidden(2)
    units[0].core_start()
    hidden(1)
    units[0].core_end()
    units[0].quad_start()
    hidden(3)
    units[1].core_start()
    feed_forward_out(cotp, wout_b, gains, shifts, outp, acc, dres, gr, datt, small)
    stores = [pltpu.make_async_copy(outp, out_hbm, out_sems.at[0])]
    stores[0].start()
    for p in range(3):
        grads[2, 1, D + p * 128 : D + p * 128 + 128, :] = t_dot(att[p], gr[...]).astype(BF)
    units[1].core_end()
    units[1].quad_start()
    attend_back_gap(datt, dqkv)
    attend_back(0, qkv, pool, datt, dqkv)
    units[0].quad_end()
    units[0].z_start()
    attend_back(1, qkv, pool, datt, dqkv)
    units[0].z_end()
    units[0].z_back_start()
    attend_back(2, qkv, pool, datt, dqkv)
    units[1].quad_end()
    units[1].z_start()
    project_back(conv, moments, wqkv_b, dqkv, dbn, sums)
    copies = send_eight(place, sums, rx3, es.at[1], er.at[1])
    rx3[place.slot] = sums[...]
    units[0].end()
    units[0].quad_back_start()
    project_grads(bn, dqkv, grads)
    units[2].core_start()
    finish(copies)
    rx4[place.z] = sum_slots(rx3, 8)
    copies = send_along(place, rx4.at[place.z], rx4, zs.at[1], zr.at[1])
    units[1].z_end()
    units[1].z_back_start()
    conv_back_zero(pool)
    units[2].core_end()
    units[2].quad_start()
    finish(copies)
    sums[...] = sum_slots(rx4, groups)
    sums_out[...] = sums[...]

    def back(k):
        conv_back(
            k, dbn, conv, moments, sums, gains, nrm, pool, kernels, cotp, rest, 1.0 / (cells * 8 * groups)
        )

    back(0)
    units[1].end()
    units[1].quad_back_start()
    back(1)
    units[2].quad_end()
    units[2].z_start()
    back(2)
    units[2].z_end()
    units[2].z_back_start()
    last_norm_back(tokp, dres, cotp, gains, outp_free(stores, outp), rest)
    rest[32:40] = small[...]
    copies = send_eight(place, rest, rx5, es.at[2], er.at[2])
    stores.append(pltpu.make_async_copy(outp, gtok_hbm, out_sems.at[1]))
    stores[-1].start()
    rx5[place.slot] = rest[...]
    units[2].end()
    units[2].quad_back_start()
    finish(copies)
    rx6[place.z] = sum_slots(rx5, 8)
    copies = send_along(place, rx6.at[place.z], rx6, zs.at[2], zr.at[2])
    units[0].end()
    stores += units[0].store(dw_hbm, dw_sems)
    units[1].end()
    stores += units[1].store(dw_hbm, dw_sems)
    finish(copies)
    rest[...] = sum_slots(rx6, groups)
    rest_out[0:36] = rest[0:36]
    rest_out[36:38] = jnp.where(place.mp == 0, rest[36:38], rest[38:40])
    rest_out[38:40] = jnp.zeros((2, D), F32)
    units[2].end()
    units[2].core_back_start()
    units[2].end()
    stores += units[2].store(dw_hbm, dw_sems)
    finish(stores[1:])


def outp_free(stores, outp):
    stores[0].wait()
    return outp


def main_call(groups, *args):
    n = 2 + 2 * groups + QUAD
    return pl.pallas_call(
        functools.partial(main_kernel, groups),
        out_shape=(
            shape(R, D), shape(R, D), shape(4, QUAD, QR, D, dtype=BF), shape(40, D), shape(8, D),
        ),
        in_specs=[VM, ANY, ANY, VM, VM, VM, ANY, ANY, ANY, ANY, VM],
        out_specs=(ANY, ANY, ANY, VM, VM),
        scratch_shapes=[
            pltpu.VMEM((POOL, 128), F32),
            pltpu.VMEM((R, D), F32), pltpu.VMEM((R, D), F32), pltpu.VMEM((3, R, D), F32),
            pltpu.VMEM((3, CONVR, D), F32), pltpu.VMEM((3 * R, D), F32),
            pltpu.VMEM((R, D), F32), pltpu.VMEM((R, D), F32),
            pltpu.VMEM((3, R, D), BF), pltpu.VMEM((3, 3, R, 128), BF), pltpu.VMEM((3, R, 128), BF),
            pltpu.VMEM((R, D), BF), pltpu.VMEM((R, D), BF), pltpu.VMEM((R, D), BF),
            pltpu.VMEM((R, D), BF), pltpu.VMEM((R, D), BF), pltpu.VMEM((3, R, 128), BF), pltpu.VMEM((3, 3, R, 128), BF),
            pltpu.VMEM((3, D, D), BF), pltpu.VMEM((D, D), BF), pltpu.VMEM((4, D, D), BF), pltpu.VMEM((4, D, D), BF),
            pltpu.VMEM((2, 8, D), F32),
            pltpu.VMEM((8, D), F32), pltpu.VMEM((8, D), F32), pltpu.VMEM((8, D), F32), pltpu.VMEM((8, D), F32),
            pltpu.VMEM((40, D), F32),
            pltpu.VMEM((3, 2, HALF, D), BF),
        ] + grad_buffers(groups) + [
            pltpu.VMEM((8, 8, D), F32), pltpu.VMEM((groups, 8, D), F32),
            pltpu.VMEM((8, 8, D), F32), pltpu.VMEM((groups, 8, D), F32),
            pltpu.VMEM((8, 40, D), F32), pltpu.VMEM((groups, 40, D), F32),
            dma(2, 3), dma(8), dma(3), dma(3), dma(2), dma(3, 8), dma(3, 8), dma(3, groups), dma(3, groups),
            dma(3, n), dma(3, n), dma(2), dma(4, QUAD),
        ],
        compiler_params=params(collective_id=0, has_side_effects=True),
    )(*args)


def last_kernel(
    seg, outp, gtok, dw, rest, sums,
    output, grad_tokens, grad_gains, grad_shifts, grad_kernels, grad_qkv, grad_out, grad_in, grad_bias, grad_down,
    scr,
):
    starts, gaps = find_columns(seg)
    for src, dst in ((outp, output), (gtok, grad_tokens)):
        to_canvas(src, scr, starts, gaps)
        for t in range(3):
            dst[0, :, t * 128 : t * 128 + 128] = scr[t, 0:CELLS, :]
    for u in range(2):
        grad_in[:, u * D : u * D + D] = dw[u, 0:D, :].astype(F32)
        grad_down[u * D : u * D + D, :] = dw[u, D : 2 * D, :].astype(F32)
    for k in range(3):
        grad_qkv[:, k * D : k * D + D] = dw[2 + k // 2, (k % 2) * D : (k % 2) * D + D, :].astype(F32)
        grad_kernels[k] = rest[k * 9 : k * 9 + 9]
    grad_out[...] = dw[3, D : 2 * D, :].astype(F32)
    grad_gains[0:1] = rest[27:28]
    grad_gains[1:4] = sums[3:6]
    grad_gains[4:5] = rest[32:33]
    grad_shifts[0:1] = rest[28:29]
    grad_shifts[1:2] = sums[0:1]
    grad_shifts[2:3] = sums[2:3]
    grad_shifts[3:4] = rest[33:34]
    grad_shifts[4:5] = rest[34:35]
    grad_shifts[5:6] = rest[35:36]
    grad_bias[...] = rest[36:38]


def last_call(*args):
    return pl.pallas_call(
        last_kernel,
        out_shape=(
            shape(1, CELLS, D), shape(1, CELLS, D), shape(5, D), shape(6, D), shape(3, 9, D), shape(D, 3 * D),
            shape(D, D), shape(D, 2 * D), shape(2, D), shape(2 * D, D),
        ),
        in_specs=[SM] + [VM] * 5,
        out_specs=(VM,) * 10,
        scratch_shapes=[pltpu.VMEM((3, CELLS + 16, 128), F32)],
        compiler_params=params(),
    )(*args)


def local(
    groups, tokens, segment_ids, gains, shifts, kernels, qkv_weight, out_weight,
    mlp_in_weight, mlp_in_bias, mlp_out_weight, cotangent,
):
    bias_h = jnp.pad(mlp_in_bias.reshape(2, D), ((0, 6), (0, 0)))
    outp, gtok, dw, rest, sums = main_call(
        groups, segment_ids, tokens, cotangent, gains, shifts, kernels,
        qkv_weight, out_weight, mlp_in_weight, mlp_out_weight, bias_h,
    )
    outs = list(last_call(segment_ids, outp, gtok, dw.reshape(4, HALF, D), rest, sums))
    outs[8] = outs[8].reshape(2 * D)
    return tuple(outs)


def solution(mesh):
    groups = mesh.shape["dp"] // QUAD
    both = P(("dp", "mp"), None, None)
    return jax.shard_map(
        functools.partial(local, groups),
        mesh=mesh,
        in_specs=(
            both, P(("dp", "mp"), None), P(), P(), P(), P(), P(), P(None, "mp"), P("mp"), P("mp", None), both,
        ),
        out_specs=(both, both, P(), P(), P(), P(), P(), P(None, "mp"), P("mp"), P("mp", None)),
        check_vma=False,
    )
```

time: 214 us -> 122 us (0.57)
  Pallas kernels: 189 us -> 115 us
  local copies, waits for them, and re-layouts: 15.5 us -> 5.56 us
  other arithmetic: 7.11 us -> 0 us
    pallas_call x7 -> x1, Pallas kernels: 184 us -> 107 us  [main_call(): pl.pallas_call(functools.partial(main_kernel, groups), out_shape=(shape(R...]
    slice x8 -> x0, local copies, waits for them, and re-layouts: 8.01 us -> none  [the longest x1 2.63 us: local(): mine = lax.dynamic_index_in_dim(done[:2], mp, 1, keepdims=False)]
    concatenate x3 -> x0, other arithmetic: 3.05 us -> none  [the longest x1 1.32 us: local(): grad_qkv = jnp.concatenate([done[2, 0, 0], done[2, 0, 1], done[2, 1, 0]], 1)]
    squeeze x3 -> x0, local copies, waits for them, and re-layouts: 2.87 us -> none  [the longest x1 1.82 us: local(): mine = lax.dynamic_index_in_dim(done[:2], mp, 1, keepdims=False)]
    convert_element_type x1 -> x0, other arithmetic: 2.84 us -> none  [local(): done = done.reshape(3, 2, 2, D, D).astype(F32)]
    pallas_call x1, Pallas kernels: 5.45 us -> 8.27 us  [last_call(): pl.pallas_call(last_kernel, out_shape=(shape(1, CELLS, D), shape(1, CELLS...]
where the time goes in v2:
time: 122 us; the launch traced here: 121 us
  Pallas kernels  115 us (94%)
  local copies, waits for them, and re-layouts  5.56 us (5%)
    pallas_call x1, Pallas kernels, main_call(): pl.pallas_call(functools.partial(main_kernel, groups), out_shape=(shape(R...  107 us
    pallas_call x1, Pallas kernels, last_call(): pl.pallas_call(last_kernel, out_shape=(shape(1, CELLS, D), shape(1, CELLS...  8.27 us
    unnamed x2, local copies, waits for them, and re-layouts  2.98 us

profile of v2, /device:TPU:0, one launch (start us, length us, event | category | flops | bytes accessed | tf_op | source)
XLA Modules:
  0.0 121.4 jit_solution(1092005048834316813)
XLA Ops:
  0.6 0.7 reshape.29
  1.3 0.6 pad.4.bias_h
  1.9 1.5 %copy.21.kernels = f32[3,9,384]{2,1,0:T(8,128)} copy(f32[3,9,384]{2,0,1:T(4,128)} %param.15) | data formatting | bytes 82944 | tf_op args[4]
  3.4 106.9 %shard_map.186 = (f32[1024,384]{1,0:T(8,128)}, f32[1024,384]{1,0:T(8,128)}, bf16[4,4,192,384]{3,2,1,0:T(8,128)(2,1)}, f32[40,384]{1,0:T(8,128)}, f32[8,384]{1,0:T(8,128)}) custom-call(s32[1,896]{1,0:T(1,128)} %seg.3, f32[1,896,384]{2,1,0:T(8,128)} %tokens.1, f32[1,896,384]{2,1,0:T(8,128)} %cot.1, f32[5,384]{1,0:T(8,128)} %gains.1, f32[6,384]{1,0:T(8,128)} %shifts.1, ...), custom_call_target="tpu_custom_call" | custom-call | tf_op jit(solution)/shard_map/pallas_call | solution.py:845
  110.3 8.3 %shard_map.187 = (f32[1,896,384]{2,1,0:T(8,128)}, f32[1,896,384]{2,1,0:T(8,128)}, f32[5,384]{1,0:T(8,128)}, f32[6,384]{1,0:T(8,128)}, f32[3,9,384]{2,1,0:T(8,128...) custom-call(s32[1,896]{1,0:T(1,128)} %seg.3, ...), custom_call_target="tpu_custom_call" | custom-call | tf_op jit(solution)/shard_map/pallas_call | solution.py:906
  118.6 1.3 %reshape.31 = f32[768]{0:T(1024)} reshape(f32[2,384]{1,0:T(2,128)} %get-tuple-element.38) | data formatting | bytes 6144 | tf_op jit(solution)/shard_map/reshape | solution.py:929
  119.9 1.5 %copy.22 = f32[3,9,384]{2,0,1:T(4,128)} copy(f32[3,9,384]{2,1,0:T(8,128)} %get-tuple-element.44) | data formatting | bytes 82944

commit v3 on v2

v3 whole, which is shorter than its diff:
```python
import functools
import math

import jax
import jax.numpy as jnp
from jax import lax
from jax.experimental import pallas as pl
from jax.experimental.pallas import tpu as pltpu
from jax.sharding import PartitionSpec as P

F32 = jnp.float32
BF = jnp.bfloat16
MESH = pl.DeviceIdType.MESH
D = 384
IMG = 14
IMAGES = 4
CW = 64
CELLS = IMG * CW
IR = 224
GAP0 = IMAGES * IR
GAPS = 112
R = 1024
CH = 256
STRIDE = IR + 16
CONVR = IMAGES * STRIDE + 16
EPS = 1e-05
MASKED = -1e30
QUAD = 4
HH = 2 * D
VLIM = 62 * 2**20
SCALE = 0.125
PCH = 512


def params(**kw):
    return pltpu.CompilerParams(vmem_limit_bytes=VLIM, **kw)


VM = pl.BlockSpec(memory_space=pltpu.VMEM)
SM = pl.BlockSpec(memory_space=pltpu.SMEM)
ANY = pl.BlockSpec(memory_space=pl.ANY)


def shape(*dims, dtype=F32):
    return jax.ShapeDtypeStruct(dims, dtype)


def dot(a, b):
    return jnp.dot(a, b, preferred_element_type=F32)


def dot_t(a, b):
    return lax.dot_general(a, b, (((1,), (1,)), ((), ())), preferred_element_type=F32)


def t_dot(a, b):
    return lax.dot_general(a, b, (((0,), (0,)), ((), ())), preferred_element_type=F32)


def cell_mask(rows):
    row = lax.broadcasted_iota(jnp.int32, (rows, 1), 0)
    return (row % 16 < IMG).astype(F32)


def rows_at(start, size, align=16):
    return pl.ds(pl.multiple_of(start, align), size)


def find_columns(seg):
    def step(col, found):
        count, starts, gaps = found
        here = seg[0, col]
        starts = tuple(jnp.minimum(s, jnp.where(here == i + 1, col, CW)) for i, s in enumerate(starts))
        empty = here == 0
        gaps = tuple(jnp.where(empty & (count == k), col, g) for k, g in enumerate(gaps))
        return count + jnp.where(empty, 1, 0), starts, gaps

    start = (jnp.int32(0), (jnp.int32(CW),) * IMAGES, (jnp.int32(0),) * 8)
    _, starts, gaps = lax.fori_loop(0, CW, step, start)
    return starts, gaps


SCR = CELLS + 16
POOL = 48 * IR


def empty_before(seg):
    lane = lax.broadcasted_iota(jnp.int32, (1, 128), 1)
    ids = seg[0:1, 0:128]
    firsts = [jnp.where((ids == i + 1) & (lane < CW), lane, CW).astype(F32) for i in range(IMAGES)]
    return [jnp.min(f, -1, keepdims=True) - float(i * IMG) for i, f in enumerate(firsts)]


def to_images(pool, base, out, ahead):
    col = lax.broadcasted_iota(jnp.int32, (16, 128), 0)
    sub = lax.broadcasted_iota(jnp.int32, (8, 128), 0).astype(F32)
    before = sum([jnp.where(a <= sub, 1.0, 0.0) for a in ahead])

    def step(r, carry):
        for t in range(3):
            row = base + t * SCR + r * CW
            for i in range(IMAGES):
                window = pool[pl.ds(row + i * IMG, 16), :]
                for e in range(1, 9):
                    moved = pool[pl.ds(row + i * IMG + e, 16), :]
                    window = jnp.where(ahead[i] == float(e), moved, window)
                out[rows_at(i * IR + r * 16, 16), t * 128 : t * 128 + 128] = jnp.where(col < IMG, window, 0.0)
            block = pool[rows_at(row, 8, 8), :]
            for n in range(1, IMAGES + 1):
                block = jnp.where(before == float(n), pool[pl.ds(row + n * IMG, 8), :], block)
            out[rows_at(GAP0 + r * 8, 8, 8), t * 128 : t * 128 + 128] = block
        return carry

    lax.fori_loop(0, IMG, step, 0)
    out[GAP0 + GAPS : R, :] = jnp.zeros((R - GAP0 - GAPS, D), F32)


def to_canvas(src, scr, starts, gaps):
    def step(r, carry):
        for t in range(3):
            for i in range(IMAGES):
                block = src[rows_at(i * IR + r * 16, 16), t * 128 : t * 128 + 128]
                scr[t, pl.ds(r * CW + starts[i], 16), :] = block
            block = src[rows_at(GAP0 + r * 8, 8, 8), t * 128 : t * 128 + 128]
            for k in range(8):
                scr[t, pl.ds(r * CW + gaps[k], 1), :] = block[k : k + 1]
        return carry

    lax.fori_loop(0, IMG, step, 0)


def norm_parts(x):
    mean = jnp.sum(x, -1, keepdims=True) * (1.0 / D)
    centred = x - mean
    var = jnp.sum(centred * centred, -1, keepdims=True) * (1.0 / D)
    rstd = lax.rsqrt(var + EPS)
    return centred * rstd, rstd


def store_shifted(dst, i, t, x):
    lanes = slice(t * 128, t * 128 + 128)
    at = rows_at(i * STRIDE + 16, IR)
    dst[0, at, lanes] = pltpu.roll(x, 1, 0)
    dst[1, at, lanes] = x
    dst[2, at, lanes] = pltpu.roll(x, IR - 1, 0)


def zero_borders(dst):
    for i in range(IMAGES + 1):
        for c in range(3):
            dst[c, i * STRIDE : i * STRIDE + 16, :] = jnp.zeros((16, D), F32)


def first_norm(tokp, gains, shifts, nrm):
    zero_borders(nrm)
    mask = cell_mask(IR)

    def step(i, carry):
        xhat, _ = norm_parts(tokp[rows_at(i * IR, IR), :])
        normed = (xhat * gains[0:1] + shifts[0:1]) * mask
        for t in range(3):
            store_shifted(nrm, i, t, normed[:, t * 128 : t * 128 + 128])
        return carry

    lax.fori_loop(0, IMAGES, step, 0)


CB = 224


def conv_forward(nrm, kernels, conv, stats):
    mask = cell_mask(CB)
    blocks = IMAGES * IR // CB
    per = IR // CB
    for t in range(3):
        lanes = slice(t * 128, t * 128 + 128)
        taps = [[kernels[o, k : k + 1, lanes] for o in range(9)] for k in range(3)]

        def step(b, sums):
            base = (b // per) * STRIDE + 16 + (b % per) * CB
            acc = [jnp.zeros((CB, 128), F32)] * 3
            for o in range(9):
                x = nrm[o % 3, rows_at(base + (o // 3 - 1) * 16, CB), lanes]
                for k in range(3):
                    acc[k] = acc[k] + x * taps[k][o]
            new = []
            for k in range(3):
                conv[k, rows_at(b * CB, CB), lanes] = acc[k]
                new.append(sums[k] + jnp.sum((acc[k] * mask).reshape(CB // 8, 8, 128), 0))
            return tuple(new)

        sums = lax.fori_loop(0, blocks, step, (jnp.zeros((8, 128), F32),) * 3)
        means = [jnp.sum(s, 0, keepdims=True) * (1.0 / (IMAGES * IMG * IMG)) for s in sums]

        def spread(b, sums):
            new = []
            for k in range(3):
                away = (conv[k, rows_at(b * CB, CB), lanes] - means[k]) * mask
                new.append(sums[k] + jnp.sum((away * away).reshape(CB // 8, 8, 128), 0))
            return tuple(new)

        squares = lax.fori_loop(0, blocks, spread, (jnp.zeros((8, 128), F32),) * 3)
        for k in range(3):
            stats[k : k + 1, lanes] = means[k]
            stats[3 + k : 4 + k, lanes] = jnp.sum(squares[k], 0, keepdims=True)
        stats[6:8, lanes] = jnp.zeros((2, 128), F32)
    for k in range(3):
        conv[k, GAP0:R, :] = jnp.zeros((R - GAP0, D), F32)


class Place:
    def __init__(self, groups):
        dp = lax.axis_index("dp")
        self.mp = lax.axis_index("mp")
        self.groups = groups
        self.quad = lax.rem(dp, QUAD)
        self.z = dp // QUAD
        self.slot = self.quad * 2 + self.mp

    def in_eight(self, offset):
        other = lax.rem(self.slot + offset, 8)
        return (self.z * QUAD + other // 2, lax.rem(other, 2))

    def in_quad(self, offset):
        return (self.z * QUAD + lax.rem(self.quad + offset, QUAD), self.mp)

    def along(self, offset):
        return (lax.rem(self.z + offset, self.groups) * QUAD + self.quad, self.mp)

    def other_core(self):
        return (self.z * QUAD + self.quad, 1 - self.mp)

    def peers(self):
        return [self.in_eight(o) for o in range(1, 8)] + [self.along(o) for o in range(1, self.groups)]

    def greet(self):
        barrier = pltpu.get_barrier_semaphore()
        for peer in self.peers():
            pl.semaphore_signal(barrier, inc=1, device_id=peer, device_id_type=MESH)

    def greeted(self):
        pl.semaphore_wait(pltpu.get_barrier_semaphore(), 7 + self.groups - 1)


def remote(src, dst, send, recv, peer):
    copy = pltpu.make_async_remote_copy(
        src_ref=src, dst_ref=dst, send_sem=send, recv_sem=recv, device_id=peer, device_id_type=MESH
    )
    copy.start()
    return copy


def send_eight(place, src, rx, send, recv):
    for o in range(1, 8):
        remote(src, rx.at[place.slot], send, recv, place.in_eight(o))
    return Pending(rx.at[pl.ds(0, 7)], send, recv)


def send_along(place, src, rx, send, recv):
    for o in range(1, place.groups):
        remote(src, rx.at[place.z], send, recv, place.along(o))
    return Pending(rx.at[pl.ds(0, place.groups - 1)], send, recv)


class Pending:
    def __init__(self, ref, send, recv):
        self.ref, self.sems = ref, (send, recv)

    def wait(self):
        for sem in self.sems:
            pltpu.make_async_copy(self.ref, self.ref, sem).wait()


def finish(copies):
    for copy in copies if isinstance(copies, list) else [copies]:
        copy.wait()


def sum_slots(rx, count):
    total = rx[0]
    for s in range(1, count):
        total = total + rx[s]
    return total


class SmallSum:
    def __init__(self, place, src, rx1, rx2, sems, n, done):
        self.place, self.src, self.rx1, self.rx2, self.done = place, src, rx1, rx2, done
        self.sems = [sems.at[n, i] for i in range(3)]
        self.steps = [self.middle, self.end]

    def start(self):
        self.copies = send_eight(self.place, self.src, self.rx1, self.sems[0], self.sems[1])
        self.rx1[self.place.slot] = self.src[...]

    def step(self):
        self.steps.pop(0)()

    def middle(self):
        finish(self.copies)
        self.rx2[self.place.z] = sum_slots(self.rx1, 8)
        self.copies = send_along(self.place, self.rx2.at[self.place.z], self.rx2, self.sems[0], self.sems[2])

    def end(self):
        finish(self.copies)
        self.done(sum_slots(self.rx2, self.place.groups))


def merge_moments(rx, count, cells):
    mean = sum([rx[s, 0:3] for s in range(1, count)], rx[0, 0:3]) * (1.0 / count)
    m2 = sum([rx[s, 3:6] for s in range(1, count)], rx[0, 3:6])
    for s in range(count):
        away = rx[s, 0:3] - mean
        m2 = m2 + away * away * float(cells)
    return mean, m2


def dma(*n):
    return pltpu.SemaphoreType.DMA(n)


def project(conv, moments, gains, shifts, wqkv, bn, qkv):
    def step(c, carry):
        rows = rows_at(c * CH, CH)
        for k in range(3):
            standard = (conv[k, rows, :] - moments[k : k + 1]) * moments[3 + k : 4 + k]
            value = standard * gains[1 + k : 2 + k]
            if k != 1:
                value = value + (shifts[1:2] if k == 0 else shifts[2:3])
            value = value.astype(BF)
            bn[k, rows, :] = value
            out = dot(value, wqkv[k]).astype(BF)
            if k == 0:
                out = (out * SCALE).astype(BF)
            for p in range(3):
                qkv[k, p, rows, :] = out[:, p * 128 : p * 128 + 128]
        return carry

    lax.fori_loop(0, R // CH, step, 0)


def key_bias():
    row = lax.broadcasted_iota(jnp.int32, (16, 256), 0)
    return jnp.where(row < IMG, 0.0, MASKED)


def query_mask():
    lane = lax.broadcasted_iota(jnp.int32, (1, 256), 1)
    return (lane < IR).astype(F32)


def by_head(x):
    lane = lax.broadcasted_iota(jnp.int32, x.shape, 1)
    zero = jnp.zeros_like(x)
    return jnp.concatenate([jnp.where(lane < 64, x, zero), jnp.where(lane < 64, zero, x)], 0)


def own_columns(x, rows):
    lane = lax.broadcasted_iota(jnp.int32, (IR, 128), 1)
    return jnp.where(lane < 64, x[:IR], x[rows : rows + IR])


def probs_at(pool, n):
    return [rows_at((2 * n + half) * IR, IR) for half in range(2)]


def attend(qkv, pool, att):
    bias = key_bias()[None]
    live = query_mask()

    def step(i, carry):
        rows = rows_at(i * IR, IR)
        for p in range(3):
            q = qkv[0, p, rows_at(i * IR, 256), :]
            both = dot_t(by_head(qkv[1, p, rows, :]), q)
            low = []
            for h in range(2):
                scores = (both[h * IR : h * IR + IR].reshape(IMG, 16, 256) + bias).reshape(IR, 256)
                largest = jnp.max(scores, 0, keepdims=True)
                expo = jnp.exp(scores - largest)
                soft = expo * (live / jnp.sum(expo, 0, keepdims=True))
                for half, at in enumerate(probs_at(pool, (i * 3 + p) * 2 + h)):
                    pool[at, :] = soft[:, half * 128 : half * 128 + 128]
                low.append(soft.astype(BF))
            out = t_dot(jnp.concatenate(low, 1), qkv[2, p, rows, :])
            att[p, rows, :] = own_columns(out, 256).astype(BF)
        return carry

    lax.fori_loop(0, IMAGES, step, 0)


def even_prob():
    return jnp.full((1, 1), 1.0 / GAPS, F32).astype(BF).astype(F32)


def attend_gap(qkv, att):
    for p in range(3):
        v = qkv[2, p, GAP0 : GAP0 + 16, :].astype(F32)
        out = (v * (even_prob() * float(GAPS))).astype(BF)
        for b in range((R - GAP0) // 16):
            att[p, GAP0 + b * 16 : GAP0 + b * 16 + 16, :] = out


def gelu_parts(x):
    cdf = 0.5 * (1.0 + lax.erf(x * (1.0 / math.sqrt(2.0))))
    density = jnp.exp(x * x * -0.5) * (1.0 / math.sqrt(2.0 * math.pi))
    return x * cdf, cdf + x * density


def col_sum(x):
    return jnp.sum(x, 0, keepdims=True)


def feed_forward_in(tokp, cotp, att, wout, gains, shifts, dres, n2, gm, small):
    small[...] = jnp.zeros((8, D), F32)

    def step(c, carry):
        rows = rows_at(c * CH, CH)
        attended = jnp.concatenate([att[p, rows, :] for p in range(3)], 1)
        residual = tokp[rows, :] + (dot(attended, wout[...]) + shifts[3:4])
        dres[rows, :] = residual
        xhat, _ = norm_parts(residual)
        n2[rows, :] = (xhat * gains[4:5] + shifts[4:5]).astype(BF)
        cot = cotp[rows, :]
        gm[rows, :] = cot.astype(BF)
        small[3:4] = small[3:4] + col_sum(cot)
        return carry

    lax.fori_loop(0, R // CH, step, 0)


HCH = 512
PARTS = 3
PW = HH // PARTS
BIAS_TILES = 2 * HH // 128


def hidden_part(part, n2, gm, win, wmo, bias, act, dpre, outp, acc, dbias):
    both = slice(0, 2 * PW)
    dbias[part, 0:1, :] = jnp.zeros((1, 2 * PW), F32)

    def step(c, carry):
        rows = rows_at(c * HCH, HCH)
        up = jnp.concatenate([win[part, h] for h in range(2)], 1)
        down = wmo[part].reshape(2 * PW, D)
        shift = jnp.concatenate([bias[h, 0:1, part * PW : part * PW + PW] for h in range(2)], 1)
        value, slope = gelu_parts(dot(n2[rows, :], up) + shift)
        value = value.astype(BF)
        act[rows, both] = value
        grad = dot_t(gm[rows, :], down) * slope
        dbias[part, 0:1, both] = dbias[part, 0:1, both] + col_sum(grad)
        grad = grad.astype(BF)
        dpre[rows, both] = grad
        forward = dot(value, down)
        back = dot_t(grad, up)
        outp[rows, :] = forward if part == 0 else outp[rows, :] + forward
        acc[rows, :] = back if part == 0 else acc[rows, :] + back
        return carry

    lax.fori_loop(0, R // HCH, step, 0)


def hidden_grads(half, n2, gm, act, dpre, grads):
    units = pl.ds(pl.multiple_of(half * PW, 128), PW)
    grads[half, 0:PW, :] = t_dot(dpre[:, units], n2[...]).astype(BF)
    grads[half, PW : 2 * PW, :] = t_dot(act[:, units], gm[...]).astype(BF)


def feed_forward_out(cotp, wout, gains, shifts, outp, acc, dres, gr, datt, small):
    def step(c, carry):
        rows = rows_at(c * CH, CH)
        residual = dres[rows, :]
        outp[rows, :] = residual + outp[rows, :] + shifts[5:6]
        xhat, rstd = norm_parts(residual)
        grad = acc[rows, :]
        scaled = grad * gains[4:5]
        one = jnp.sum(scaled, -1, keepdims=True) * (1.0 / D)
        two = jnp.sum(scaled * xhat, -1, keepdims=True) * (1.0 / D)
        total = cotp[rows, :] + rstd * (scaled - one - xhat * two)
        dres[rows, :] = total
        low = total.astype(BF)
        gr[rows, :] = low
        back = dot_t(low, wout[...]).astype(BF)
        for p in range(3):
            datt[p, rows, :] = back[:, p * 128 : p * 128 + 128]
        small[0:1] = small[0:1] + col_sum(grad * xhat)
        small[1:2] = small[1:2] + col_sum(total)
        small[2:3] = small[2:3] + col_sum(grad)
        return carry

    lax.fori_loop(0, R // CH, step, 0)


def attend_back_values(pool, datt, dqkv):
    def step(i, carry):
        rows = rows_at(i * IR, IR)
        for p in range(3):
            low = []
            for h in range(2):
                soft = [pool[at, :] for at in probs_at(pool, (i * 3 + p) * 2 + h)]
                low.append(jnp.concatenate(soft, 1).astype(BF))
            dv = dot(jnp.concatenate(low, 0), datt[p, rows_at(i * IR, 256), :])
            dqkv[2, p, rows, :] = own_columns(dv, IR).astype(BF)
        return carry

    lax.fori_loop(0, IMAGES, step, 0)


def attend_back(first, last, qkv, pool, datt, dqkv):
    def step(i, carry):
        rows = rows_at(i * IR, IR)
        wide = rows_at(i * IR, 256)
        for p in range(3):
            both = dot_t(by_head(qkv[2, p, rows, :]), datt[p, wide, :])
            ds = []
            for h in range(2):
                soft = jnp.concatenate([pool[at, :] for at in probs_at(pool, (i * 3 + p) * 2 + h)], 1)
                grad = both[h * IR : h * IR + IR]
                delta = jnp.sum(soft * grad, 0, keepdims=True)
                ds.append((soft * (grad - delta)).astype(BF))
            dk = dot(jnp.concatenate(ds, 0), qkv[0, p, wide, :])
            dq = t_dot(jnp.concatenate(ds, 1), qkv[1, p, rows, :])
            dqkv[0, p, rows, :] = (own_columns(dq, 256) * SCALE).astype(BF)
            dqkv[1, p, rows, :] = own_columns(dk, IR).astype(BF)
        return carry

    lax.fori_loop(first, last, step, 0)


def attend_back_gap(datt, dqkv):
    for p in range(3):
        total = col_sum(datt[p, GAP0 : GAP0 + GAPS, :].astype(F32))
        grad = jnp.broadcast_to((total * even_prob()).astype(BF), (16, 128))
        zero = jnp.zeros((16, 128), BF)
        for b in range((R - GAP0) // 16):
            rows = slice(GAP0 + b * 16, GAP0 + b * 16 + 16)
            dqkv[0, p, rows, :] = zero
            dqkv[1, p, rows, :] = zero
            dqkv[2, p, rows, :] = grad if b < GAPS // 16 else zero


def project_back(k, conv, moments, wqkv, dqkv, dbn, sums, one, two):
    sums[one : one + 1] = jnp.zeros((1, D), F32)
    sums[two : two + 1] = jnp.zeros((1, D), F32)

    def step(c, carry):
        rows = rows_at(c * PCH, PCH)
        grad = jnp.concatenate([dqkv[k, p, rows, :] for p in range(3)], 1)
        back = dot_t(grad, wqkv[k])
        dbn[rows_at(k * R + c * PCH, PCH), :] = back
        standard = (conv[k, rows, :] - moments[k : k + 1]) * moments[3 + k : 4 + k]
        sums[one : one + 1] = sums[one : one + 1] + col_sum(back)
        sums[two : two + 1] = sums[two : two + 1] + col_sum(back * standard)
        return carry

    lax.fori_loop(0, R // PCH, step, 0)


def project_grads(k, bn, dqkv, grads):
    for p in range(3):
        grads[:, p * 128 : p * 128 + 128] = t_dot(bn[k], dqkv[k, p]).astype(BF)


def shifted_at(c, t, row, size):
    return rows_at((c * 3 + t) * CONVR + row, size)


def conv_back_zero(pool):
    for c in range(3):
        for t in range(3):
            for i in range(IMAGES + 1):
                pool[shifted_at(c, t, i * STRIDE, 16), :] = jnp.zeros((16, 128), F32)


CONV_ROWS = 16


def conv_back(k, first, last, dbn, conv, moments, one, two, gains, shifts, nrm, pool, kernels, dn, dker, inverse_total):
    mask = cell_mask(IR)
    cells = cell_mask(CB)

    def spread(i, carry):
        rows = rows_at(i * IR, IR)
        for t in range(3):
            lanes = slice(t * 128, t * 128 + 128)
            inv = moments[3 + k : 4 + k, lanes]
            standard = (conv[k, rows, lanes] - moments[k : k + 1, lanes]) * inv
            shift = (one[:, lanes] + standard * two[:, lanes]) * inverse_total
            grad = dbn[rows_at(k * R + i * IR, IR), lanes]
            grad = (gains[1 + k : 2 + k, lanes] * inv) * (grad - mask * shift)
            pool[shifted_at(0, t, i * STRIDE + 16, IR), :] = pltpu.roll(grad, 1, 0)
            pool[shifted_at(1, t, i * STRIDE + 16, IR), :] = grad
            pool[shifted_at(2, t, i * STRIDE + 16, IR), :] = pltpu.roll(grad, IR - 1, 0)
        return carry

    lax.fori_loop(0, IMAGES, spread, 0)
    blocks = IMAGES * IR // CB
    per = IR // CB
    for t in range(3):
        lanes = slice(t * 128, t * 128 + 128)
        taps = [kernels[o, k : k + 1, lanes] for o in range(9)]

        def step(b, sums9):
            base = (b // per) * STRIDE + 16 + (b % per) * CB
            here = nrm[1, rows_at(base, CB), lanes]
            acc = jnp.zeros((CB, 128), F32)
            new = []
            for o in range(9):
                x = pool[shifted_at(2 - o % 3, t, base - (o // 3 - 1) * 16, CB), :]
                acc = acc + x * taps[o]
                new.append(sums9[o] + jnp.sum((x * here).reshape(CB // 8, 8, 128), 0))
            rows = rows_at(b * CB, CB)
            if not first:
                acc = acc + dn[rows, lanes]
            dn[rows, lanes] = acc
            if last:
                new.append(sums9[9] + jnp.sum((acc * here).reshape(CB // 8, 8, 128), 0))
                new.append(sums9[10] + jnp.sum((acc * cells).reshape(CB // 8, 8, 128), 0))
            return tuple(new)

        found = lax.fori_loop(0, blocks, step, (jnp.zeros((8, 128), F32),) * (11 if last else 9))
        found = [col_sum(f) for f in found]
        for o in range(9):
            dker[k, o : o + 1, lanes] = found[o]
        if last:
            dker[k, 9:10, lanes] = (found[9] - found[10] * shifts[0:1, lanes]) / gains[0:1, lanes]
            dker[k, 10:11, lanes] = found[10]


def last_norm_back(tokp, dres, dn, gains, gtok):
    mask = cell_mask(IR)

    def step(i, carry):
        rows = rows_at(i * IR, IR)
        xhat, rstd = norm_parts(tokp[rows, :])
        scaled = dn[rows, :] * mask * gains[0:1]
        one = jnp.sum(scaled, -1, keepdims=True) * (1.0 / D)
        two = jnp.sum(scaled * xhat, -1, keepdims=True) * (1.0 / D)
        gtok[rows, :] = dres[rows, :] + rstd * (scaled - one - xhat * two)
        return carry

    lax.fori_loop(0, IMAGES, step, 0)
    gtok[GAP0:R, :] = dres[GAP0:R, :]


class GradSum:
    def __init__(self, place, grads, bufs, sems, both):
        self.place, self.grads, self.both = place, grads, both
        self.rx_core, self.rx_one, self.mid, self.rx_z, self.fin, self.done = bufs
        self.own = grads.at[place.mp]
        self.slot = place.mp if both else 0
        self.rows = grads.shape[1]
        self.quarter = self.rows // QUAD
        self.part = z_part(self.rows, place.groups)
        self.block = min(self.quarter, 128)
        self.sems = sems
        self.stage = 0
        self.pending = []
        self.steps = [[self.core_start], [self.core_end, self.quad_start], [self.quad_end, self.z_start]]
        self.steps += [[self.z_end, self.z_back_start], [self.z_back_end, self.quad_back_start]]
        self.steps += [[self.end, self.core_back_start], [self.end]] if both else [[self.end]]

    def step(self):
        for part in self.steps.pop(0):
            part()

    def copies(self, ref, triples):
        self.stage += 1
        for src, dst, peer in triples:
            remote(src, dst, self.sems.at[0], self.sems.at[self.stage], peer)
        self.pending = [Pending(ref, self.sems.at[0], self.sems.at[self.stage])]

    def end(self):
        finish(self.pending)
        self.pending = []

    def add(self, dst, dst_at, mine, mine_at, theirs, rows, lanes):
        def step(b, carry):
            at = b * self.block
            total = mine[rows_at(mine_at + at, self.block), lanes].astype(F32)
            for ref in theirs:
                total = total + ref[rows_at(at, self.block), lanes].astype(F32)
            dst[rows_at(dst_at + at, self.block), lanes] = total.astype(BF)
            return carry

        lax.fori_loop(0, rows // self.block, step, 0)

    def core_start(self):
        self.copies(self.rx_core, [(self.grads.at[1 - self.place.mp], self.rx_core, self.place.other_core())])

    def core_end(self):
        self.end()
        self.add(self.own, 0, self.own, 0, [self.rx_core], self.rows, slice(None))

    def fill(self):
        if self.part * self.place.groups > self.quarter:
            self.mid[self.quarter :, :] = jnp.zeros((self.part * self.place.groups - self.quarter, D), BF)

    def quad_start(self):
        triples = []
        for o in range(1, QUAD):
            there = rows_at(lax.rem(self.place.quad + o, QUAD) * self.quarter, self.quarter)
            triples.append((self.own.at[there], self.rx_one.at[o - 1], self.place.in_quad(o)))
        self.copies(self.rx_one, triples)

    def quad_end(self):
        self.end()
        theirs = [self.rx_one.at[o] for o in range(QUAD - 1)]
        self.add(self.mid, 0, self.own, self.place.quad * self.quarter, theirs, self.quarter, slice(None))
        self.fill()

    def z_start(self):
        triples = []
        for o in range(1, self.place.groups):
            there = rows_at(lax.rem(self.place.z + o, self.place.groups) * self.part, self.part)
            triples.append((self.mid.at[there], self.rx_z.at[o - 1], self.place.along(o)))
        self.copies(self.rx_z, triples)

    def z_end(self):
        self.end()
        here = rows_at(self.place.z * self.part, self.part)
        total = self.mid[here, :].astype(F32)
        for o in range(self.place.groups - 1):
            total = total + self.rx_z[o].astype(F32)
        self.fin[here, :] = total.astype(BF)

    def z_back_start(self):
        here = self.fin.at[rows_at(self.place.z * self.part, self.part)]
        self.copies(self.rx_z, [(here, here, self.place.along(o)) for o in range(1, self.place.groups)])

    def z_back_end(self):
        self.end()
        here = rows_at(self.place.quad * self.quarter, self.quarter)
        self.done[self.slot, here, :] = self.fin[0 : self.quarter, :]

    def quad_back_start(self):
        here = self.done.at[self.slot, rows_at(self.place.quad * self.quarter, self.quarter)]
        self.copies(self.rx_one, [(here, here, self.place.in_quad(o)) for o in range(1, QUAD)])

    def core_back_start(self):
        here = self.done.at[self.place.mp]
        self.copies(self.rx_core, [(here, here, self.place.other_core())])


def z_part(rows, groups):
    return -(-rows // QUAD // (16 * groups)) * 16


UNITS = ((2 * PW, False), (2 * PW, False), (2 * PW, False), (D, True), (D, True))


def unit_buffers(groups, rows, both):
    span = z_part(rows, groups) * groups
    dims = [(rows, D), (QUAD - 1, rows // QUAD, D), (span, D)]
    dims += [(groups - 1, span // groups, D), (span, D), (2 if both else 1, rows, D)]
    return [pltpu.VMEM((2, rows, D), BF)] + [pltpu.VMEM(d, BF) for d in dims]


def main_kernel(
    groups, seg, tokens, cot, gains, shifts, kernels, wqkv, wout, win, wmo, bias_h,
    out_hbm, gtok_hbm, dw0, dw1, dw2, dw3, dw4, rest_out,
    pool, tokp, cotp, conv, nrm, dbn, outp, dres, bn, qkv, att, n2, gm, gr, act, dpre, datt, dqkv,
    wqkv_b, wout_b, win_f, wmo_f, bias_f, stats, moments, sums, sums_v, small, dbias, dker,
    mx1, mx2, sx1, sx2, lx1, lx2, vx1, vx2, kx1, kx2,
    in_sems, w_sems, pair_s, pair_r, sems, unit_sems, out_sems, dw_sems, *unit_flat,
):
    dws = (dw0, dw1, dw2, dw3, dw4)
    unit_refs = [unit_flat[n * 7 : n * 7 + 7] for n in range(len(UNITS))]
    place = Place(groups)
    place.greet()
    copies = []
    for n, src in enumerate((tokens, cot)):
        for t in range(3):
            copy = pltpu.make_async_copy(
                src.at[0, :, pl.ds(t * 128, 128)], pool.at[pl.ds((n * 3 + t) * SCR, CELLS)], in_sems.at[n, t]
            )
            copy.start()
            copies.append(copy)
    blocks = [(wqkv.at[:, pl.ds(k * D, D)], dbn.at[pl.ds(k * D, D)]) for k in range(3)]
    blocks.append((wout, dbn.at[pl.ds(3 * D, D)]))
    for j in range(PARTS):
        blocks.append((win.at[:, pl.ds(j * PW, PW)], dbn.at[pl.ds((4 + j) * D, D), pl.ds(0, PW)]))
    blocks.append((wmo, dres.at[pl.ds(0, HH)]))
    weights = []
    for n, (src, dst) in enumerate(blocks):
        copy = pltpu.make_async_copy(src, dst, w_sems.at[n])
        copy.start()
        weights.append(copy)
    ahead = empty_before(seg)
    finish(copies)
    to_images(pool, 0, tokp, ahead)
    first_norm(tokp, gains, shifts, nrm)
    conv_forward(nrm, kernels, conv, stats)
    place.greeted()

    cells = IMAGES * IMG * IMG
    copies = send_eight(place, stats, mx1, sems.at[0, 0], sems.at[0, 1])
    mx1[place.slot] = stats[...]
    finish(weights)
    for k in range(3):
        wqkv_b[k] = dbn[k * D : k * D + D, :].astype(BF)
    wout_b[...] = dbn[3 * D : 4 * D, :].astype(BF)
    for j in range(PARTS):
        win_f[j, place.mp] = dbn[(4 + j) * D : (5 + j) * D, 0:PW].astype(BF)
        wmo_f[j, place.mp] = dres[j * PW : j * PW + PW, :].astype(BF)
    bias_f[place.mp] = jnp.broadcast_to(bias_h[...].reshape(1, HH), (8, HH))
    pairs = [
        remote(ref, ref, pair_s.at[n], pair_r.at[n], place.other_core())
        for n, ref in enumerate((win_f.at[:, place.mp], wmo_f.at[:, place.mp], bias_f.at[place.mp]))
    ]
    to_images(pool, 3 * SCR, cotp, ahead)
    finish(copies)
    mean, m2 = merge_moments(mx1, 8, cells)
    mx2[place.z, 0:3] = mean
    mx2[place.z, 3:6] = m2
    mx2[place.z, 6:8] = jnp.zeros((2, D), F32)
    finish(send_along(place, mx2.at[place.z], mx2, sems.at[0, 0], sems.at[0, 2]))
    mean, m2 = merge_moments(mx2, groups, 8 * cells)
    moments[0:3] = mean
    moments[3:6] = lax.rsqrt(m2 * (1.0 / (cells * 8 * groups)) + EPS)
    moments[6:8] = jnp.zeros((2, D), F32)

    project(conv, moments, gains, shifts, wqkv_b, bn, qkv)
    attend(qkv, pool, att)
    attend_gap(qkv, att)
    feed_forward_in(tokp, cotp, att, wout_b, gains, shifts, dres, n2, gm, small)
    finish(pairs)

    units = []
    for n, (rows, both) in enumerate(UNITS):
        units.append(GradSum(place, unit_refs[n][0], unit_refs[n][1:], unit_sems.at[n], both))
    ua, ub, ue, uc, ud = units
    grads = [refs[0] for refs in unit_refs]
    acc = dbn.at[pl.ds(0, R)]
    mine, theirs = place.mp, 1 - place.mp
    stores = []

    def keep(at, ref=None):
        def done(total):
            rest_out[at : at + total.shape[0]] = total
            if ref is not None:
                ref[...] = total

        return done

    def keep_small(total):
        rest_out[8:16] = total
        tiles = [total[4 + c // 3 : 5 + c // 3, c % 3 * 128 : c % 3 * 128 + 128] for c in range(BIAS_TILES)]
        for c in range(BIAS_TILES // 2):
            at = c // 2 * 4 + c % 2
            kept = jnp.where(place.mp == 0, tiles[at], tiles[at + 2])
            rest_out[72 + c // 2 : 73 + c // 2, c % 2 * 128 : c % 2 * 128 + 128] = kept

    small_sum = SmallSum(place, small, lx1, lx2, sems, 2, keep_small)
    sum_v = SmallSum(place, sums_v, vx1, vx2, sems, 6, keep(64, sums_v))
    sum_qk = SmallSum(place, sums, sx1, sx2, sems, 1, keep(0, sums))
    ker_sums = [SmallSum(place, dker.at[k], kx1.at[k], kx2.at[k], sems, 3 + k, keep(16 + 16 * k)) for k in range(3)]

    def forward(part):
        hidden_part(part, n2, gm, win_f, wmo_f, bias_f, act, dpre, outp, acc, dbias)

    def hidden(half, part):
        hidden_grads(half, n2, gm, act, dpre, grads[part])
        if half is theirs:
            units[part].step()

    def values():
        attend_back_values(pool, datt, dqkv)
        attend_back_gap(datt, dqkv)

    def after_forward():
        feed_forward_out(cotp, wout_b, gains, shifts, outp, acc, dres, gr, datt, small)
        for c in range(BIAS_TILES):
            tile = slice(c % 4 * 128, c % 4 * 128 + 128)
            small[4 + c // 3 : 5 + c // 3, c % 3 * 128 : c % 3 * 128 + 128] = dbias[c // 4, 0:1, tile]
        small_sum.start()
        stores.append(pltpu.make_async_copy(outp, out_hbm, out_sems.at[0]))
        stores[0].start()

    def out_grad():
        for p in range(3):
            grads[3][1, p * 128 : p * 128 + 128, :] = t_dot(att[p], gr[...]).astype(BF)

    def value_grads():
        project_grads(2, bn, dqkv, grads[3].at[0])
        uc.step()

    def query_grads():
        for k in range(2):
            project_grads(k, bn, dqkv, grads[4].at[k])
        ud.step()

    def value_back():
        project_back(2, conv, moments, wqkv_b, dqkv, dbn, sums_v, 0, 1)
        sum_v.start()

    def query_back():
        for k in range(2):
            project_back(k, conv, moments, wqkv_b, dqkv, dbn, sums, k, 2 + k)
        sum_qk.start()
        conv_back_zero(pool)

    def back(k, begin=False, last=False):
        one, two = (sums_v[0:1], sums_v[1:2]) if k == 2 else (sums[k : k + 1], sums[2 + k : 3 + k])
        conv_back(
            k, begin, last, dbn, conv, moments, one, two, gains, shifts, nrm, pool, kernels, cotp, dker,
            1.0 / (cells * 8 * groups),
        )
        ker_sums[k].start()

    def last_norm():
        stores[0].wait()
        last_norm_back(tokp, dres, cotp, gains, outp)
        stores.append(pltpu.make_async_copy(outp, gtok_hbm, out_sems.at[1]))
        stores[-1].start()

    def unit(n):
        units[n].step()
        if not units[n].steps:
            stores.append(pltpu.make_async_copy(units[n].done, dws[n], dw_sems.at[n]))
            stores[-1].start()

    forward(0)
    hidden(theirs, 0)
    hidden(mine, 0)
    forward(1)
    unit(0)
    hidden(theirs, 1)
    hidden(mine, 1)
    forward(2)
    unit(1)
    hidden(theirs, 2)
    hidden(mine, 2)
    after_forward()
    unit(0)
    unit(2)
    values()
    out_grad()
    value_grads()
    unit(1)
    value_back()
    small_sum.step()
    unit(0)
    unit(3)
    attend_back(0, 2, qkv, pool, datt, dqkv)
    unit(1)
    unit(2)
    attend_back(2, 4, qkv, pool, datt, dqkv)
    unit(0)
    small_sum.step()
    sum_v.step()
    unit(3)
    query_grads()
    query_back()
    unit(4)
    unit(1)
    unit(0)
    unit(2)
    sum_qk.step()
    sum_v.step()
    back(2, begin=True)
    unit(4)
    unit(3)
    unit(2)
    sum_qk.step()
    back(1)
    unit(4)
    unit(1)
    ker_sums[2].step()
    back(0, last=True)
    unit(3)
    last_norm()
    unit(2)
    unit(4)
    ker_sums[1].step()
    ker_sums[0].step()
    ker_sums[2].step()
    unit(3)
    unit(3)
    ker_sums[1].step()
    unit(4)
    ker_sums[0].step()
    unit(4)
    finish(stores[1:])


def main_call(groups, *args):
    units = [buf for unit in UNITS for buf in unit_buffers(groups, *unit)]
    return pl.pallas_call(
        functools.partial(main_kernel, groups),
        out_shape=(shape(R, D), shape(R, D))
        + tuple(shape(2 if both else 1, rows, D, dtype=BF) for rows, both in UNITS)
        + (shape(80, D),),
        in_specs=[VM, ANY, ANY, VM, VM, VM, ANY, ANY, ANY, ANY, VM],
        out_specs=(ANY,) * 7 + (VM,),
        scratch_shapes=[
            pltpu.VMEM((POOL, 128), F32),
            pltpu.VMEM((R, D), F32), pltpu.VMEM((R, D), F32), pltpu.VMEM((3, R, D), F32),
            pltpu.VMEM((3, CONVR, D), F32), pltpu.VMEM((3 * R, D), F32),
            pltpu.VMEM((R, D), F32), pltpu.VMEM((R, D), F32),
            pltpu.VMEM((3, R, D), BF), pltpu.VMEM((3, 3, R, 128), BF), pltpu.VMEM((3, R, 128), BF),
            pltpu.VMEM((R, D), BF), pltpu.VMEM((R, D), BF), pltpu.VMEM((R, D), BF),
            pltpu.VMEM((R, 512), BF), pltpu.VMEM((R, 512), BF), pltpu.VMEM((3, R, 128), BF), pltpu.VMEM((3, 3, R, 128), BF),
            pltpu.VMEM((3, D, D), BF), pltpu.VMEM((D, D), BF), pltpu.VMEM((PARTS, 2, D, PW), BF), pltpu.VMEM((PARTS, 2, PW, D), BF),
            pltpu.VMEM((2, 8, HH), F32),
            pltpu.VMEM((8, D), F32), pltpu.VMEM((8, D), F32), pltpu.VMEM((8, D), F32), pltpu.VMEM((8, D), F32),
            pltpu.VMEM((8, D), F32), pltpu.VMEM((PARTS, 8, 2 * PW), F32), pltpu.VMEM((3, CONV_ROWS, D), F32),
            pltpu.VMEM((8, 8, D), F32), pltpu.VMEM((groups, 8, D), F32),
            pltpu.VMEM((8, 8, D), F32), pltpu.VMEM((groups, 8, D), F32),
            pltpu.VMEM((8, 8, D), F32), pltpu.VMEM((groups, 8, D), F32),
            pltpu.VMEM((8, 8, D), F32), pltpu.VMEM((groups, 8, D), F32),
            pltpu.VMEM((3, 8, CONV_ROWS, D), F32), pltpu.VMEM((3, groups, CONV_ROWS, D), F32),
            dma(2, 3), dma(8), dma(3), dma(3), dma(7, 3), dma(5, 7), dma(2), dma(5),
        ] + units,
        compiler_params=params(collective_id=0, has_side_effects=True),
    )(*args)


def last_kernel(
    seg, outp, gtok, dwa, dwb, dwe, dwc, dwd, rest,
    output, grad_tokens, grad_gains, grad_shifts, grad_kernels, grad_qkv, grad_out, grad_in, grad_bias, grad_down,
    held, lowa, lowb, lowe, lowc, lowd, scr, wide, in_sems, out_sems,
):
    loads = []
    pairs = ((outp, held.at[0]), (gtok, held.at[1]))
    pairs += ((dwa, lowa), (dwb, lowb), (dwe, lowe), (dwc, lowc), (dwd, lowd))
    for n, (src, dst) in enumerate(pairs):
        copy = pltpu.make_async_copy(src, dst, in_sems.at[n])
        copy.start()
        loads.append(copy)
    starts, gaps = find_columns(seg)
    stores = []

    def store(src, dst):
        copy = pltpu.make_async_copy(src, dst, out_sems.at[len(stores)])
        copy.start()
        stores.append(copy)

    for n, dst in enumerate((output, grad_tokens)):
        loads[n].wait()
        to_canvas(held.at[n], scr.at[n], starts, gaps)
        for t in range(3):
            store(scr.at[n, t, pl.ds(0, CELLS)], dst.at[0, :, pl.ds(t * 128, 128)])
    for n, low in enumerate((lowa, lowb, lowe)):
        loads[2 + n].wait()
        start, size = n * PW, PW
        grad_in[:, start : start + size] = low[0, 0:size, :].astype(F32).T
        wide[start : start + size, :] = low[0, size : 2 * size, :].astype(F32)
        store(wide.at[pl.ds(start, size)], grad_down.at[pl.ds(start, size)])
    for n, low in enumerate((lowc, lowd)):
        loads[5 + n].wait()
        for j in range(2):
            at = HH + (n * 2 + j) * D
            wide[at : at + D, :] = low[j].astype(F32)
            here = wide.at[pl.ds(at, D)]
            if n == 0 and j == 1:
                store(here, grad_out)
            else:
                store(here, grad_qkv.at[:, pl.ds((2 if n == 0 else j) * D, D)])
    for k in range(3):
        for o in range(9):
            row = 16 + k * CONV_ROWS + o
            grad_kernels[o, k : k + 1] = rest[row : row + 1]
    grad_gains[0:1] = rest[25:26]
    grad_gains[1:3] = rest[2:4]
    grad_gains[3:4] = rest[65:66]
    grad_gains[4:5] = rest[8:9]
    grad_shifts[0:1] = rest[26:27]
    grad_shifts[1:2] = rest[0:1]
    grad_shifts[2:3] = rest[64:65]
    grad_shifts[3:4] = rest[9:10]
    grad_shifts[4:5] = rest[10:11]
    grad_shifts[5:6] = rest[11:12]
    for j in range(PARTS):
        grad_bias[j * PW : j * PW + PW] = rest[72 + j, 0:PW]
    finish(stores)


def last_call(*args):
    return pl.pallas_call(
        last_kernel,
        out_shape=(
            shape(1, CELLS, D), shape(1, CELLS, D), shape(5, D), shape(6, D), shape(9, 3, D), shape(D, 3 * D),
            shape(D, D), shape(D, HH), shape(HH), shape(HH, D),
        ),
        in_specs=[SM] + [ANY] * 7 + [VM],
        out_specs=(ANY, ANY, VM, VM, VM, ANY, ANY, VM, VM, ANY),
        scratch_shapes=[
            pltpu.VMEM((2, R, D), F32),
            *(pltpu.VMEM((2 if both else 1, rows, D), BF) for rows, both in UNITS),
            pltpu.VMEM((2, 3, CELLS + 16, 128), F32), pltpu.VMEM((HH + 4 * D, D), F32), dma(7), dma(13),
        ],
        compiler_params=params(),
    )(*args)


def local(
    groups, tokens, segment_ids, gains, shifts, kernels, qkv_weight, out_weight,
    mlp_in_weight, mlp_in_bias, mlp_out_weight, cotangent,
):
    found = main_call(
        groups, segment_ids, tokens, cotangent, gains, shifts, kernels.transpose(1, 0, 2),
        qkv_weight, out_weight, mlp_in_weight, mlp_out_weight, mlp_in_bias,
    )
    outs = list(last_call(segment_ids, *found))
    outs[4] = outs[4].transpose(1, 0, 2)
    return tuple(outs)


def solution(mesh):
    groups = mesh.shape["dp"] // QUAD
    both = P(("dp", "mp"), None, None)
    return jax.shard_map(
        functools.partial(local, groups),
        mesh=mesh,
        in_specs=(
            both, P(("dp", "mp"), None), P(), P(), P(), P(), P(), P(None, "mp"), P("mp"), P("mp", None), both,
        ),
        out_specs=(both, both, P(), P(), P(), P(), P(), P(None, "mp"), P("mp"), P("mp", None)),
        check_vma=False,
    )
```

time: 122 us -> 96.5 us (0.79)
  Pallas kernels: 115 us -> 95.4 us
  local copies, waits for them, and re-layouts: 5.56 us -> 0 us
    pallas_call x1, Pallas kernels: 107 us -> 88.6 us  [main_call(): pl.pallas_call(functools.partial(main_kernel, groups), out_shape=(shape(R...]
    unnamed x2 -> x0, local copies, waits for them, and re-layouts: 2.98 us -> none
    reshape x2 -> x0, local copies, waits for them, and re-layouts: 1.98 us -> none  [the longest x1 1.28 us: local(): outs[8] = outs[8].reshape(2 * D)]
    pallas_call x1, Pallas kernels: 8.27 us -> 6.83 us  [last_call(): pl.pallas_call(last_kernel, out_shape=(shape(1, CELLS, D), shape(1, CELLS...]
where the time goes in v3:
time: 96.5 us; the launch traced here: 96.2 us
  Pallas kernels  95.4 us (99%)
    pallas_call x1, Pallas kernels, main_call(): pl.pallas_call(functools.partial(main_kernel, groups), out_shape=(shape(R...  88.6 us
    pallas_call x1, Pallas kernels, last_call(): pl.pallas_call(last_kernel, out_shape=(shape(1, CELLS, D), shape(1, CELLS...  6.83 us

profile of v3, /device:TPU:0, one launch (start us, length us, event | category | flops | bytes accessed | tf_op | source)
XLA Modules:
  0.0 96.2 jit_solution(13493186887061962267)
XLA Ops:
  0.6 88.6 %shard_map.186 = (f32[1024,384]{1,0:T(8,128)}, f32[1024,384]{1,0:T(8,128)}, bf16[1,512,384]{2,1,0:T(8,128)(2,1)}, bf16[1,512,384]{2,1,0:T(8,128)(2,1)}, bf16[1,5...) custom-call(s32[1,896]{1,0:T(1,128)} %seg.3, ...), custom_call_target="tpu_custom_call" | custom-call | tf_op jit(solution)/shard_map/pallas_call | solution.py:989
  89.2 6.8 %shard_map.187 = (f32[1,896,384]{2,1,0:T(8,128)}, f32[1,896,384]{2,1,0:T(8,128)}, f32[5,384]{1,0:T(8,128)}, f32[6,384]{1,0:T(8,128)}, f32[9,3,384]{2,1,0:T(4,128...) custom-call(s32[1,896]{1,0:T(1,128)} %seg.3, ...), custom_call_target="tpu_custom_call" | custom-call | tf_op jit(solution)/shard_map/pallas_call | solution.py:1080

commit v4 on v3

--- a/solution.py
+++ b/solution.py
@@ -20,7 +20,7 @@
 GAP0 = IMAGES * IR
 GAPS = 112
 R = 1024
-CH = 256
+DCH = 1024
 STRIDE = IR + 16
 CONVR = IMAGES * STRIDE + 16
 EPS = 1e-05
@@ -277,9 +277,9 @@
 
 
 def sum_slots(rx, count):
-    total = rx[0]
+    total = rx[0].astype(F32)
     for s in range(1, count):
-        total = total + rx[s]
+        total = total + rx[s].astype(F32)
     return total
 
 
@@ -298,12 +298,57 @@
 
     def middle(self):
         finish(self.copies)
-        self.rx2[self.place.z] = sum_slots(self.rx1, 8)
+        self.rx2[self.place.z] = sum_slots(self.rx1, 8).astype(self.rx2.dtype)
         self.copies = send_along(self.place, self.rx2.at[self.place.z], self.rx2, self.sems[0], self.sems[2])
 
     def end(self):
         finish(self.copies)
         self.done(sum_slots(self.rx2, self.place.groups))
+
+
+class PairedSum:
+    def __init__(self, place, src, rx_core, rx_quad, rx_z, both, sems, n, done):
+        self.place, self.src, self.both, self.done = place, src, both, done
+        self.rx_core, self.rx_quad, self.rx_z = rx_core, rx_quad, rx_z
+        self.sems = [sems.at[n, i] for i in range(5)]
+        self.steps = [self.quad, self.along, self.core_back, self.end]
+
+    def exchange(self, stage, ref, src, dst, peers):
+        for peer in peers:
+            remote(src, dst, self.sems[0], self.sems[stage], peer)
+        self.copies = Pending(ref, self.sems[0], self.sems[stage])
+
+    def half(self, mp):
+        return rows_at(mp * 8, 8, 8)
+
+    def start(self):
+        there = self.src.at[self.half(1 - self.place.mp)]
+        self.exchange(1, self.rx_core, there, self.rx_core, [self.place.other_core()])
+
+    def step(self):
+        finish(self.copies)
+        self.steps.pop(0)()
+
+    def quad(self):
+        slot = self.place.quad
+        self.rx_quad[slot] = self.src[self.half(self.place.mp), :] + self.rx_core[...]
+        here = self.rx_quad.at[slot]
+        peers = [self.place.in_quad(o) for o in range(1, QUAD)]
+        self.exchange(2, self.rx_quad.at[pl.ds(0, QUAD - 1)], here, here, peers)
+
+    def along(self):
+        self.rx_z[self.place.z] = sum_slots(self.rx_quad, QUAD)
+        here = self.rx_z.at[self.place.z]
+        peers = [self.place.along(o) for o in range(1, self.place.groups)]
+        self.exchange(3, self.rx_z.at[pl.ds(0, self.place.groups - 1)], here, here, peers)
+
+    def core_back(self):
+        self.both[self.half(self.place.mp), :] = sum_slots(self.rx_z, self.place.groups)
+        here = self.both.at[self.half(self.place.mp)]
+        self.exchange(4, here, here, here, [self.place.other_core()])
+
+    def end(self):
+        self.done(self.both[...])
 
 
 def merge_moments(rx, count, cells):
@@ -321,7 +366,7 @@
 
 def project(conv, moments, gains, shifts, wqkv, bn, qkv):
     def step(c, carry):
-        rows = rows_at(c * CH, CH)
+        rows = rows_at(c * DCH, DCH)
         for k in range(3):
             standard = (conv[k, rows, :] - moments[k : k + 1]) * moments[3 + k : 4 + k]
             value = standard * gains[1 + k : 2 + k]
@@ -336,7 +381,7 @@
                 qkv[k, p, rows, :] = out[:, p * 128 : p * 128 + 128]
         return carry
 
-    lax.fori_loop(0, R // CH, step, 0)
+    lax.fori_loop(0, R // DCH, step, 0)
 
 
 def key_bias():
@@ -386,7 +431,7 @@
             att[p, rows, :] = own_columns(out, 256).astype(BF)
         return carry
 
-    lax.fori_loop(0, IMAGES, step, 0)
+    lax.fori_loop(0, IMAGES, step, 0, unroll=4)
 
 
 def even_prob():
@@ -415,7 +460,7 @@
     small[...] = jnp.zeros((8, D), F32)
 
     def step(c, carry):
-        rows = rows_at(c * CH, CH)
+        rows = rows_at(c * DCH, DCH)
         attended = jnp.concatenate([att[p, rows, :] for p in range(3)], 1)
         residual = tokp[rows, :] + (dot(attended, wout[...]) + shifts[3:4])
         dres[rows, :] = residual
@@ -426,10 +471,10 @@
         small[3:4] = small[3:4] + col_sum(cot)
         return carry
 
-    lax.fori_loop(0, R // CH, step, 0)
-
-
-HCH = 512
+    lax.fori_loop(0, R // DCH, step, 0)
+
+
+HCH = 1024
 PARTS = 3
 PW = HH // PARTS
 BIAS_TILES = 2 * HH // 128
@@ -468,7 +513,7 @@
 
 def feed_forward_out(cotp, wout, gains, shifts, outp, acc, dres, gr, datt, small):
     def step(c, carry):
-        rows = rows_at(c * CH, CH)
+        rows = rows_at(c * DCH, DCH)
         residual = dres[rows, :]
         outp[rows, :] = residual + outp[rows, :] + shifts[5:6]
         xhat, rstd = norm_parts(residual)
@@ -488,7 +533,7 @@
         small[2:3] = small[2:3] + col_sum(grad)
         return carry
 
-    lax.fori_loop(0, R // CH, step, 0)
+    lax.fori_loop(0, R // DCH, step, 0)
 
 
 def attend_back_values(pool, datt, dqkv):
@@ -524,7 +569,7 @@
             dqkv[1, p, rows, :] = own_columns(dk, IR).astype(BF)
         return carry
 
-    lax.fori_loop(first, last, step, 0)
+    lax.fori_loop(first, last, step, 0, unroll=2)
 
 
 def attend_back_gap(datt, dqkv):
@@ -539,21 +584,20 @@
             dqkv[2, p, rows, :] = grad if b < GAPS // 16 else zero
 
 
-def project_back(k, conv, moments, wqkv, dqkv, dbn, sums, one, two):
-    sums[one : one + 1] = jnp.zeros((1, D), F32)
-    sums[two : two + 1] = jnp.zeros((1, D), F32)
-
+def project_back(k, conv, moments, wqkv, dqkv, dbn, sums, at):
     def step(c, carry):
         rows = rows_at(c * PCH, PCH)
         grad = jnp.concatenate([dqkv[k, p, rows, :] for p in range(3)], 1)
         back = dot_t(grad, wqkv[k])
         dbn[rows_at(k * R + c * PCH, PCH), :] = back
         standard = (conv[k, rows, :] - moments[k : k + 1]) * moments[3 + k : 4 + k]
-        sums[one : one + 1] = sums[one : one + 1] + col_sum(back)
-        sums[two : two + 1] = sums[two : two + 1] + col_sum(back * standard)
-        return carry
-
-    lax.fori_loop(0, R // PCH, step, 0)
+        return carry[0] + col_sum(back), carry[1] + col_sum(back * standard)
+
+    found = lax.fori_loop(0, R // PCH, step, (jnp.zeros((1, D), F32),) * 2)
+    for n in range(2):
+        for t in range(3):
+            row = at + n * 3 + t
+            sums[row : row + 1] = found[n][:, t * 128 : t * 128 + 128]
 
 
 def project_grads(k, bn, dqkv, grads):
@@ -575,56 +619,50 @@
 CONV_ROWS = 16
 
 
-def conv_back(k, first, last, dbn, conv, moments, one, two, gains, shifts, nrm, pool, kernels, dn, dker, inverse_total):
+def conv_back(k, t, first, last, dbn, conv, moments, sums, at, gains, shifts, nrm, pool, kernels, dn, dker, inverse_total):
     mask = cell_mask(IR)
     cells = cell_mask(CB)
+    lanes = slice(t * 128, t * 128 + 128)
+    inv = moments[3 + k : 4 + k, lanes]
 
     def spread(i, carry):
         rows = rows_at(i * IR, IR)
-        for t in range(3):
-            lanes = slice(t * 128, t * 128 + 128)
-            inv = moments[3 + k : 4 + k, lanes]
-            standard = (conv[k, rows, lanes] - moments[k : k + 1, lanes]) * inv
-            shift = (one[:, lanes] + standard * two[:, lanes]) * inverse_total
-            grad = dbn[rows_at(k * R + i * IR, IR), lanes]
-            grad = (gains[1 + k : 2 + k, lanes] * inv) * (grad - mask * shift)
-            pool[shifted_at(0, t, i * STRIDE + 16, IR), :] = pltpu.roll(grad, 1, 0)
-            pool[shifted_at(1, t, i * STRIDE + 16, IR), :] = grad
-            pool[shifted_at(2, t, i * STRIDE + 16, IR), :] = pltpu.roll(grad, IR - 1, 0)
+        standard = (conv[k, rows, lanes] - moments[k : k + 1, lanes]) * inv
+        shift = (sums[at + t : at + t + 1] + standard * sums[at + 3 + t : at + 4 + t]) * inverse_total
+        grad = dbn[rows_at(k * R + i * IR, IR), lanes]
+        grad = (gains[1 + k : 2 + k, lanes] * inv) * (grad - mask * shift)
+        pool[shifted_at(0, t, i * STRIDE + 16, IR), :] = pltpu.roll(grad, 1, 0)
+        pool[shifted_at(1, t, i * STRIDE + 16, IR), :] = grad
+        pool[shifted_at(2, t, i * STRIDE + 16, IR), :] = pltpu.roll(grad, IR - 1, 0)
         return carry
 
     lax.fori_loop(0, IMAGES, spread, 0)
-    blocks = IMAGES * IR // CB
-    per = IR // CB
-    for t in range(3):
-        lanes = slice(t * 128, t * 128 + 128)
-        taps = [kernels[o, k : k + 1, lanes] for o in range(9)]
-
-        def step(b, sums9):
-            base = (b // per) * STRIDE + 16 + (b % per) * CB
-            here = nrm[1, rows_at(base, CB), lanes]
-            acc = jnp.zeros((CB, 128), F32)
-            new = []
-            for o in range(9):
-                x = pool[shifted_at(2 - o % 3, t, base - (o // 3 - 1) * 16, CB), :]
-                acc = acc + x * taps[o]
-                new.append(sums9[o] + jnp.sum((x * here).reshape(CB // 8, 8, 128), 0))
-            rows = rows_at(b * CB, CB)
-            if not first:
-                acc = acc + dn[rows, lanes]
-            dn[rows, lanes] = acc
-            if last:
-                new.append(sums9[9] + jnp.sum((acc * here).reshape(CB // 8, 8, 128), 0))
-                new.append(sums9[10] + jnp.sum((acc * cells).reshape(CB // 8, 8, 128), 0))
-            return tuple(new)
-
-        found = lax.fori_loop(0, blocks, step, (jnp.zeros((8, 128), F32),) * (11 if last else 9))
-        found = [col_sum(f) for f in found]
+    taps = [kernels[o, k : k + 1, lanes] for o in range(9)]
+
+    def step(b, found):
+        base = b * STRIDE + 16
+        here = nrm[1, rows_at(base, CB), lanes]
+        acc = jnp.zeros((CB, 128), F32)
+        new = []
         for o in range(9):
-            dker[k, o : o + 1, lanes] = found[o]
+            x = pool[shifted_at(2 - o % 3, t, base - (o // 3 - 1) * 16, CB), :]
+            acc = acc + x * taps[o]
+            new.append(found[o] + jnp.sum((x * here).reshape(CB // 8, 8, 128), 0))
+        rows = rows_at(b * CB, CB)
+        if not first:
+            acc = acc + dn[rows, lanes]
+        dn[rows, lanes] = acc
         if last:
-            dker[k, 9:10, lanes] = (found[9] - found[10] * shifts[0:1, lanes]) / gains[0:1, lanes]
-            dker[k, 10:11, lanes] = found[10]
+            new.append(found[9] + jnp.sum((acc * here).reshape(CB // 8, 8, 128), 0))
+            new.append(found[10] + jnp.sum((acc * cells).reshape(CB // 8, 8, 128), 0))
+        return tuple(new)
+
+    found = lax.fori_loop(0, IMAGES, step, (jnp.zeros((8, 128), F32),) * (11 if last else 9))
+    found = [col_sum(f) for f in found]
+    if last:
+        found[9] = (found[9] - found[10] * shifts[0:1, lanes]) / gains[0:1, lanes]
+    found += [jnp.zeros((1, 128), F32)] * (CONV_ROWS - len(found))
+    dker[k, :, lanes] = jnp.concatenate(found, 0)
 
 
 def last_norm_back(tokp, dres, dn, gains, gtok):
@@ -761,7 +799,7 @@
     out_hbm, gtok_hbm, dw0, dw1, dw2, dw3, dw4, rest_out,
     pool, tokp, cotp, conv, nrm, dbn, outp, dres, bn, qkv, att, n2, gm, gr, act, dpre, datt, dqkv,
     wqkv_b, wout_b, win_f, wmo_f, bias_f, stats, moments, sums, sums_v, small, dbias, dker,
-    mx1, mx2, sx1, sx2, lx1, lx2, vx1, vx2, kx1, kx2,
+    mx1, mx2, sx1, sx2, lx1, lx2, vx1, vx2, kx1, kx2, kx3, kx4,
     in_sems, w_sems, pair_s, pair_r, sems, unit_sems, out_sems, dw_sems, *unit_flat,
 ):
     dws = (dw0, dw1, dw2, dw3, dw4)
@@ -837,14 +875,14 @@
 
     def keep(at, ref=None):
         def done(total):
-            rest_out[at : at + total.shape[0]] = total
+            rest_out[at : at + total.shape[0], 0 : total.shape[1]] = total
             if ref is not None:
                 ref[...] = total
 
         return done
 
     def keep_small(total):
-        rest_out[8:16] = total
+        rest_out[80:88] = total
         tiles = [total[4 + c // 3 : 5 + c // 3, c % 3 * 128 : c % 3 * 128 + 128] for c in range(BIAS_TILES)]
         for c in range(BIAS_TILES // 2):
             at = c // 2 * 4 + c % 2
@@ -854,7 +892,10 @@
     small_sum = SmallSum(place, small, lx1, lx2, sems, 2, keep_small)
     sum_v = SmallSum(place, sums_v, vx1, vx2, sems, 6, keep(64, sums_v))
     sum_qk = SmallSum(place, sums, sx1, sx2, sems, 1, keep(0, sums))
-    ker_sums = [SmallSum(place, dker.at[k], kx1.at[k], kx2.at[k], sems, 3 + k, keep(16 + 16 * k)) for k in range(3)]
+    ker_sums = [
+        PairedSum(place, dker.at[k], *(x.at[k] for x in (kx1, kx2, kx3, kx4)), sems, 3 + k, keep(16 + 16 * k))
+        for k in range(3)
+    ]
 
     def forward(part):
         hidden_part(part, n2, gm, win_f, wmo_f, bias_f, act, dpre, outp, acc, dbias)
@@ -866,7 +907,6 @@
 
     def values():
         attend_back_values(pool, datt, dqkv)
-        attend_back_gap(datt, dqkv)
 
     def after_forward():
         feed_forward_out(cotp, wout_b, gains, shifts, outp, acc, dres, gr, datt, small)
@@ -874,6 +914,7 @@
             tile = slice(c % 4 * 128, c % 4 * 128 + 128)
             small[4 + c // 3 : 5 + c // 3, c % 3 * 128 : c % 3 * 128 + 128] = dbias[c // 4, 0:1, tile]
         small_sum.start()
+        attend_back_gap(datt, dqkv)
         stores.append(pltpu.make_async_copy(outp, out_hbm, out_sems.at[0]))
         stores[0].start()
 
@@ -891,22 +932,22 @@
         ud.step()
 
     def value_back():
-        project_back(2, conv, moments, wqkv_b, dqkv, dbn, sums_v, 0, 1)
+        project_back(2, conv, moments, wqkv_b, dqkv, dbn, sums_v, 0)
         sum_v.start()
 
-    def query_back():
-        for k in range(2):
-            project_back(k, conv, moments, wqkv_b, dqkv, dbn, sums, k, 2 + k)
-        sum_qk.start()
-        conv_back_zero(pool)
-
-    def back(k, begin=False, last=False):
-        one, two = (sums_v[0:1], sums_v[1:2]) if k == 2 else (sums[k : k + 1], sums[2 + k : 3 + k])
+    def query_back(k):
+        project_back(k, conv, moments, wqkv_b, dqkv, dbn, sums, 6 * k)
+        if k == 1:
+            sum_qk.start()
+
+    def back(k, t):
+        held, at = (sums_v, 0) if k == 2 else (sums, 6 * k)
         conv_back(
-            k, begin, last, dbn, conv, moments, one, two, gains, shifts, nrm, pool, kernels, cotp, dker,
+            k, t, k == 0, k == 2, dbn, conv, moments, held, at, gains, shifts, nrm, pool, kernels, cotp, dker,
             1.0 / (cells * 8 * groups),
         )
-        ker_sums[k].start()
+        if t == 2:
+            ker_sums[k].start()
 
     def last_norm():
         stores[0].wait()
@@ -934,51 +975,65 @@
     after_forward()
     unit(0)
     unit(2)
-    values()
-    out_grad()
-    value_grads()
-    unit(1)
-    value_back()
-    small_sum.step()
-    unit(0)
-    unit(3)
     attend_back(0, 2, qkv, pool, datt, dqkv)
-    unit(1)
-    unit(2)
     attend_back(2, 4, qkv, pool, datt, dqkv)
     unit(0)
     small_sum.step()
-    sum_v.step()
+    unit(1)
+    query_back(0)
+    query_back(1)
+    values()
+    unit(0)
+    unit(2)
+    out_grad()
+    value_grads()
+    sum_qk.step()
+    small_sum.step()
+    unit(1)
     unit(3)
     query_grads()
-    query_back()
+    unit(2)
+    value_back()
+    unit(0)
     unit(4)
+    sum_qk.step()
     unit(1)
-    unit(0)
-    unit(2)
-    sum_qk.step()
-    sum_v.step()
-    back(2, begin=True)
-    unit(4)
+    conv_back_zero(pool)
+    back(0, 0)
+    back(0, 1)
     unit(3)
     unit(2)
-    sum_qk.step()
-    back(1)
+    back(0, 2)
+    sum_v.step()
+    back(1, 0)
+    ker_sums[0].step()
+    back(1, 1)
     unit(4)
+    back(1, 2)
+    unit(3)
+    ker_sums[1].step()
+    sum_v.step()
+    back(2, 0)
+    back(2, 1)
     unit(1)
+    unit(4)
+    back(2, 2)
+    last_norm()
     ker_sums[2].step()
-    back(0, last=True)
     unit(3)
-    last_norm()
     unit(2)
+    ker_sums[0].step()
+    ker_sums[1].step()
+    unit(4)
+    ker_sums[2].step()
+    unit(3)
+    ker_sums[0].step()
+    ker_sums[1].step()
+    unit(3)
+    ker_sums[2].step()
     unit(4)
     ker_sums[1].step()
-    ker_sums[0].step()
     ker_sums[2].step()
-    unit(3)
-    unit(3)
-    ker_sums[1].step()
-    unit(4)
     ker_sums[0].step()
     unit(4)
     finish(stores[1:])
@@ -990,7 +1045,7 @@
         functools.partial(main_kernel, groups),
         out_shape=(shape(R, D), shape(R, D))
         + tuple(shape(2 if both else 1, rows, D, dtype=BF) for rows, both in UNITS)
-        + (shape(80, D),),
+        + (shape(88, D),),
         in_specs=[VM, ANY, ANY, VM, VM, VM, ANY, ANY, ANY, ANY, VM],
         out_specs=(ANY,) * 7 + (VM,),
         scratch_shapes=[
@@ -1003,14 +1058,15 @@
             pltpu.VMEM((R, 512), BF), pltpu.VMEM((R, 512), BF), pltpu.VMEM((3, R, 128), BF), pltpu.VMEM((3, 3, R, 128), BF),
             pltpu.VMEM((3, D, D), BF), pltpu.VMEM((D, D), BF), pltpu.VMEM((PARTS, 2, D, PW), BF), pltpu.VMEM((PARTS, 2, PW, D), BF),
             pltpu.VMEM((2, 8, HH), F32),
-            pltpu.VMEM((8, D), F32), pltpu.VMEM((8, D), F32), pltpu.VMEM((8, D), F32), pltpu.VMEM((8, D), F32),
+            pltpu.VMEM((8, D), F32), pltpu.VMEM((8, D), F32), pltpu.VMEM((16, 128), F32), pltpu.VMEM((8, 128), F32),
             pltpu.VMEM((8, D), F32), pltpu.VMEM((PARTS, 8, 2 * PW), F32), pltpu.VMEM((3, CONV_ROWS, D), F32),
             pltpu.VMEM((8, 8, D), F32), pltpu.VMEM((groups, 8, D), F32),
+            pltpu.VMEM((8, 16, 128), F32), pltpu.VMEM((groups, 16, 128), F32),
             pltpu.VMEM((8, 8, D), F32), pltpu.VMEM((groups, 8, D), F32),
-            pltpu.VMEM((8, 8, D), F32), pltpu.VMEM((groups, 8, D), F32),
-            pltpu.VMEM((8, 8, D), F32), pltpu.VMEM((groups, 8, D), F32),
-            pltpu.VMEM((3, 8, CONV_ROWS, D), F32), pltpu.VMEM((3, groups, CONV_ROWS, D), F32),
-            dma(2, 3), dma(8), dma(3), dma(3), dma(7, 3), dma(5, 7), dma(2), dma(5),
+            pltpu.VMEM((8, 8, 128), F32), pltpu.VMEM((groups, 8, 128), F32),
+            pltpu.VMEM((3, 8, D), F32), pltpu.VMEM((3, QUAD, 8, D), F32), pltpu.VMEM((3, groups, 8, D), F32),
+            pltpu.VMEM((3, CONV_ROWS, D), F32),
+            dma(2, 3), dma(8), dma(3), dma(3), dma(7, 5), dma(5, 7), dma(2), dma(5),
         ] + units,
         compiler_params=params(collective_id=0, has_side_effects=True),
     )(*args)
@@ -1019,7 +1075,7 @@
 def last_kernel(
     seg, outp, gtok, dwa, dwb, dwe, dwc, dwd, rest,
     output, grad_tokens, grad_gains, grad_shifts, grad_kernels, grad_qkv, grad_out, grad_in, grad_bias, grad_down,
-    held, lowa, lowb, lowe, lowc, lowd, scr, wide, in_sems, out_sems,
+    held, lowa, lowb, lowe, lowc, lowd, scr, wide, turned, in_sems, out_sems,
 ):
     loads = []
     pairs = ((outp, held.at[0]), (gtok, held.at[1]))
@@ -1044,8 +1100,9 @@
     for n, low in enumerate((lowa, lowb, lowe)):
         loads[2 + n].wait()
         start, size = n * PW, PW
-        grad_in[:, start : start + size] = low[0, 0:size, :].astype(F32).T
+        turned[:, start : start + size] = low[0, 0:size, :].astype(F32).T
         wide[start : start + size, :] = low[0, size : 2 * size, :].astype(F32)
+        store(turned.at[:, pl.ds(start, size)], grad_in.at[:, pl.ds(start, size)])
         store(wide.at[pl.ds(start, size)], grad_down.at[pl.ds(start, size)])
     for n, low in enumerate((lowc, lowd)):
         loads[5 + n].wait()
@@ -1061,16 +1118,16 @@
         for o in range(9):
             row = 16 + k * CONV_ROWS + o
             grad_kernels[o, k : k + 1] = rest[row : row + 1]
-    grad_gains[0:1] = rest[25:26]
-    grad_gains[1:3] = rest[2:4]
-    grad_gains[3:4] = rest[65:66]
-    grad_gains[4:5] = rest[8:9]
-    grad_shifts[0:1] = rest[26:27]
-    grad_shifts[1:2] = rest[0:1]
-    grad_shifts[2:3] = rest[64:65]
-    grad_shifts[3:4] = rest[9:10]
-    grad_shifts[4:5] = rest[10:11]
-    grad_shifts[5:6] = rest[11:12]
+    grad_gains[0:1] = rest[57:58]
+    grad_gains[4:5] = rest[80:81]
+    grad_shifts[0:1] = rest[58:59]
+    grad_shifts[3:6] = rest[81:84]
+    for t in range(3):
+        lanes = slice(t * 128, t * 128 + 128)
+        for k, at in enumerate((0, 6, 64)):
+            grad_gains[1 + k : 2 + k, lanes] = rest[at + 3 + t : at + 4 + t, 0:128]
+            if k != 1:
+                grad_shifts[1 + k // 2 : 2 + k // 2, lanes] = rest[at + t : at + t + 1, 0:128]
     for j in range(PARTS):
         grad_bias[j * PW : j * PW + PW] = rest[72 + j, 0:PW]
     finish(stores)
@@ -1084,11 +1141,12 @@
             shape(D, D), shape(D, HH), shape(HH), shape(HH, D),
         ),
         in_specs=[SM] + [ANY] * 7 + [VM],
-        out_specs=(ANY, ANY, VM, VM, VM, ANY, ANY, VM, VM, ANY),
+        out_specs=(ANY, ANY, VM, VM, VM, ANY, ANY, ANY, VM, ANY),
         scratch_shapes=[
             pltpu.VMEM((2, R, D), F32),
             *(pltpu.VMEM((2 if both else 1, rows, D), BF) for rows, both in UNITS),
-            pltpu.VMEM((2, 3, CELLS + 16, 128), F32), pltpu.VMEM((HH + 4 * D, D), F32), dma(7), dma(13),
+            pltpu.VMEM((2, 3, CELLS + 16, 128), F32), pltpu.VMEM((HH + 4 * D, D), F32),
+            pltpu.VMEM((D, HH), F32), dma(7), dma(16),
         ],
         compiler_params=params(),
     )(*args)

time: 96.5 us -> 89.8 us (0.931)
  Pallas kernels: 95.4 us -> 88.7 us
    pallas_call x1, Pallas kernels: 88.6 us -> 81.9 us  [main_call(): pl.pallas_call(functools.partial(main_kernel, groups), out_shape=(shape(R...]
where the time goes in v4:
time: 89.8 us; the launch traced here: 89.5 us
  Pallas kernels  88.7 us (99%)
    pallas_call x1, Pallas kernels, main_call(): pl.pallas_call(functools.partial(main_kernel, groups), out_shape=(shape(R...  81.9 us
    pallas_call x1, Pallas kernels, last_call(): pl.pallas_call(last_kernel, out_shape=(shape(1, CELLS, D), shape(1, CELLS...  6.82 us

profile of v4, /device:TPU:0, one launch (start us, length us, event | category | flops | bytes accessed | tf_op | source)
XLA Modules:
  0.0 89.5 jit_solution(2924073177768111249)
XLA Ops:
  0.6 81.9 %shard_map.186 = (f32[1024,384]{1,0:T(8,128)}, f32[1024,384]{1,0:T(8,128)}, bf16[1,512,384]{2,1,0:T(8,128)(2,1)}, bf16[1,512,384]{2,1,0:T(8,128)(2,1)}, bf16[1,5...) custom-call(s32[1,896]{1,0:T(1,128)} %seg.3, ...), custom_call_target="tpu_custom_call" | custom-call | tf_op jit(solution)/shard_map/pallas_call | solution.py:1044
  82.5 6.8 %shard_map.187 = (f32[1,896,384]{2,1,0:T(8,128)}, f32[1,896,384]{2,1,0:T(8,128)}, f32[5,384]{1,0:T(8,128)}, f32[6,384]{1,0:T(8,128)}, f32[9,3,384]{2,1,0:T(4,128...) custom-call(s32[1,896]{1,0:T(1,128)} %seg.3, ...), custom_call_target="tpu_custom_call" | custom-call | tf_op jit(solution)/shard_map/pallas_call | solution.py:1137

commit v5 on v4

--- a/solution.py
+++ b/solution.py
@@ -806,14 +806,19 @@
     unit_refs = [unit_flat[n * 7 : n * 7 + 7] for n in range(len(UNITS))]
     place = Place(groups)
     place.greet()
-    copies = []
-    for n, src in enumerate((tokens, cot)):
+
+    def load(n, src):
+        copies = []
         for t in range(3):
             copy = pltpu.make_async_copy(
                 src.at[0, :, pl.ds(t * 128, 128)], pool.at[pl.ds((n * 3 + t) * SCR, CELLS)], in_sems.at[n, t]
             )
             copy.start()
             copies.append(copy)
+        return copies
+
+    finish(load(0, tokens))
+    loads = load(1, cot)
     blocks = [(wqkv.at[:, pl.ds(k * D, D)], dbn.at[pl.ds(k * D, D)]) for k in range(3)]
     blocks.append((wout, dbn.at[pl.ds(3 * D, D)]))
     for j in range(PARTS):
@@ -825,7 +830,6 @@
         copy.start()
         weights.append(copy)
     ahead = empty_before(seg)
-    finish(copies)
     to_images(pool, 0, tokp, ahead)
     first_norm(tokp, gains, shifts, nrm)
     conv_forward(nrm, kernels, conv, stats)
@@ -846,6 +850,7 @@
         remote(ref, ref, pair_s.at[n], pair_r.at[n], place.other_core())
         for n, ref in enumerate((win_f.at[:, place.mp], wmo_f.at[:, place.mp], bias_f.at[place.mp]))
     ]
+    finish(loads)
     to_images(pool, 3 * SCR, cotp, ahead)
     finish(copies)
     mean, m2 = merge_moments(mx1, 8, cells)

time: 89.8 us -> 88.3 us (0.983)
  Pallas kernels: 88.7 us -> 87.2 us
    pallas_call x1, Pallas kernels: 81.9 us -> 80.4 us  [main_call(): pl.pallas_call(functools.partial(main_kernel, groups), out_shape=(shape(R...]
where the time goes in v5:
time: 88.3 us; the launch traced here: 88.1 us
  Pallas kernels  87.2 us (99%)
    pallas_call x1, Pallas kernels, main_call(): pl.pallas_call(functools.partial(main_kernel, groups), out_shape=(shape(R...  80.4 us
    pallas_call x1, Pallas kernels, last_call(): pl.pallas_call(last_kernel, out_shape=(shape(1, CELLS, D), shape(1, CELLS...  6.82 us

profile of v5, /device:TPU:0, one launch (start us, length us, event | category | flops | bytes accessed | tf_op | source)
XLA Modules:
  0.0 88.1 jit_solution(14986684607028227076)
XLA Ops:
  0.6 80.4 %shard_map.186 = (f32[1024,384]{1,0:T(8,128)}, f32[1024,384]{1,0:T(8,128)}, bf16[1,512,384]{2,1,0:T(8,128)(2,1)}, bf16[1,512,384]{2,1,0:T(8,128)(2,1)}, bf16[1,5...) custom-call(s32[1,896]{1,0:T(1,128)} %seg.3, ...), custom_call_target="tpu_custom_call" | custom-call | tf_op jit(solution)/shard_map/pallas_call | solution.py:1049
  81.1 6.8 %shard_map.187 = (f32[1,896,384]{2,1,0:T(8,128)}, f32[1,896,384]{2,1,0:T(8,128)}, f32[5,384]{1,0:T(8,128)}, f32[6,384]{1,0:T(8,128)}, f32[9,3,384]{2,1,0:T(4,128...) custom-call(s32[1,896]{1,0:T(1,128)} %seg.3, ...), custom_call_target="tpu_custom_call" | custom-call | tf_op jit(solution)/shard_map/pallas_call | solution.py:1142

commit v6 on v5

--- a/solution.py
+++ b/solution.py
@@ -169,40 +169,40 @@
 
 
 def conv_forward(nrm, kernels, conv, stats):
-    mask = cell_mask(CB)
-    blocks = IMAGES * IR // CB
-    per = IR // CB
+    mask = cell_mask(IR)
+    count = float(IMG * IMG)
     for t in range(3):
         lanes = slice(t * 128, t * 128 + 128)
         taps = [[kernels[o, k : k + 1, lanes] for o in range(9)] for k in range(3)]
 
-        def step(b, sums):
-            base = (b // per) * STRIDE + 16 + (b % per) * CB
-            acc = [jnp.zeros((CB, 128), F32)] * 3
+        def convolve(b):
+            base = b * STRIDE + 16
+            acc = [jnp.zeros((IR, 128), F32)] * 3
             for o in range(9):
-                x = nrm[o % 3, rows_at(base + (o // 3 - 1) * 16, CB), lanes]
+                x = nrm[o % 3, rows_at(base + (o // 3 - 1) * 16, IR), lanes]
                 for k in range(3):
                     acc[k] = acc[k] + x * taps[k][o]
+            for k in range(3):
+                conv[k, rows_at(b * IR, IR), lanes] = acc[k]
+            return acc
+
+        def spread(acc, centres, sums):
             new = []
             for k in range(3):
-                conv[k, rows_at(b * CB, CB), lanes] = acc[k]
-                new.append(sums[k] + jnp.sum((acc[k] * mask).reshape(CB // 8, 8, 128), 0))
+                away = (acc[k] - centres[k]) * mask
+                new.append(sums[2 * k] + jnp.sum(away.reshape(IR // 8, 8, 128), 0))
+                new.append(sums[2 * k + 1] + jnp.sum((away * away).reshape(IR // 8, 8, 128), 0))
             return tuple(new)
 
-        sums = lax.fori_loop(0, blocks, step, (jnp.zeros((8, 128), F32),) * 3)
-        means = [jnp.sum(s, 0, keepdims=True) * (1.0 / (IMAGES * IMG * IMG)) for s in sums]
-
-        def spread(b, sums):
-            new = []
-            for k in range(3):
-                away = (conv[k, rows_at(b * CB, CB), lanes] - means[k]) * mask
-                new.append(sums[k] + jnp.sum((away * away).reshape(CB // 8, 8, 128), 0))
-            return tuple(new)
-
-        squares = lax.fori_loop(0, blocks, spread, (jnp.zeros((8, 128), F32),) * 3)
+        acc = convolve(0)
+        centres = [jnp.sum(a * mask, 0, keepdims=True) * (1.0 / count) for a in acc]
+        sums = spread(acc, centres, (jnp.zeros((8, 128), F32),) * 6)
+        sums = lax.fori_loop(1, IMAGES, lambda b, found: spread(convolve(b), centres, found), sums)
+        sums = [jnp.sum(x, 0, keepdims=True) for x in sums]
         for k in range(3):
-            stats[k : k + 1, lanes] = means[k]
-            stats[3 + k : 4 + k, lanes] = jnp.sum(squares[k], 0, keepdims=True)
+            one, two = sums[2 * k] * (1.0 / (IMAGES * count)), sums[2 * k + 1]
+            stats[k : k + 1, lanes] = centres[k] + one
+            stats[3 + k : 4 + k, lanes] = two - one * one * (IMAGES * count)
         stats[6:8, lanes] = jnp.zeros((2, 128), F32)
     for k in range(3):
         conv[k, GAP0:R, :] = jnp.zeros((R - GAP0, D), F32)
@@ -456,8 +456,7 @@
     return jnp.sum(x, 0, keepdims=True)
 
 
-def feed_forward_in(tokp, cotp, att, wout, gains, shifts, dres, n2, gm, small):
-    small[...] = jnp.zeros((8, D), F32)
+def feed_forward_in(tokp, att, wout, gains, shifts, dres, n2):
 
     def step(c, carry):
         rows = rows_at(c * DCH, DCH)
@@ -466,6 +465,16 @@
         dres[rows, :] = residual
         xhat, _ = norm_parts(residual)
         n2[rows, :] = (xhat * gains[4:5] + shifts[4:5]).astype(BF)
+        return carry
+
+    lax.fori_loop(0, R // DCH, step, 0)
+
+
+def cotangent_parts(cotp, gm, small):
+    small[...] = jnp.zeros((8, D), F32)
+
+    def step(c, carry):
+        rows = rows_at(c * DCH, DCH)
         cot = cotp[rows, :]
         gm[rows, :] = cot.astype(BF)
         small[3:4] = small[3:4] + col_sum(cot)
@@ -852,6 +861,7 @@
     ]
     finish(loads)
     to_images(pool, 3 * SCR, cotp, ahead)
+    cotangent_parts(cotp, gm, small)
     finish(copies)
     mean, m2 = merge_moments(mx1, 8, cells)
     mx2[place.z, 0:3] = mean
@@ -866,7 +876,7 @@
     project(conv, moments, gains, shifts, wqkv_b, bn, qkv)
     attend(qkv, pool, att)
     attend_gap(qkv, att)
-    feed_forward_in(tokp, cotp, att, wout_b, gains, shifts, dres, n2, gm, small)
+    feed_forward_in(tokp, att, wout_b, gains, shifts, dres, n2)
     finish(pairs)
 
     units = []
@@ -948,7 +958,7 @@
     def back(k, t):
         held, at = (sums_v, 0) if k == 2 else (sums, 6 * k)
         conv_back(
-            k, t, k == 0, k == 2, dbn, conv, moments, held, at, gains, shifts, nrm, pool, kernels, cotp, dker,
+            k, t, k == 1, k == 2, dbn, conv, moments, held, at, gains, shifts, nrm, pool, kernels, cotp, dker,
             1.0 / (cells * 8 * groups),
         )
         if t == 2:
@@ -990,57 +1000,57 @@
     values()
     unit(0)
     unit(2)
+    query_grads()
+    small_sum.step()
+    sum_qk.step()
+    unit(1)
+    unit(4)
     out_grad()
     value_grads()
-    sum_qk.step()
-    small_sum.step()
-    unit(1)
-    unit(3)
-    query_grads()
     unit(2)
     value_back()
     unit(0)
-    unit(4)
+    unit(3)
     sum_qk.step()
     unit(1)
     conv_back_zero(pool)
+    back(1, 0)
+    back(1, 1)
+    unit(4)
+    unit(2)
+    back(1, 2)
+    sum_v.step()
     back(0, 0)
+    ker_sums[1].step()
     back(0, 1)
     unit(3)
-    unit(2)
     back(0, 2)
-    sum_v.step()
-    back(1, 0)
+    unit(4)
     ker_sums[0].step()
-    back(1, 1)
-    unit(4)
-    back(1, 2)
-    unit(3)
-    ker_sums[1].step()
     sum_v.step()
     back(2, 0)
     back(2, 1)
     unit(1)
-    unit(4)
+    unit(3)
     back(2, 2)
     last_norm()
     ker_sums[2].step()
-    unit(3)
+    unit(4)
     unit(2)
+    ker_sums[1].step()
     ker_sums[0].step()
-    ker_sums[1].step()
-    unit(4)
-    ker_sums[2].step()
-    unit(3)
-    ker_sums[0].step()
-    ker_sums[1].step()
     unit(3)
     ker_sums[2].step()
     unit(4)
     ker_sums[1].step()
+    ker_sums[0].step()
+    ker_sums[1].step()
     ker_sums[2].step()
+    unit(3)
     ker_sums[0].step()
+    ker_sums[2].step()
     unit(4)
+    unit(3)
     finish(stores[1:])
 
 

time: 88.3 us -> 87.9 us (level)
  no operation moved by 1% of the time
where the time goes in v6:
time: 87.9 us; the launch traced here: 87.6 us
  Pallas kernels  86.8 us (99%)
    pallas_call x1, Pallas kernels, main_call(): pl.pallas_call(functools.partial(main_kernel, groups), out_shape=(shape(R...  80 us
    pallas_call x1, Pallas kernels, last_call(): pl.pallas_call(last_kernel, out_shape=(shape(1, CELLS, D), shape(1, CELLS...  6.82 us

profile of v6, /device:TPU:0, one launch (start us, length us, event | category | flops | bytes accessed | tf_op | source)
XLA Modules:
  0.0 87.6 jit_solution(11909022543321963785)
XLA Ops:
  0.6 80.0 %shard_map.186 = (f32[1024,384]{1,0:T(8,128)}, f32[1024,384]{1,0:T(8,128)}, bf16[1,512,384]{2,1,0:T(8,128)(2,1)}, bf16[1,512,384]{2,1,0:T(8,128)(2,1)}, bf16[1,5...) custom-call(s32[1,896]{1,0:T(1,128)} %seg.3, ...), custom_call_target="tpu_custom_call" | custom-call | tf_op jit(solution)/shard_map/pallas_call | solution.py:1059
  80.6 6.8 %shard_map.187 = (f32[1,896,384]{2,1,0:T(8,128)}, f32[1,896,384]{2,1,0:T(8,128)}, f32[5,384]{1,0:T(8,128)}, f32[6,384]{1,0:T(8,128)}, f32[9,3,384]{2,1,0:T(4,128...) custom-call(s32[1,896]{1,0:T(1,128)} %seg.3, ...), custom_call_target="tpu_custom_call" | custom-call | tf_op jit(solution)/shard_map/pallas_call | solution.py:1152
